TPU v7x, 256 devices: a whole 4x4x8 slice. The times are simulated.
256 devices in a mesh: req: 64 (over z, x, core), head: 4 (over y).
Axes of the slice: x: 4, y: 4, z: 8, core: 2. Of those that a mesh axis runs over, the one named last changes fastest.
Arguments:
- latent_pages: bfloat16 [16384, 96, 512], P(('req', 'head')), may hold values from -6 to 6
- rope_pages: bfloat16 [16384, 6144], P(('req', 'head')), may hold values from -6 to 6
- page_place: int32 [16384], P('req'), may hold values from 0 to 255, as said below
- lengths: int32 [128], P('req'), may hold values from 1 to 12288
- q_latent: bfloat16 [128, 2, 128, 512], P('req', None, 'head'), may hold values from -6 to 6
- q_rope: bfloat16 [128, 2, 128, 64], P('req', None, 'head'), may hold values from -220 to 220
- new_latent: bfloat16 [128, 2, 512], P('req'), may hold values from -6 to 6
- new_rope: bfloat16 [128, 2, 64], P('req'), may hold values from -4 to 4
Outputs:
- head_out: bfloat16 [128, 2, 128, 512], P('req', None, 'head')
Inputs may be any that keep to these rules, and one draw needn't show every extreme that they name: `page_place`: within each block of 256 entries every value 0 to 255 appears once.
All inputs are finite; a program needn't handle non-finite values.
Results may differ from a plain program's by a relative error of at most 0.008.
Values may be sent and summed in bfloat16 or wider, within the bound.
No kernel may reach another device: no remote copies, remote signals or barrier semaphores. Data moves between devices by JAX's collectives and lax.ppermute only.
A program may use at most 128 MiB of HBM per device.

v0:
```python
import jax
import jax.numpy as jnp
from jax import lax
from jax.sharding import PartitionSpec as P

ROPE = 64
NOPE = 128


NEG = -1e30


def contract(left, right):
    return lax.dot_general(
        left, right, (((1,), (1,)), ((), ())), preferred_element_type=jnp.float32
    )


def softmax_part(
    latent_rows,
    rope_rows,
    key_mask,
    query_lat,
    query_rope,
    fresh_lat,
    fresh_rope,
    fresh_mask,
    scaling,
):
    score = (contract(query_lat, latent_rows) + contract(query_rope, rope_rows)) * scaling
    fresh = (contract(query_lat, fresh_lat) + contract(query_rope, fresh_rope)) * scaling
    score = jnp.where(key_mask[None, :], score, NEG)
    fresh = jnp.where(fresh_mask, fresh, NEG)
    maxima = jnp.maximum(jnp.max(score, axis=1), jnp.max(fresh, axis=1))
    weight = jnp.where(key_mask[None, :], jnp.exp(score - maxima[:, None]), 0.0)
    weight_new = jnp.where(fresh_mask, jnp.exp(fresh - maxima[:, None]), 0.0)
    totals = jnp.sum(weight, axis=1) + jnp.sum(weight_new, axis=1)
    weighted = jnp.dot(weight.astype(jnp.bfloat16), latent_rows, preferred_element_type=jnp.float32)
    weighted = weighted + jnp.dot(
        weight_new.astype(jnp.bfloat16), fresh_lat, preferred_element_type=jnp.float32
    )
    return (maxima, totals, weighted)


def fresh_allowed(step_count, head_count):
    row_step = jnp.arange(step_count * head_count, dtype=jnp.int32) // head_count
    return jnp.arange(step_count, dtype=jnp.int32)[None, :] <= row_step[:, None]


def on_device(
    latent_pages, rope_pages, page_place, lengths, q_latent, q_rope, new_latent, new_rope
):
    scaling = float(NOPE + ROPE) ** (-0.5)
    recv_lat, recv_rope = (
        lax.all_to_all(latent_pages, "req", split_axis=0, concat_axis=0, tiled=True),
        lax.all_to_all(rope_pages, "req", split_axis=0, concat_axis=0, tiled=True),
    )
    request_count = lengths.shape[0]
    step_count = q_latent.shape[1]
    head_count = q_latent.shape[2]
    width = q_latent.shape[3]
    rope_width = q_rope.shape[3]
    page_len = recv_lat.shape[1]
    group_pages = page_place.shape[0]
    per_request = group_pages // request_count
    whole_lat, whole_rope = (
        lax.all_gather(recv_lat, "head", axis=0, tiled=True),
        lax.all_gather(recv_rope, "head", axis=0, tiled=True),
    )
    inverse = (
        jnp.zeros((group_pages,), jnp.int32)
        .at[page_place]
        .set(jnp.arange(group_pages, dtype=jnp.int32))
    )
    fresh_mask = fresh_allowed(step_count, head_count)

    def one_request(request):
        slots = lax.dynamic_slice_in_dim(inverse, request * per_request, per_request)
        latent_rows = whole_lat[slots].reshape(per_request * page_len, width)
        rope_rows = whole_rope[slots].reshape(per_request * page_len, rope_width)
        key_mask = jnp.arange(per_request * page_len, dtype=jnp.int32) < lengths[request]
        query_lat = q_latent[request].reshape(step_count * head_count, width)
        query_rope = q_rope[request].reshape(step_count * head_count, rope_width)
        maxima, totals, weighted = softmax_part(
            latent_rows,
            rope_rows,
            key_mask,
            query_lat,
            query_rope,
            new_latent[request],
            new_rope[request],
            fresh_mask,
            scaling,
        )
        return (
            (weighted / totals[:, None]).astype(jnp.bfloat16).reshape(step_count, head_count, width)
        )

    return lax.map(one_request, jnp.arange(request_count, dtype=jnp.int32))


def solution(mesh):
    return jax.shard_map(
        on_device,
        mesh=mesh,
        in_specs=(
            P(("req", "head"), None, None),
            P(("req", "head"), None),
            P("req"),
            P("req"),
            P("req", None, "head", None),
            P("req", None, "head", None),
            P("req", None, None),
            P("req", None, None),
        ),
        out_specs=P("req", None, "head", None),
        check_vma=False,
    )
```

profile of v0, /device:TPU:1, one launch (start us, length us, event | category | flops | bytes accessed | tf_op | source)
XLA Modules:
  0.0 518.0 jit_solution(2116464217127431893)
XLA Ops:
  7.0 2.3 reduce
  9.9 35.5 %all_to_all.17 = bf16[64,2,3072]{2,1,0:T(2,128)(2,1)S(1)} all-to-all(bf16[64,2,3072]{2,1,0:T(2,128)(2,1)S(1)} %reshape.75), channel_id=1, replica_groups=mesh['req'=64,'head'=4] {'req'}, dimensions={0} | all-to-all | bytes 1572864 | tf_op jit(solution)/shard_map/all_to_all | solution.py:56
  45.5 6.4 %all-to-all-start = ((bf16[64,96,512]{2,1,0:T(8,128)(2,1)}), bf16[64,96,512]{2,1,0:T(8,128)(2,1)}, u32[]{:S(2)}, u32[]{:S(2)}) async-start(bf16[64,96,512]{2,1,0:T(8,128)(2,1)} %param.10), calls=%async_computation | async-start | bytes 12582912 | tf_op jit(solution)/shard_map/all_to_all | solution.py:55
  52.6 1.3 copy.10
  54.0 136.4 %all-to-all-done = bf16[64,96,512]{2,1,0:T(8,128)(2,1)} async-done(((bf16[64,96,512]{2,1,0:T(8,128)(2,1)}), bf16[64,96,512]{2,1,0:T(8,128)(2,1)}, u32[]{:S(2)}, u32[]{:S(2)}) %all-to-all-start) | async-done | bytes 6291488 | tf_op jit(solution)/shard_map/all_to_all | solution.py:55
  191.1 1.6 scatter_custom_fusion
  192.7 223.4 %all-gather.4.cloned.1.call-done = bf16[256,96,512]{2,1,0:T(8,128)(2,1)} async-done(((bf16[64,96,512]{2,1,0:T(8,128)(2,1)}), bf16[256,96,512]{2,1,0:T(8,128)(2,1)}) %all-gather.4.cloned.1.call-update) | async-done | bytes 25165840 | tf_op jit(solution)/shard_map/all_gather | solution.py:67
  416.2 95.0 %while.12 = (s32[]{:T(128)}, bf16[2,2,32,512]{3,2,1,0:T(8,128)(2,1)}, s32[2]{0:T(128)S(1)}, s32[2]{0:T(128)S(1)}, bf16[2,2,32,512]{3,2,1,0:T(8,128)(2,1)S(1)}, /...) while((s32[]{:T(128)}, ...), condition=%wide.region_6.7_spmd.clone.clone, body=%wide.region_1.6_spmd.clone.clone.sunk | while | flops 1719532544 | bytes 113553816 | solution.py:99
  421.3 6.5 %gather_fusion.1 = bf16[128,6144]{1,0:T(8,128)(2,1)} fusion(bf16[256,6144]{1,0:T(8,128)(2,1)} %get-tuple-element.277, s32[1024]{0:T(1024)S(1)} %pad_clamp_fusion.2), kind=kCustom, calls=%fused_computation.1.clone.clone.1 | custom fusion | bytes 3146240 | tf_op jit(solution)/shard_map/while/body/eval_jaxpr/gather | solution.py:80
  427.8 4.3 reshape.86
  432.1 16.6 %gather_fusion = bf16[128,96,512]{2,1,0:T(8,128)(2,1)} fusion(bf16[256,96,512]{2,1,0:T(8,128)(2,1)} %get-tuple-element.275, s32[1024]{0:T(1024)S(1)} %pad_clamp_fusion.2), kind=kCustom, calls=%fused_computation.clone.clone.1 | custom fusion | bytes 25166336 | tf_op jit(solution)/shard_map/while/body/eval_jaxpr/gather | solution.py:79
  448.8 8.6 %fusion.67 = f32[64,12288]{1,0:T(8,128)S(1)} fusion(bf16[64,512]{1,0:T(8,128)(2,1)S(1)} %bitcast.64, bf16[12288,512]{1,0:T(8,128)(2,1)} %bitcast.58), kind=kOutput, calls=%fused_computation.46.clone.1 | convolution fusion | flops 805306368 | bytes 15794176 | tf_op jit(solution)/shard_map/while/body/eval_jaxpr/dot_general | solution.py:14
  457.4 1.4 fusion.68
  458.8 0.8 slice-done.2
  459.5 2.3 fusion.71
  461.9 0.8 fusion.72
  468.8 6.5 %gather_fusion.1 = bf16[128,6144]{1,0:T(8,128)(2,1)} fusion(bf16[256,6144]{1,0:T(8,128)(2,1)} %get-tuple-element.277, s32[1024]{0:T(1024)S(1)} %pad_clamp_fusion.2), kind=kCustom, calls=%fused_computation.1.clone.clone.1 | custom fusion | bytes 3146240 | tf_op jit(solution)/shard_map/while/body/eval_jaxpr/gather | solution.py:80
  475.3 4.3 reshape.86
  479.6 16.6 %gather_fusion = bf16[128,96,512]{2,1,0:T(8,128)(2,1)} fusion(bf16[256,96,512]{2,1,0:T(8,128)(2,1)} %get-tuple-element.275, s32[1024]{0:T(1024)S(1)} %pad_clamp_fusion.2), kind=kCustom, calls=%fused_computation.clone.clone.1 | custom fusion | bytes 25166336 | tf_op jit(solution)/shard_map/while/body/eval_jaxpr/gather | solution.py:79
  496.2 8.6 %fusion.67 = f32[64,12288]{1,0:T(8,128)S(1)} fusion(bf16[64,512]{1,0:T(8,128)(2,1)S(1)} %bitcast.64, bf16[12288,512]{1,0:T(8,128)(2,1)} %bitcast.58), kind=kOutput, calls=%fused_computation.46.clone.1 | convolution fusion | flops 805306368 | bytes 15794176 | tf_op jit(solution)/shard_map/while/body/eval_jaxpr/dot_general | solution.py:14
  504.8 1.4 fusion.68
  506.2 0.8 slice-done.2
  507.0 2.3 fusion.71
  509.4 0.8 fusion.72
  (73 shorter events, 9.1 us)
Async XLA Ops:
  45.5 144.9 %all-to-all-start = ((bf16[64,96,512]{2,1,0:T(8,128)(2,1)}), bf16[64,96,512]{2,1,0:T(8,128)(2,1)}, u32[]{:S(2)}, u32[]{:S(2)}) async-start(bf16[64,96,512]{2,1,0:T(8,128)(2,1)} %param.10), calls=%async_computation | async-start | bytes 12582912 | tf_op jit(solution)/shard_map/all_to_all | solution.py:55
  51.9 140.8 %all-gather.6.cloned.1.call-start = ((), (), s32[]{:S(2)}) async-start(), calls=%async_computation.3 | async-start | bytes 3932160 | tf_op jit(solution)/shard_map/all_gather | solution.py:68
  53.9 362.2 %all-gather.4.cloned.1.call-start = ((), (), s32[]{:S(2)}) async-start(), calls=%async_computation.2 | async-start | bytes 31457280 | tf_op jit(solution)/shard_map/all_gather | solution.py:67
  190.4 0.7 copy-start.4
  190.4 225.7 %copy-start = (bf16[2,2,32,512]{3,2,1,0:T(8,128)(2,1)S(1)}, bf16[2,2,32,512]{3,2,1,0:T(8,128)(2,1)}, u32[]{:S(2)}) copy-start(bf16[2,2,32,512]{3,2,1,0:T(8,128)(2,1)} %param.14) | copy-start | bytes 393220
  190.4 225.7 %copy-start.1 = (bf16[2,2,32,64]{3,2,1,0:T(8,128)(2,1)S(1)}, bf16[2,2,32,64]{3,2,1,0:T(8,128)(2,1)}, u32[]{:S(2)}) copy-start(bf16[2,2,32,64]{3,2,1,0:T(8,128)(2,1)} %param.15) | copy-start | bytes 49156
  190.4 225.7 %copy-start.2 = (bf16[2,2,512]{2,1,0:T(2,128)(2,1)S(1)}, bf16[2,2,512]{2,1,0:T(2,128)(2,1)}, u32[]{:S(2)}) copy-start(bf16[2,2,512]{2,1,0:T(2,128)(2,1)} %param.16) | copy-start | bytes 12292
  190.4 225.7 %copy-start.3 = (bf16[2,2,64]{2,1,0:T(2,128)(2,1)S(1)}, bf16[2,2,64]{2,1,0:T(2,128)(2,1)}, u32[]{:S(2)}) copy-start(bf16[2,2,64]{2,1,0:T(2,128)(2,1)} %param.17) | copy-start | bytes 1540
  190.4 225.7 %copy-start.7 = (s32[2]{0:T(128)S(1)}, s32[2]{0:T(128)}, u32[]{:S(2)}) copy-start(s32[2]{0:T(128)} %param.13) | copy-start | bytes 28
  448.8 10.0 %slice-start = ((s8[12582912]{0:T(1024)(128)(4,1)}), s8[4194304]{0:T(1024)(128)(4,1)S(1)}, s32[]{:S(2)}) async-start(s8[12582912]{0:T(1024)(128)(4,1)} %bitcast.59), calls=%async_computation.4 | async-start | bytes 8388608 | tf_op jit(solution)/shard_map/while
  448.8 10.0 %slice-start.1 = ((s8[12582912]{0:T(1024)(128)(4,1)}), s8[4194304]{0:T(1024)(128)(4,1)S(1)}, s32[]{:S(2)}) async-start(s8[12582912]{0:T(1024)(128)(4,1)} %bitcast.59), calls=%async_computation.5 | async-start | bytes 8388608 | tf_op jit(solution)/shard_map/while
  457.3 2.2 slice-start.2
  461.9 1.1 copy-start.5
  463.0 0.7 copy-start.6
  496.2 10.0 %slice-start = ((s8[12582912]{0:T(1024)(128)(4,1)}), s8[4194304]{0:T(1024)(128)(4,1)S(1)}, s32[]{:S(2)}) async-start(s8[12582912]{0:T(1024)(128)(4,1)} %bitcast.59), calls=%async_computation.4 | async-start | bytes 8388608 | tf_op jit(solution)/shard_map/while
  496.2 10.0 %slice-start.1 = ((s8[12582912]{0:T(1024)(128)(4,1)}), s8[4194304]{0:T(1024)(128)(4,1)S(1)}, s32[]{:S(2)}) async-start(s8[12582912]{0:T(1024)(128)(4,1)} %bitcast.59), calls=%async_computation.5 | async-start | bytes 8388608 | tf_op jit(solution)/shard_map/while
  504.8 2.2 slice-start.2
  509.4 1.1 copy-start.5
  510.5 0.7 copy-start.6
Sparse Core Ops, SparseCore 0:
  54.5 43.2 all-gather.5
  190.6 225.4 all-gather.3
where the time goes:
time: 519 us; the launch traced here: 518 us
  waiting for transfers between devices  360 us (69%)
  local copies, waits for them, and re-layouts  65.7 us (13%)
  blocking collectives  35.5 us (7%)
  matrix products  25.6 us (5%)
  between operations  13.5 us (3%)
  starting transfers between devices  6.49 us (1%)
  loops' own time  5.65 us (1%)
  other arithmetic  5.63 us (1%)
    all_gather x1, waiting for transfers between devices, on_device(): lax.all_gather(recv_lat, 'head', axis=0, tiled=True)  223 us
    all_to_all x1, waiting for transfers between devices, on_device(): lax.all_to_all(latent_pages, 'req', split_axis=0, concat_axis=0, tiled=True)  136 us
    all_to_all x1, blocking collectives, on_device(): lax.all_to_all(rope_pages, 'req', split_axis=0, concat_axis=0, tiled=True)  35.5 us
    gather x2, local copies, waits for them, and re-layouts, one_request(): latent_rows = whole_lat[slots].reshape(per_request * page_len, width)  33.3 us
    dot_general x8, matrix products, contract(): lax.dot_general(left, right, (((1,), (1,)), ((), ())), preferred_element_...  20.5 us
    gather x2, local copies, waits for them, and re-layouts, one_request(): rope_rows = whole_rope[slots].reshape(per_request * page_len, rope_width)  13 us
  transfers between devices with their start and end apart: 3, of which 2 were waited for; matrix products, arithmetic and copies ran while one was open for 1% of the time, Pallas kernels for 0%

commit v1 on v0

v1 whole, which is shorter than its diff:
```python
import functools

import jax
import jax.numpy as jnp
from jax import lax
from jax.experimental import pallas as pl
from jax.experimental.pallas import tpu as pltpu
from jax.sharding import PartitionSpec as P

ROPE = 64
NOPE = 128
SCALE = float(NOPE + ROPE) ** -0.5
NEG = -1e30

NZ, NX, NC, NY = 8, 4, 2, 4
AXES = ("req", "head")
PAIRS = NZ // 2
SLOTS = NZ * NX * NC
PAGE = 96
BLOCK = 4
TOKENS = BLOCK * PAGE
ROWS = 64
META = 16


def device_id(z, x, core, y):
    return ((z * NX + x) * NC + core) * NY + y


def page_groups():
    return [
        [
            device_id(2 * j + zo % 2, x, c, (zo // 2 + j) % NY)
            for zo in range(NZ)
            for x in range(NX)
            for c in range(NC)
        ]
        for j in range(PAIRS)
    ]


def home_pairs(d):
    pairs = []
    for z in range(NZ):
        for x in range(NX):
            for c in range(NC):
                for y in range(NY):
                    zo = 2 * ((y - z // 2) % PAIRS) + z % 2
                    pairs.append((device_id(z, x, c, y), device_id(zo, x, c, (y + d) % NY)))
    return pairs


def contract(left, right):
    return lax.dot_general(
        left, right, (((1,), (1,)), ((), ())), preferred_element_type=jnp.float32
    )


def attend_kernel(
    order_ref, valid_ref, count_ref, lat_ref, rope_ref, q0, q1, q2, q3, o0, o1, o2, o3,
    score_ref, acc_ref, total_ref
):
    queries, outs = (q0, q1, q2, q3), (o0, o1, o2, o3)
    token = lax.broadcasted_iota(jnp.int32, (TOKENS, TOKENS // 2), 0)
    pair = lax.broadcasted_iota(jnp.int32, (TOKENS, TOKENS // 2), 1)
    spread = (token // 2 == pair).astype(jnp.bfloat16)
    half = (
        lax.broadcasted_iota(jnp.int32, (TOKENS, 2 * ROPE), 0) % 2
        == lax.broadcasted_iota(jnp.int32, (TOKENS, 2 * ROPE), 1) // ROPE
    )
    lane = lax.broadcasted_iota(jnp.int32, (1, TOKENS), 1)
    sums = []
    for request in range(2):
        rows = slice(request * ROWS, (request + 1) * ROWS)
        query = jnp.concatenate([q[rows, :] for q in queries], axis=0)
        query_lat, query_rope = query[:, :512], query[:, 512:]
        start = count_ref[0] * request
        count = count_ref[request]
        blocks = (count + BLOCK - 1) // BLOCK

        def slot(block, index):
            return order_ref[jnp.minimum(start + block * BLOCK + index, SLOTS - 1)]

        def latents(block):
            return jnp.concatenate([lat_ref[slot(block, i)] for i in range(BLOCK)], axis=0)

        def score_block(block, maxima):
            keys = latents(block)
            pairs = jnp.concatenate([rope_ref[slot(block, i)] for i in range(BLOCK)], axis=0)
            spread_keys = jnp.dot(spread, pairs, preferred_element_type=jnp.float32)
            rope_keys = jnp.where(half, spread_keys, 0.0).astype(jnp.bfloat16)
            score = contract(query_lat, keys) + contract(query_rope, rope_keys)
            limit = jnp.zeros((1, TOKENS), jnp.int32)
            for i in range(BLOCK):
                place = block * BLOCK + i
                valid = valid_ref[jnp.minimum(start + place, SLOTS - 1)]
                valid = jnp.where(place < count, valid, 0)
                limit = jnp.where(lane >= i * PAGE, i * PAGE + valid, limit)
            score = score * SCALE + jnp.where(lane < limit, 0.0, NEG)
            score_ref[block] = score
            for i in range(TOKENS // 128):
                maxima = jnp.maximum(maxima, score[:, i * 128 : (i + 1) * 128])
            return maxima

        maxima = lax.fori_loop(
            0, blocks, score_block, jnp.full((4 * ROWS, 128), NEG, jnp.float32)
        )
        top = jnp.max(maxima, axis=1, keepdims=True)
        acc_ref[...] = jnp.zeros_like(acc_ref)
        total_ref[...] = jnp.zeros_like(total_ref)

        def weigh_block(block, carry):
            weight = jnp.exp(score_ref[block] - top)
            part = weight[:, :128]
            for i in range(1, TOKENS // 128):
                part = part + weight[:, i * 128 : (i + 1) * 128]
            total_ref[...] += part
            acc_ref[...] += jnp.dot(
                weight.astype(jnp.bfloat16), latents(block), preferred_element_type=jnp.float32
            )
            return carry

        lax.fori_loop(0, blocks, weigh_block, 0)
        total = jnp.sum(total_ref[...], axis=1, keepdims=True)
        total = jnp.where(total > 0.0, total, 1.0)
        result = (acc_ref[...] / total).astype(jnp.bfloat16)
        sums.append(top + jnp.log(total))
        for out, i in zip(outs, range(4)):
            out[rows, :] = result[i * ROWS : (i + 1) * ROWS, :]
    lane = lax.broadcasted_iota(jnp.int32, (4 * ROWS, 128), 1)
    meta = jnp.zeros((4 * ROWS, 128), jnp.float32)
    for request in range(2):
        rest = sums[request]
        for part in range(3):
            piece = rest.astype(jnp.bfloat16).astype(jnp.float32)
            meta = jnp.where(lane == request * 3 + part, piece, meta)
            rest = rest - piece
    meta = meta.astype(jnp.bfloat16)
    for out, i in zip(outs, range(4)):
        part = meta[i * ROWS : (i + 1) * ROWS, :]
        out[2 * ROWS :, :] = jnp.concatenate(
            [part[k * META : (k + 1) * META, :] for k in range(4)], axis=1
        )


def merge_kernel(p0, p1, p2, p3, query_ref, new_lat_ref, new_rope_ref, out_ref):
    parts = (p0, p1, p2, p3)
    meta = [
        jnp.concatenate(
            [p[2 * ROWS :, k * 128 : (k + 1) * 128] for k in range(4)], axis=0
        ).astype(jnp.float32)
        for p in parts
    ]
    first_step = lax.broadcasted_iota(jnp.int32, (ROWS, 1), 0) < ROWS // 2
    for request in range(2):
        rows = slice(request * ROWS, (request + 1) * ROWS)
        query = query_ref[rows, :].astype(jnp.float32)
        fresh = []
        for step in range(2):
            key = new_lat_ref[request, step : step + 1, :].astype(jnp.float32)
            rope = new_rope_ref[request, step : step + 1, :].astype(jnp.float32)
            score = jnp.sum(query[:, :512] * key, axis=1, keepdims=True)
            score = score + jnp.sum(query[:, 512 : 512 + ROPE] * rope, axis=1, keepdims=True)
            fresh.append((score * SCALE, key))
        later = jnp.where(first_step, NEG, fresh[1][0])
        fresh[1] = (later, fresh[1][1])
        sums = [
            m[:, 3 * request : 3 * request + 1]
            + m[:, 3 * request + 1 : 3 * request + 2]
            + m[:, 3 * request + 2 : 3 * request + 3]
            for m in meta
        ]
        top = functools.reduce(jnp.maximum, sums + [s for s, _ in fresh])
        total = jnp.zeros((ROWS, 1), jnp.float32)
        acc = jnp.zeros((ROWS, 512), jnp.float32)
        for p, s in zip(parts, sums):
            weight = jnp.exp(s - top)
            total = total + weight
            acc = acc + weight * p[rows, :].astype(jnp.float32)
        for score, key in fresh:
            weight = jnp.exp(score - top)
            total = total + weight
            acc = acc + weight.astype(jnp.bfloat16).astype(jnp.float32) * key
        out_ref[request] = (acc / total).astype(jnp.bfloat16)


def page_table(query, pair):
    row = query[2 * ROWS].astype(jnp.int32)
    slot = jnp.arange(SLOTS, dtype=jnp.int32)
    zo, xc = slot // (NX * NC), slot % (NX * NC)
    holder = (2 * pair + zo % 2) * (NX * NC) + xc
    place = row[((zo // 2 + pair) % NY) * SLOTS + holder]
    request = place // 128
    length = jnp.where(
        request == 0, row[256] * 128 + row[258], row[257] * 128 + row[259]
    )
    valid = jnp.clip(length - (place % 128) * PAGE, 0, PAGE)
    key = jnp.where(valid > 0, request, 2)
    before = (key[None, :] < key[:, None]) | (
        (key[None, :] == key[:, None]) & (slot[None, :] < slot[:, None])
    )
    rank = jnp.sum(before.astype(jnp.int32), axis=1)
    hit = rank[:, None] == slot[None, :]
    order = jnp.sum(jnp.where(hit, slot[:, None], 0), axis=0)
    valid = jnp.sum(jnp.where(hit, valid[:, None], 0), axis=0)
    count = jnp.stack([jnp.sum((key == r).astype(jnp.int32)) for r in range(2)])
    return order, valid, count


def on_device(
    latent_pages, rope_pages, page_place, lengths, q_latent, q_rope, new_latent, new_rope
):
    groups = page_groups()
    pair = lax.axis_index("req") // (2 * NX * NC)
    rope_keys = q_rope.reshape(2 * ROWS, ROPE)
    place = page_place.astype(jnp.bfloat16)
    length = jnp.concatenate([lengths // 128, lengths % 128]).astype(jnp.bfloat16)
    row = jnp.concatenate([place, length, jnp.zeros((640 - 260,), jnp.bfloat16)])
    query = jnp.concatenate([q_latent.reshape(2 * ROWS, 512), rope_keys, rope_keys], axis=1)
    query = jnp.concatenate(
        [query, row[None, :], jnp.zeros((META - 1, 640), jnp.bfloat16)], axis=0
    )
    queries = [
        lax.ppermute(query, AXES, [(b, a) for a, b in home_pairs(d)]) for d in range(4)
    ]
    exchange = functools.partial(
        lax.all_to_all,
        axis_name=AXES,
        split_axis=0,
        concat_axis=0,
        axis_index_groups=groups,
        tiled=True,
    )
    rope = exchange(rope_pages.reshape(SLOTS, PAGE // 2, 2 * ROPE))
    lat = exchange(latent_pages)
    order, valid, count = page_table(queries[0], pair)
    whole = pl.BlockSpec(memory_space=pltpu.VMEM)
    scalars = pl.BlockSpec(memory_space=pltpu.SMEM)
    partial = jax.ShapeDtypeStruct((2 * ROWS + META, 512), jnp.bfloat16)
    parts = pl.pallas_call(
        attend_kernel,
        out_shape=[partial] * 4,
        in_specs=[scalars] * 3 + [whole] * 6,
        out_specs=[whole] * 4,
        scratch_shapes=[
            pltpu.VMEM((SLOTS // BLOCK, 4 * ROWS, TOKENS), jnp.float32),
            pltpu.VMEM((4 * ROWS, 512), jnp.float32),
            pltpu.VMEM((4 * ROWS, 128), jnp.float32),
        ],
        compiler_params=pltpu.CompilerParams(vmem_limit_bytes=40 * 1024 * 1024),
        cost_estimate=pl.CostEstimate(
            flops=4 * ROWS * 6144 * 1152 * 2, bytes_accessed=8 << 20, transcendentals=1 << 20
        ),
        name="attend",
    )(order, valid, count, lat, rope, *queries)
    home = [lax.ppermute(part, AXES, home_pairs(d)) for d, part in enumerate(parts)]
    out = pl.pallas_call(
        merge_kernel,
        out_shape=jax.ShapeDtypeStruct((2, ROWS, 512), jnp.bfloat16),
        in_specs=[whole] * 7,
        out_specs=whole,
        name="merge",
    )(*home, query, new_latent, new_rope)
    return out.reshape(q_latent.shape)


def solution(mesh):
    return jax.shard_map(
        on_device,
        mesh=mesh,
        in_specs=(
            P(("req", "head"), None, None),
            P(("req", "head"), None),
            P("req"),
            P("req"),
            P("req", None, "head", None),
            P("req", None, "head", None),
            P("req", None, None),
            P("req", None, None),
        ),
        out_specs=P("req", None, "head", None),
        check_vma=False,
    )
```

time: 519 us -> 179 us (0.34)
  the two profiles are of different devices: /device:TPU:1 before, /device:TPU:72 now
where the time goes in v1:
time: 179 us; the launch traced here: 176 us
  waiting for transfers between devices  94.9 us (53%)
  starting transfers between devices  37.4 us (21%)
  blocking collectives  23.3 us (13%)
  Pallas kernels  11.3 us (6%)
  local copies, waits for them, and re-layouts  4 us (2%)
  between operations  2.7 us (2%)
  other arithmetic  2.56 us (1%)
    ppermute x4, waiting for transfers between devices, on_device(): lax.ppermute(query, AXES, [(b, a) for a, b in home_pairs(d)])  78 us
    all_to_all x1, blocking collectives, on_device(): rope = exchange(rope_pages.reshape(SLOTS, PAGE // 2, 2 * ROPE))  23.3 us
    ppermute x4, starting transfers between devices, on_device(): lax.ppermute(part, AXES, home_pairs(d))  18.2 us
    ppermute x4, waiting for transfers between devices, on_device(): lax.ppermute(part, AXES, home_pairs(d))  16.9 us
    ppermute x4, starting transfers between devices, on_device(): lax.ppermute(query, AXES, [(b, a) for a, b in home_pairs(d)])  13.4 us
    pallas_call x1, Pallas kernels, on_device(): pl.pallas_call(attend_kernel, out_shape=[partial] * 4, in_specs=[scalars]...  8.97 us
    all_to_all x1, starting transfers between devices, on_device(): lat = exchange(latent_pages)  5.85 us
  transfers between devices with their start and end apart: 9, of which 4 were waited for; matrix products, arithmetic and copies ran while one was open for 2% of the time, Pallas kernels for 0%

profile of v1, /device:TPU:72, one launch (start us, length us, event | category | flops | bytes accessed | tf_op | source)
XLA Modules:
  0.0 176.1 jit_solution(1433122662641884077)
XLA Ops:
  0.0 1.3 copy.9
  1.3 23.3 %all_to_all.10.rope_ref = bf16[64,48,128]{2,1,0:T(8,128)(2,1)S(1)} all-to-all(bf16[64,48,128]{2,1,0:T(8,128)(2,1)S(1)} %bitcast.11), channel_id=1, replica_groups={{0,4,8,12,16,20,24,28,32,36,40,44,48,52,56,60,1,5,9,13,17,21,25,29,33,3..., dimensions={0} | all-to-all | bytes 1572864 | tf_op jit(solution)/shard_map/all_to_all | solution.py:234
  24.6 5.8 %all-to-all-start = ((bf16[64,96,512]{2,1,0:T(8,128)(2,1)}), bf16[64,96,512]{2,1,0:T(8,128)(2,1)}, u32[]{:S(2)}, u32[]{:S(2)}) async-start(bf16[64,96,512]{2,1,0:T(8,128)(2,1)} %param.8), calls=%async_computation | async-start | bytes 12582912 | tf_op jit(solution)/shard_map/all_to_all | solution.py:235
  30.6 0.1 maximum_maximum_fusion.query_ref
  30.8 2.4 %collective-permute-start = (bf16[144,640]{1,0:T(8,128)(2,1)S(1)}, bf16[144,640]{1,0:T(8,128)(2,1)S(1)}, u32[]{:S(2)}, u32[]{:S(2)}) collective-permute-start(bf16[144,640]{1,0:T(8,128)(2,1)S(1)} %maximum_maximum_fusion.query_ref), channel_id=1, source_target_pairs={{0,0},{65,1},{130,2},{195,3},{4,4},{69,5},{134,6},{199,7},{8,8},{7... | collective-permute-start | bytes 552968 | tf_op jit(solution)/shard_map/ppermute | solution.py:224
  33.2 6.6 %collective-permute-start.1 = (bf16[144,640]{1,0:T(8,128)(2,1)S(1)}, bf16[144,640]{1,0:T(8,128)(2,1)S(1)}, u32[]{:S(2)}, u32[]{:S(2)}) collective-permute-start(bf16[144,640]{1,0:T(8,128)(2,1)S(1)} %maximum_maximum_fusion.query_ref), channel_id=1, source_target_pairs={{1,0},{66,1},{131,2},{192,3},{5,4},{70,5},{135,6},{196,7},{9,8},{7... | collective-permute-start | bytes 552968 | tf_op jit(solution)/shard_map/ppermute | solution.py:224
  39.9 3.3 %collective-permute-start.2 = (bf16[144,640]{1,0:T(8,128)(2,1)S(1)}, bf16[144,640]{1,0:T(8,128)(2,1)S(1)}, u32[]{:S(2)}, u32[]{:S(2)}) collective-permute-start(bf16[144,640]{1,0:T(8,128)(2,1)S(1)} %maximum_maximum_fusion.query_ref), channel_id=1, source_target_pairs={{2,0},{67,1},{128,2},{193,3},{6,4},{71,5},{132,6},{197,7},{10,8},{... | collective-permute-start | bytes 552968 | tf_op jit(solution)/shard_map/ppermute | solution.py:224
  43.2 1.0 collective-permute-start.3
  44.2 76.0 %collective-permute-done.q0 = bf16[144,640]{1,0:T(8,128)(2,1)S(1)} collective-permute-done((bf16[144,640]{1,0:T(8,128)(2,1)S(1)}, bf16[144,640]{1,0:T(8,128)(2,1)S(1)}, u32[]{:S(2)}, u32[]{:S(2)}) %collective-permute-start) | collective-permute-done | bytes 184352 | tf_op jit(solution)/shard_map/ppermute | solution.py:224
  120.2 0.6 fusion.18
  122.1 0.7 gather_fusion
  124.1 0.7 fusion.10
  124.8 0.2 convert_reduce_fusion
  125.0 1.3 pad_add_fusion.count_ref
  126.4 2.0 %collective-permute-done.1.q1 = bf16[144,640]{1,0:T(8,128)(2,1)S(1)} collective-permute-done((bf16[144,640]{1,0:T(8,128)(2,1)S(1)}, bf16[144,640]{1,0:T(8,128)(2,1)S(1)}, u32[]{:S(2)}, u32[]{:S(2)}) %collective-permute-start.1) | collective-permute-done | bytes 184352 | tf_op jit(solution)/shard_map/ppermute | solution.py:224
  128.4 9.0 %attend.1 = (bf16[144,512]{1,0:T(8,128)(2,1)S(1)}, bf16[144,512]{1,0:T(8,128)(2,1)S(1)}, bf16[144,512]{1,0:T(8,128)(2,1)S(1)}, bf16[144,512]{1,0:T(8,128)(2,1)S(1)}) custom-call(s32[64]{0:T(128)S(1)} %get-tuple-element.16.order_ref, s32[64]{0:T(128)S(1)} %get-tuple-element.15.valid_ref, s32[2]{0:T(128)S(1)} %pad_add_fusion.count_ref, ...), custom_call_target="tpu_custom_call" | custom-call | flops 3623878656 | bytes 8388608 | tf_op jit(solution)/shard_map/attend/pallas_call | solution.py:240
  137.4 1.9 %collective-permute-start.4 = (bf16[144,512]{1,0:T(8,128)(2,1)S(1)}, bf16[144,512]{1,0:T(8,128)(2,1)S(1)}, u32[]{:S(2)}, u32[]{:S(2)}) collective-permute-start(bf16[144,512]{1,0:T(8,128)(2,1)S(1)} %get-tuple-element.9), channel_id=1, source_target_pairs={{0,0},{1,65},{2,130},{3,195},{4,4},{5,69},{6,134},{7,199},{8,8},{9... | collective-permute-start | bytes 442376 | tf_op jit(solution)/shard_map/ppermute | solution.py:256
  139.4 5.0 %collective-permute-start.5 = (bf16[144,512]{1,0:T(8,128)(2,1)S(1)}, bf16[144,512]{1,0:T(8,128)(2,1)S(1)}, u32[]{:S(2)}, u32[]{:S(2)}) collective-permute-start(bf16[144,512]{1,0:T(8,128)(2,1)S(1)} %get-tuple-element.10), channel_id=1, source_target_pairs={{0,1},{1,66},{2,131},{3,192},{4,5},{5,70},{6,135},{7,196},{8,9},{9... | collective-permute-start | bytes 442376 | tf_op jit(solution)/shard_map/ppermute | solution.py:256
  144.4 11.2 %collective-permute-start.6 = (bf16[144,512]{1,0:T(8,128)(2,1)S(1)}, bf16[144,512]{1,0:T(8,128)(2,1)S(1)}, u32[]{:S(2)}, u32[]{:S(2)}) collective-permute-start(bf16[144,512]{1,0:T(8,128)(2,1)S(1)} %get-tuple-element.11), channel_id=1, source_target_pairs={{0,2},{1,67},{2,128},{3,193},{4,6},{5,71},{6,132},{7,197},{8,10},{... | collective-permute-start | bytes 442376 | tf_op jit(solution)/shard_map/ppermute | solution.py:256
  155.6 3.2 %collective-permute-done.5.p1 = bf16[144,512]{1,0:T(8,128)(2,1)S(1)} collective-permute-done((bf16[144,512]{1,0:T(8,128)(2,1)S(1)}, bf16[144,512]{1,0:T(8,128)(2,1)S(1)}, u32[]{:S(2)}, u32[]{:S(2)}) %collective-permute-start.5) | collective-permute-done | bytes 147488 | tf_op jit(solution)/shard_map/ppermute | solution.py:256
  158.9 13.6 %collective-permute-done.6.p2 = bf16[144,512]{1,0:T(8,128)(2,1)S(1)} collective-permute-done((bf16[144,512]{1,0:T(8,128)(2,1)S(1)}, bf16[144,512]{1,0:T(8,128)(2,1)S(1)}, u32[]{:S(2)}, u32[]{:S(2)}) %collective-permute-start.6) | collective-permute-done | bytes 147488 | tf_op jit(solution)/shard_map/ppermute | solution.py:256
  172.5 0.6 copy-done.3
  173.1 0.6 copy-done.4
  173.8 2.4 %merge.1 = bf16[2,64,512]{2,1,0:T(8,128)(2,1)} custom-call(bf16[144,512]{1,0:T(8,128)(2,1)} %copy-done.1, bf16[144,512]{1,0:T(8,128)(2,1)} %copy-done.2, bf16[144,512]{1,0:T(8,128)(2,1)} %copy-done.3, bf16[144,512]{1,0:T(8,128)(2,1)} %copy-done.4, bf16[144,640]{1,0:T(8,128)(2,1)} %copy-done, bf16[2,2,512]{2,1,0:T(2,128)(2,1)} %new_lat_ref.1, ...), custom_call_target="tpu_custom_call" | custom-call | tf_op jit(solution)/shard_map/merge/pallas_call | solution.py:257
  (34 shorter events, 0.4 us)
Async XLA Ops:
  24.5 5.9 %copy-start.7 = (s32[256]{0:T(256)S(1)}, s32[256]{0:T(256)}, u32[]{:S(2)}) copy-start(s32[256]{0:T(256)} %param.10) | copy-start | bytes 3076
  24.5 5.9 %copy-start.8 = (s32[2]{0:T(128)S(1)}, s32[2]{0:T(128)}, u32[]{:S(2)}) copy-start(s32[2]{0:T(128)} %param.11) | copy-start | bytes 28
  24.5 6.1 %copy-start.5 = (bf16[2,2,32,512]{3,2,1,0:T(8,128)(2,1)S(1)}, bf16[2,2,32,512]{3,2,1,0:T(8,128)(2,1)}, u32[]{:S(2)}) copy-start(bf16[2,2,32,512]{3,2,1,0:T(8,128)(2,1)} %param.12) | copy-start | bytes 393220
  24.5 6.1 %copy-start.6 = (bf16[2,2,32,64]{3,2,1,0:T(8,128)(2,1)S(1)}, bf16[2,2,32,64]{3,2,1,0:T(8,128)(2,1)}, u32[]{:S(2)}) copy-start(bf16[2,2,32,64]{3,2,1,0:T(8,128)(2,1)} %param.13) | copy-start | bytes 49156
  24.6 103.9 %all-to-all-start = ((bf16[64,96,512]{2,1,0:T(8,128)(2,1)}), bf16[64,96,512]{2,1,0:T(8,128)(2,1)}, u32[]{:S(2)}, u32[]{:S(2)}) async-start(bf16[64,96,512]{2,1,0:T(8,128)(2,1)} %param.8), calls=%async_computation | async-start | bytes 12582912 | tf_op jit(solution)/shard_map/all_to_all | solution.py:235
  30.8 106.7 %copy-start = (bf16[144,640]{1,0:T(8,128)(2,1)}, bf16[144,640]{1,0:T(8,128)(2,1)S(1)}, u32[]{:S(2)}) copy-start(bf16[144,640]{1,0:T(8,128)(2,1)S(1)} %maximum_maximum_fusion.query_ref) | copy-start | bytes 552964
  30.8 89.4 %collective-permute-start = (bf16[144,640]{1,0:T(8,128)(2,1)S(1)}, bf16[144,640]{1,0:T(8,128)(2,1)S(1)}, u32[]{:S(2)}, u32[]{:S(2)}) collective-permute-start(bf16[144,640]{1,0:T(8,128)(2,1)S(1)} %maximum_maximum_fusion.query_ref), channel_id=1, source_target_pairs={{0,0},{65,1},{130,2},{195,3},{4,4},{69,5},{134,6},{199,7},{8,8},{7... | collective-permute-start | bytes 552968 | tf_op jit(solution)/shard_map/ppermute | solution.py:224
  33.2 95.2 %collective-permute-start.1 = (bf16[144,640]{1,0:T(8,128)(2,1)S(1)}, bf16[144,640]{1,0:T(8,128)(2,1)S(1)}, u32[]{:S(2)}, u32[]{:S(2)}) collective-permute-start(bf16[144,640]{1,0:T(8,128)(2,1)S(1)} %maximum_maximum_fusion.query_ref), channel_id=1, source_target_pairs={{1,0},{66,1},{131,2},{192,3},{5,4},{70,5},{135,6},{196,7},{9,8},{7... | collective-permute-start | bytes 552968 | tf_op jit(solution)/shard_map/ppermute | solution.py:224
  39.9 88.6 %collective-permute-start.2 = (bf16[144,640]{1,0:T(8,128)(2,1)S(1)}, bf16[144,640]{1,0:T(8,128)(2,1)S(1)}, u32[]{:S(2)}, u32[]{:S(2)}) collective-permute-start(bf16[144,640]{1,0:T(8,128)(2,1)S(1)} %maximum_maximum_fusion.query_ref), channel_id=1, source_target_pairs={{2,0},{67,1},{128,2},{193,3},{6,4},{71,5},{132,6},{197,7},{10,8},{... | collective-permute-start | bytes 552968 | tf_op jit(solution)/shard_map/ppermute | solution.py:224
  43.2 85.3 %collective-permute-start.3 = (bf16[144,640]{1,0:T(8,128)(2,1)S(1)}, bf16[144,640]{1,0:T(8,128)(2,1)S(1)}, u32[]{:S(2)}, u32[]{:S(2)}) collective-permute-start(bf16[144,640]{1,0:T(8,128)(2,1)S(1)} %maximum_maximum_fusion.query_ref), channel_id=1, source_target_pairs={{3,0},{64,1},{129,2},{194,3},{7,4},{68,5},{133,6},{198,7},{11,8},{... | collective-permute-start | bytes 552968 | tf_op jit(solution)/shard_map/ppermute | solution.py:224
  137.4 18.2 %collective-permute-start.4 = (bf16[144,512]{1,0:T(8,128)(2,1)S(1)}, bf16[144,512]{1,0:T(8,128)(2,1)S(1)}, u32[]{:S(2)}, u32[]{:S(2)}) collective-permute-start(bf16[144,512]{1,0:T(8,128)(2,1)S(1)} %get-tuple-element.9), channel_id=1, source_target_pairs={{0,0},{1,65},{2,130},{3,195},{4,4},{5,69},{6,134},{7,199},{8,8},{9... | collective-permute-start | bytes 442376 | tf_op jit(solution)/shard_map/ppermute | solution.py:256
  139.4 19.5 %collective-permute-start.5 = (bf16[144,512]{1,0:T(8,128)(2,1)S(1)}, bf16[144,512]{1,0:T(8,128)(2,1)S(1)}, u32[]{:S(2)}, u32[]{:S(2)}) collective-permute-start(bf16[144,512]{1,0:T(8,128)(2,1)S(1)} %get-tuple-element.10), channel_id=1, source_target_pairs={{0,1},{1,66},{2,131},{3,192},{4,5},{5,70},{6,135},{7,196},{8,9},{9... | collective-permute-start | bytes 442376 | tf_op jit(solution)/shard_map/ppermute | solution.py:256
  144.4 28.1 %collective-permute-start.6 = (bf16[144,512]{1,0:T(8,128)(2,1)S(1)}, bf16[144,512]{1,0:T(8,128)(2,1)S(1)}, u32[]{:S(2)}, u32[]{:S(2)}) collective-permute-start(bf16[144,512]{1,0:T(8,128)(2,1)S(1)} %get-tuple-element.11), channel_id=1, source_target_pairs={{0,2},{1,67},{2,128},{3,193},{4,6},{5,71},{6,132},{7,197},{8,10},{... | collective-permute-start | bytes 442376 | tf_op jit(solution)/shard_map/ppermute | solution.py:256
  155.6 16.9 %collective-permute-start.7 = (bf16[144,512]{1,0:T(8,128)(2,1)S(1)}, bf16[144,512]{1,0:T(8,128)(2,1)S(1)}, u32[]{:S(2)}, u32[]{:S(2)}) collective-permute-start(bf16[144,512]{1,0:T(8,128)(2,1)S(1)} %get-tuple-element.12), channel_id=1, source_target_pairs={{0,3},{1,64},{2,129},{3,194},{4,7},{5,68},{6,133},{7,198},{8,11},{... | collective-permute-start | bytes 442376 | tf_op jit(solution)/shard_map/ppermute | solution.py:256
  155.6 16.9 %copy-start.1 = (bf16[144,512]{1,0:T(8,128)(2,1)}, bf16[144,512]{1,0:T(8,128)(2,1)S(1)}, u32[]{:S(2)}) copy-start(bf16[144,512]{1,0:T(8,128)(2,1)S(1)} %collective-permute-done.4.p0) | copy-start | bytes 442372
  158.8 13.6 %copy-start.2 = (bf16[144,512]{1,0:T(8,128)(2,1)}, bf16[144,512]{1,0:T(8,128)(2,1)S(1)}, u32[]{:S(2)}) copy-start(bf16[144,512]{1,0:T(8,128)(2,1)S(1)} %collective-permute-done.5.p1) | copy-start | bytes 442372
  172.5 0.6 copy-start.3
  173.1 0.7 copy-start.4

commit v2 on v1

v2 whole, which is shorter than its diff:
```python
import functools

import jax
import jax.numpy as jnp
from jax import lax
from jax.experimental import pallas as pl
from jax.experimental.pallas import tpu as pltpu
from jax.sharding import PartitionSpec as P

ROPE = 64
NOPE = 128
SCALE = float(NOPE + ROPE) ** -0.5
NEG = -1e30

NZ, NX, NC, NY = 8, 4, 2, 4
AXES = ("req", "head")
PAIRS = NZ // 2
SLOTS = NZ * NX * NC
PAGE = 96
BLOCK = 8
TOKENS = BLOCK * PAGE
ROWS = 64
META = 16


def device_id(z, x, core, y):
    return ((z * NX + x) * NC + core) * NY + y


def served_pair(pair, y, core):
    shift = y + 2 * (pair % 2)
    return (pair + (1 - 2 * core) * shift) % PAIRS


def serving_y(owner_pair, pair, core):
    return ((1 - 2 * core) * (owner_pair - pair) - 2 * (pair % 2)) % NY


def devices():
    return [
        (z, x, c, y) for z in range(NZ) for x in range(NX) for c in range(NC) for y in range(NY)
    ]


def page_groups():
    return [
        [
            device_id(2 * j + zo % 2, x, c, serving_y(zo // 2, j, c))
            for zo in range(NZ)
            for x in range(NX)
            for c in range(NC)
        ]
        for j in range(PAIRS)
    ]


def home_pairs(d):
    return [
        (
            device_id(z, x, c, y),
            device_id(2 * served_pair(z // 2, y, c) + z % 2, x, c, (y + d) % NY),
        )
        for z, x, c, y in devices()
    ]


def contract(left, right):
    return lax.dot_general(
        left, right, (((1,), (1,)), ((), ())), preferred_element_type=jnp.float32
    )


def attend_kernel(
    order_ref, rope_order_ref, valid_ref, count_ref, lat_ref, rope_ref, query_ref,
    o0, o1, o2, o3, page_ref, score_ref, acc_ref, sems
):
    outs = (o0, o1, o2, o3)

    def copy(place):
        return pltpu.make_async_copy(
            lat_ref.at[order_ref[place]], page_ref.at[place], sems.at[place]
        )

    def begin(place, carry):
        copy(place).start()
        return carry

    lax.fori_loop(0, count_ref[0] + count_ref[1], begin, 0)
    token = lax.broadcasted_iota(jnp.int32, (TOKENS, TOKENS // 2), 0)
    pair = lax.broadcasted_iota(jnp.int32, (TOKENS, TOKENS // 2), 1)
    spread = (token // 2 == pair).astype(jnp.bfloat16)
    half = (
        lax.broadcasted_iota(jnp.int32, (TOKENS, 2 * ROPE), 0) % 2
        == lax.broadcasted_iota(jnp.int32, (TOKENS, 2 * ROPE), 1) // ROPE
    )
    lane = lax.broadcasted_iota(jnp.int32, (1, TOKENS), 1)
    meta_lane = lax.broadcasted_iota(jnp.int32, (4 * ROWS, 128), 1)
    meta = jnp.zeros((4 * ROWS, 128), jnp.float32)
    for request in range(2):
        rows = slice(request * ROWS, (request + 1) * ROWS)
        start = count_ref[0] * request
        count = count_ref[request]
        blocks = (count + BLOCK - 1) // BLOCK

        def place_of(block, index):
            return start + jnp.minimum(block * BLOCK + index, count - 1)

        def latents(block):
            return jnp.concatenate([page_ref[place_of(block, i)] for i in range(BLOCK)], axis=0)

        def score_block(block, maxima):
            for i in range(BLOCK):

                @pl.when(block * BLOCK + i < count)
                def _():
                    copy(start + block * BLOCK + i).wait()

            pairs = jnp.concatenate(
                [rope_ref[rope_order_ref[place_of(block, i)]] for i in range(BLOCK)], axis=0
            )
            spread_keys = jnp.dot(spread, pairs, preferred_element_type=jnp.float32)
            rope_keys = jnp.where(half, spread_keys, 0.0).astype(jnp.bfloat16)
            keys = jnp.concatenate([latents(block), rope_keys], axis=1)
            limit = jnp.zeros((1, TOKENS), jnp.int32)
            for i in range(BLOCK):
                valid = jnp.where(block * BLOCK + i < count, valid_ref[place_of(block, i)], 0)
                limit = jnp.where(lane >= i * PAGE, i * PAGE + valid, limit)
            score = contract(query_ref[request], keys) * SCALE + jnp.where(lane < limit, 0.0, NEG)
            score_ref[block] = score
            for i in range(TOKENS // 128):
                maxima = jnp.maximum(maxima, score[:, i * 128 : (i + 1) * 128])
            return maxima

        maxima = lax.fori_loop(
            0, blocks, score_block, jnp.full((4 * ROWS, 128), NEG, jnp.float32)
        )
        top = jnp.max(maxima, axis=1, keepdims=True)
        acc_ref[...] = jnp.zeros_like(acc_ref)

        def weigh_block(block, total):
            weight = jnp.exp(score_ref[block] - top)
            for i in range(TOKENS // 128):
                total = total + weight[:, i * 128 : (i + 1) * 128]
            acc_ref[...] += jnp.dot(
                weight.astype(jnp.bfloat16), latents(block), preferred_element_type=jnp.float32
            )
            return total

        total = lax.fori_loop(
            0, blocks, weigh_block, jnp.zeros((4 * ROWS, 128), jnp.float32)
        )
        total = jnp.sum(total, axis=1, keepdims=True)
        total = jnp.where(total > 0.0, total, 1.0)
        result = (acc_ref[...] / total).astype(jnp.bfloat16)
        for i, out in enumerate(outs):
            out[rows, :] = result[i * ROWS : (i + 1) * ROWS, :]
        rest = top + jnp.log(total)
        for part in range(3):
            piece = rest.astype(jnp.bfloat16).astype(jnp.float32)
            meta = jnp.where(meta_lane == request * 3 + part, piece, meta)
            rest = rest - piece
    meta = meta.astype(jnp.bfloat16)
    for i, out in enumerate(outs):
        part = meta[i * ROWS : (i + 1) * ROWS, :]
        out[2 * ROWS :, :] = jnp.concatenate(
            [part[k * META : (k + 1) * META, :] for k in range(4)], axis=1
        )


def merge_kernel(
    p0, p1, p2, p3, query_lat_ref, query_rope_ref, new_lat_ref, new_rope_ref, out_ref
):
    parts = (p0, p1, p2, p3)
    meta = [
        jnp.concatenate(
            [p[2 * ROWS :, k * 128 : (k + 1) * 128] for k in range(4)], axis=0
        ).astype(jnp.float32)
        for p in parts
    ]
    first_step = lax.broadcasted_iota(jnp.int32, (ROWS, 1), 0) < ROWS // 2
    for request in range(2):
        rows = slice(request * ROWS, (request + 1) * ROWS)
        query_lat = query_lat_ref[rows, :].astype(jnp.float32)
        query_rope = query_rope_ref[rows, :].astype(jnp.float32)
        fresh = []
        for step in range(2):
            key = new_lat_ref[request, step : step + 1, :].astype(jnp.float32)
            rope = new_rope_ref[request, step : step + 1, :].astype(jnp.float32)
            score = jnp.sum(query_lat * key, axis=1, keepdims=True)
            score = score + jnp.sum(query_rope * rope, axis=1, keepdims=True)
            fresh.append((score * SCALE, key))
        later = jnp.where(first_step, NEG, fresh[1][0])
        fresh[1] = (later, fresh[1][1])
        sums = [
            m[:, 3 * request : 3 * request + 1]
            + m[:, 3 * request + 1 : 3 * request + 2]
            + m[:, 3 * request + 2 : 3 * request + 3]
            for m in meta
        ]
        top = functools.reduce(jnp.maximum, sums + [s for s, _ in fresh])
        total = jnp.zeros((ROWS, 1), jnp.float32)
        acc = jnp.zeros((ROWS, 512), jnp.float32)
        for p, s in zip(parts, sums):
            weight = jnp.exp(s - top)
            total = total + weight
            acc = acc + weight * p[rows, :].astype(jnp.float32)
        for score, key in fresh:
            weight = jnp.exp(score - top)
            total = total + weight
            acc = acc + weight.astype(jnp.bfloat16).astype(jnp.float32) * key
        out_ref[request] = (acc / total).astype(jnp.bfloat16)


def page_table(row, pair, a, x, c, y):
    slot = jnp.arange(SLOTS, dtype=jnp.int32)
    owner_pair, a_from = slot // (2 * NX * NC), slot // (NX * NC) % 2
    x_from, c_from = slot // NC % NX, slot % NC
    y_from = serving_y(owner_pair, pair, c_from)
    holder = ((2 * pair + a_from) * NX + x_from) * NC + c_from
    place = row[y_from * SLOTS + holder]
    rope_slot = ((a_from ^ a) * 2 + (c_from ^ c)) * (NY * NX)
    rope_slot = rope_slot + (y - y_from) % NY * NX + (x - x_from) % NX
    request = place // 128
    length = jnp.where(
        request == 0, row[256] * 128 + row[258], row[257] * 128 + row[259]
    )
    valid = jnp.clip(length - (place % 128) * PAGE, 0, PAGE)
    key = jnp.where(valid > 0, request, 2)
    before = (key[None, :] < key[:, None]) | (
        (key[None, :] == key[:, None]) & (slot[None, :] < slot[:, None])
    )
    rank = jnp.sum(before.astype(jnp.int32), axis=1)
    hit = rank[:, None] == slot[None, :]
    order, rope_order, valid = (
        jnp.sum(jnp.where(hit, v[:, None], 0), axis=0) for v in (slot, rope_slot, valid)
    )
    count = jnp.stack([jnp.sum((key == r).astype(jnp.int32)) for r in range(2)])
    return order, rope_order, valid, count


def pick(array, index, axis):
    return lax.dynamic_index_in_dim(array, index, axis, keepdims=False)


def move_ropes(ropes, pair, a, x, c, y):
    ropes = ropes.reshape(PAIRS, 2, NX, NC, PAGE // 2, 2 * ROPE)
    came = []
    for s in range(NX):
        part = pick(ropes, (x + s) % NX, 2)
        if s:
            pairs = [
                (device_id(z, i, k, 0) // NY, device_id(z, (i + s) % NX, k, 0) // NY)
                for z, i, k, _ in devices()[::NY]
            ]
            part = lax.ppermute(part, "req", pairs)
        came.append(part)
    ropes = jnp.stack(came)
    came = []
    for t in range(NY):
        part = jnp.stack(
            [
                pick(ropes[:, :, :, k], served_pair(pair, (y + t) % NY, k), 1)
                for k in range(NC)
            ]
        )
        if t:
            part = lax.ppermute(part, "head", [(i, (i + t) % NY) for i in range(NY)])
        came.append(part)
    ropes = jnp.stack(came)
    came = []
    for da in range(2):
        for dc in range(2):
            part = pick(pick(ropes, c ^ dc, 1), a ^ da, 2)
            if da or dc:
                pairs = [
                    (device_id(z, i, k, 0) // NY, device_id(z ^ da, i, k ^ dc, 0) // NY)
                    for z, i, k, _ in devices()[::NY]
                ]
                part = lax.ppermute(part, "req", pairs)
            came.append(part)
    return jnp.concatenate(came).reshape(SLOTS, PAGE // 2, 2 * ROPE)


def on_device(
    latent_pages, rope_pages, page_place, lengths, q_latent, q_rope, new_latent, new_rope
):
    here = lax.axis_index("req")
    y = lax.axis_index("head")
    pair, a = here // (2 * NX * NC), here // (NX * NC) % 2
    x, c = here // NC % NX, here % NC
    lat = lax.all_to_all(
        latent_pages, AXES, 0, 0, axis_index_groups=page_groups(), tiled=True
    )
    place = page_place.astype(jnp.bfloat16)
    length = jnp.concatenate([lengths // 128, lengths % 128]).astype(jnp.bfloat16)
    row = jnp.concatenate([place, length, jnp.zeros((512 - 260,), jnp.bfloat16)])
    query_lat = q_latent.reshape(2 * ROWS, 512)
    query_rope = q_rope.reshape(2 * ROWS, ROPE)
    query = jnp.concatenate([query_lat, query_rope.reshape(META, 512)], axis=0)
    first = jnp.concatenate(
        [query, row[None, :], jnp.zeros((META - 1, 512), jnp.bfloat16)], axis=0
    )
    came = [
        lax.ppermute(query if d else first, AXES, [(t, s) for s, t in home_pairs(d)])
        for d in range(4)
    ]
    queries = []
    for part in came:
        part_rope = part[2 * ROWS : 2 * ROWS + META].reshape(2, ROWS, ROPE)
        part_lat = part[: 2 * ROWS].reshape(2, ROWS, 512)
        queries.append(jnp.concatenate([part_lat, part_rope, part_rope], axis=2))
    queries = jnp.concatenate(queries, axis=1)
    table = page_table(came[0][2 * ROWS + META].astype(jnp.int32), pair, a, x, c, y)
    rope = move_ropes(rope_pages, pair, a, x, c, y)
    whole = pl.BlockSpec(memory_space=pltpu.VMEM)
    scalars = pl.BlockSpec(memory_space=pltpu.SMEM)
    partial = jax.ShapeDtypeStruct((2 * ROWS + META, 512), jnp.bfloat16)
    parts = pl.pallas_call(
        attend_kernel,
        out_shape=[partial] * 4,
        in_specs=[scalars] * 4 + [pl.BlockSpec(memory_space=pl.ANY), whole, whole],
        out_specs=[whole] * 4,
        scratch_shapes=[
            pltpu.VMEM((SLOTS, PAGE, 512), jnp.bfloat16),
            pltpu.VMEM((SLOTS // BLOCK, 4 * ROWS, TOKENS), jnp.float32),
            pltpu.VMEM((4 * ROWS, 512), jnp.float32),
            pltpu.SemaphoreType.DMA((SLOTS,)),
        ],
        compiler_params=pltpu.CompilerParams(vmem_limit_bytes=48 * 1024 * 1024),
        cost_estimate=pl.CostEstimate(
            flops=4 * ROWS * 6144 * 1152 * 2, bytes_accessed=8 << 20, transcendentals=1 << 20
        ),
        name="attend",
    )(*table, lat, rope, queries)
    home = [lax.ppermute(part, AXES, home_pairs(d)) for d, part in enumerate(parts)]
    out = pl.pallas_call(
        merge_kernel,
        out_shape=jax.ShapeDtypeStruct((2, ROWS, 512), jnp.bfloat16),
        in_specs=[whole] * 8,
        out_specs=whole,
        name="merge",
    )(*home, query_lat, query_rope, new_latent, new_rope)
    return out.reshape(q_latent.shape)


def solution(mesh):
    return jax.shard_map(
        on_device,
        mesh=mesh,
        in_specs=(
            P(("req", "head"), None, None),
            P(("req", "head"), None),
            P("req"),
            P("req"),
            P("req", None, "head", None),
            P("req", None, "head", None),
            P("req", None, None),
            P("req", None, None),
        ),
        out_specs=P("req", None, "head", None),
        check_vma=False,
    )
```

time: 179 us -> 170 us (0.950)
  the two profiles are of different devices: /device:TPU:72 before, /device:TPU:1 now
where the time goes in v2:
time: 170 us; the launch traced here: 168 us
  waiting for transfers between devices  97.3 us (57%)
  starting transfers between devices  50.2 us (30%)
  Pallas kernels  11.5 us (7%)
  between operations  3.23 us (2%)
  local copies, waits for them, and re-layouts  3.19 us (2%)
  other arithmetic  2.93 us (2%)
    ppermute x4, waiting for transfers between devices, on_device(): lax.ppermute(query if d else first, AXES, [(t, s) for s, t in home_pairs(...  71.8 us
    ppermute x4, starting transfers between devices, on_device(): lax.ppermute(part, AXES, home_pairs(d))  12.2 us
    ppermute x3, starting transfers between devices, move_ropes(): part = lax.ppermute(part, 'head', [(i, (i + t) % NY) for i in range(NY)])  11.8 us
    all_to_all x1, starting transfers between devices, on_device(): lax.all_to_all(latent_pages, AXES, 0, 0, axis_index_groups=page_groups(),...  10.7 us
    ppermute x4, waiting for transfers between devices, on_device(): lax.ppermute(part, AXES, home_pairs(d))  10.5 us
    ppermute x4, starting transfers between devices, on_device(): lax.ppermute(query if d else first, AXES, [(t, s) for s, t in home_pairs(...  9.4 us
    pallas_call x1, Pallas kernels, on_device(): pl.pallas_call(attend_kernel, out_shape=[partial] * 4, in_specs=[scalars]...  9.13 us
    ppermute x6, waiting for transfers between devices, move_ropes(): part = lax.ppermute(part, 'req', pairs)  8.98 us
  transfers between devices with their start and end apart: 18, of which 10 were waited for; matrix products, arithmetic and copies ran while one was open for 3% of the time, Pallas kernels for 0%

profile of v2, /device:TPU:1, one launch (start us, length us, event | category | flops | bytes accessed | tf_op | source)
XLA Modules:
  0.0 168.3 jit_solution(2639088027590103157)
XLA Ops:
  0.0 10.7 %all-to-all-start = ((bf16[64,96,512]{2,1,0:T(8,128)(2,1)}), bf16[64,96,512]{2,1,0:T(8,128)(2,1)}, u32[]{:S(2)}, u32[]{:S(2)}) async-start(bf16[64,96,512]{2,1,0:T(8,128)(2,1)} %param.8), calls=%async_computation | async-start | bytes 12582912 | tf_op jit(solution)/shard_map/all_to_all | solution.py:291
  10.8 5.5 %collective-permute-start.10 = (bf16[144,512]{1,0:T(8,128)(2,1)S(1)}, bf16[144,512]{1,0:T(8,128)(2,1)S(1)}, u32[]{:S(2)}, u32[]{:S(2)}) collective-permute-start(bf16[144,512]{1,0:T(8,128)(2,1)S(1)} %pad_maximum_fusion.6), channel_id=1, source_target_pairs={{1,0},{66,1},{131,2},{192,3},{5,4},{198,5},{135,6},{68,7},{9,8},{7... | collective-permute-start | bytes 442376 | tf_op jit(solution)/shard_map/ppermute | solution.py:304
  16.3 2.6 %collective-permute-start.11 = (bf16[144,512]{1,0:T(8,128)(2,1)S(1)}, bf16[144,512]{1,0:T(8,128)(2,1)S(1)}, u32[]{:S(2)}, u32[]{:S(2)}) collective-permute-start(bf16[144,512]{1,0:T(8,128)(2,1)S(1)} %pad_maximum_fusion.6), channel_id=1, source_target_pairs={{2,0},{67,1},{128,2},{193,3},{6,4},{199,5},{132,6},{69,7},{10,8},{... | collective-permute-start | bytes 442376 | tf_op jit(solution)/shard_map/ppermute | solution.py:304
  19.8 2.8 %collective-permute-start.2 = (bf16[4,2,2,48,128]{4,3,2,1,0:T(8,128)(2,1)S(1)}, bf16[4,2,2,48,128]{4,3,2,1,0:T(8,128)(2,1)S(1)}, u32[]{:S(2)}, u32[]{:S(2)}) collective-permute-start(bf16[4,2,2,48,128]{4,3,2,1,0:T(8,128)(2,1)S(1)} %get-tuple-element.28), channel_id=1, source_target_pairs={{0,16},{4,20},{8,24},{12,28},{16,0},{20,4},{24,8},{28,12},{32,48},... | collective-permute-start | bytes 589832 | tf_op jit(solution)/shard_map/ppermute | solution.py:255
  23.9 68.7 %collective-permute-done.10 = bf16[144,512]{1,0:T(8,128)(2,1)S(1)} collective-permute-done((bf16[144,512]{1,0:T(8,128)(2,1)S(1)}, bf16[144,512]{1,0:T(8,128)(2,1)S(1)}, u32[]{:S(2)}, u32[]{:S(2)}) %collective-permute-start.10) | collective-permute-done | bytes 147488 | tf_op jit(solution)/shard_map/ppermute | solution.py:304
  92.7 3.1 %collective-permute-done.11 = bf16[144,512]{1,0:T(8,128)(2,1)S(1)} collective-permute-done((bf16[144,512]{1,0:T(8,128)(2,1)S(1)}, bf16[144,512]{1,0:T(8,128)(2,1)S(1)}, u32[]{:S(2)}, u32[]{:S(2)}) %collective-permute-start.11) | collective-permute-done | bytes 147488 | tf_op jit(solution)/shard_map/ppermute | solution.py:304
  100.9 1.4 collective-permute-done.1
  102.6 5.6 %collective-permute-start.4 = (bf16[2,4,2,48,128]{4,3,1,2,0:T(8,128)(2,1)S(1)}, bf16[2,4,2,48,128]{4,3,1,2,0:T(8,128)(2,1)S(1)}, u32[]{:S(2)}, u32[]{:S(2)}) collective-permute-start(bf16[2,4,2,48,128]{4,3,1,2,0:T(8,128)(2,1)S(1)} %pad_maximum_fusion.3), channel_id=1, source_target_pairs={{0,1},{1,2},{2,3},{3,0},{4,5},{5,6},{6,7},{7,4},{8,9},{9,10},{10,1... | collective-permute-start | bytes 589832 | tf_op jit(solution)/shard_map/ppermute | solution.py:267
  108.2 4.1 %collective-permute-start.5 = (bf16[2,4,2,48,128]{4,3,1,2,0:T(8,128)(2,1)S(1)}, bf16[2,4,2,48,128]{4,3,1,2,0:T(8,128)(2,1)S(1)}, u32[]{:S(2)}, u32[]{:S(2)}) collective-permute-start(bf16[2,4,2,48,128]{4,3,1,2,0:T(8,128)(2,1)S(1)} %pad_maximum_fusion.4), channel_id=1, source_target_pairs={{0,2},{1,3},{2,0},{3,1},{4,6},{5,7},{6,4},{7,5},{8,10},{9,11},{10,... | collective-permute-start | bytes 589832 | tf_op jit(solution)/shard_map/ppermute | solution.py:267
  112.4 2.1 %collective-permute-start.6 = (bf16[2,4,2,48,128]{4,3,1,2,0:T(8,128)(2,1)S(1)}, bf16[2,4,2,48,128]{4,3,1,2,0:T(8,128)(2,1)S(1)}, u32[]{:S(2)}, u32[]{:S(2)}) collective-permute-start(bf16[2,4,2,48,128]{4,3,1,2,0:T(8,128)(2,1)S(1)} %pad_maximum_fusion.5), channel_id=1, source_target_pairs={{0,3},{1,0},{2,1},{3,2},{4,7},{5,4},{6,5},{7,6},{8,11},{9,8},{10,9... | collective-permute-start | bytes 589832 | tf_op jit(solution)/shard_map/ppermute | solution.py:267
  114.7 3.9 %collective-permute-done.5 = bf16[2,4,2,48,128]{4,3,1,2,0:T(8,128)(2,1)S(1)} collective-permute-done((bf16[2,4,2,48,128]{4,3,1,2,0:T(8,128)(2,1)S(1)}, bf16[2,4,2,48,128]{4,3,1,2,0:T(8,128)(2,1)S(1)}, u32[]{:S(2)}, u32[]{:S(2)}) %collective-permute-start.5) | collective-permute-done | bytes 196640 | tf_op jit(solution)/shard_map/ppermute | solution.py:267
  118.6 2.1 %collective-permute-done.6 = bf16[2,4,2,48,128]{4,3,1,2,0:T(8,128)(2,1)S(1)} collective-permute-done((bf16[2,4,2,48,128]{4,3,1,2,0:T(8,128)(2,1)S(1)}, bf16[2,4,2,48,128]{4,3,1,2,0:T(8,128)(2,1)S(1)}, u32[]{:S(2)}, u32[]{:S(2)}) %collective-permute-start.6) | collective-permute-done | bytes 196640 | tf_op jit(solution)/shard_map/ppermute | solution.py:267
  120.9 1.6 collective-permute-start.7
  122.5 1.7 %collective-permute-start.9 = (bf16[4,4,48,128]{3,2,1,0:T(8,128)(2,1)S(1)}, bf16[4,4,48,128]{3,2,1,0:T(8,128)(2,1)S(1)}, u32[]{:S(2)}, u32[]{:S(2)}) collective-permute-start(bf16[4,4,48,128]{3,2,1,0:T(8,128)(2,1)S(1)} %get-tuple-element.21), channel_id=1, source_target_pairs={{0,36},{4,32},{8,44},{12,40},{16,52},{20,48},{24,60},{28,56},{32,4... | collective-permute-start | bytes 589832 | tf_op jit(solution)/shard_map/ppermute | solution.py:279
  124.3 1.2 pad_add_fusion.count_ref
  125.8 3.2 %collective-permute-done.8 = bf16[4,4,48,128]{3,2,1,0:T(8,128)(2,1)S(1)} collective-permute-done((bf16[4,4,48,128]{3,2,1,0:T(8,128)(2,1)S(1)}, bf16[4,4,48,128]{3,2,1,0:T(8,128)(2,1)S(1)}, u32[]{:S(2)}, u32[]{:S(2)}) %collective-permute-start.8) | collective-permute-done | bytes 196640 | tf_op jit(solution)/shard_map/ppermute | solution.py:279
  129.0 4.4 %collective-permute-done.9 = bf16[4,4,48,128]{3,2,1,0:T(8,128)(2,1)S(1)} collective-permute-done((bf16[4,4,48,128]{3,2,1,0:T(8,128)(2,1)S(1)}, bf16[4,4,48,128]{3,2,1,0:T(8,128)(2,1)S(1)}, u32[]{:S(2)}, u32[]{:S(2)}) %collective-permute-start.9) | collective-permute-done | bytes 196640 | tf_op jit(solution)/shard_map/ppermute | solution.py:279
  133.5 9.1 %attend.1 = (bf16[144,512]{1,0:T(8,128)(2,1)S(1)}, bf16[144,512]{1,0:T(8,128)(2,1)S(1)}, bf16[144,512]{1,0:T(8,128)(2,1)S(1)}, bf16[144,512]{1,0:T(8,128)(2,1)S(1)}) custom-call(s32[64]{0:T(128)S(1)} %get-tuple-element.17.order_ref, s32[64]{0:T(128)S(1)} %get-tuple-element.16.rope_order_ref, s32[64]{0:T(128)S(1)} %get-tuple-element.15.valid_ref, ...), custom_call_target="tpu_custom_call" | custom-call | flops 3623878656 | bytes 8388608 | tf_op jit(solution)/shard_map/attend/pallas_call | solution.py:318
  143.3 6.0 %collective-permute-start.14 = (bf16[144,512]{1,0:T(8,128)(2,1)S(1)}, bf16[144,512]{1,0:T(8,128)(2,1)S(1)}, u32[]{:S(2)}, u32[]{:S(2)}) collective-permute-start(bf16[144,512]{1,0:T(8,128)(2,1)S(1)} %get-tuple-element.10), channel_id=1, source_target_pairs={{0,1},{1,66},{2,131},{3,192},{4,5},{5,198},{6,135},{7,68},{8,9},{9... | collective-permute-start | bytes 442376 | tf_op jit(solution)/shard_map/ppermute | solution.py:335
  149.3 4.5 %collective-permute-start.15 = (bf16[144,512]{1,0:T(8,128)(2,1)S(1)}, bf16[144,512]{1,0:T(8,128)(2,1)S(1)}, u32[]{:S(2)}, u32[]{:S(2)}) collective-permute-start(bf16[144,512]{1,0:T(8,128)(2,1)S(1)} %get-tuple-element.11), channel_id=1, source_target_pairs={{0,2},{1,67},{2,128},{3,193},{4,6},{5,199},{6,132},{7,69},{8,10},{... | collective-permute-start | bytes 442376 | tf_op jit(solution)/shard_map/ppermute | solution.py:335
  153.8 1.1 collective-permute-start.16
  154.8 7.8 %collective-permute-done.14.p1 = bf16[144,512]{1,0:T(8,128)(2,1)S(1)} collective-permute-done((bf16[144,512]{1,0:T(8,128)(2,1)S(1)}, bf16[144,512]{1,0:T(8,128)(2,1)S(1)}, u32[]{:S(2)}, u32[]{:S(2)}) %collective-permute-start.14) | collective-permute-done | bytes 147488 | tf_op jit(solution)/shard_map/ppermute | solution.py:335
  163.1 2.2 %collective-permute-done.16.p3 = bf16[144,512]{1,0:T(8,128)(2,1)S(1)} collective-permute-done((bf16[144,512]{1,0:T(8,128)(2,1)S(1)}, bf16[144,512]{1,0:T(8,128)(2,1)S(1)}, u32[]{:S(2)}, u32[]{:S(2)}) %collective-permute-start.16) | collective-permute-done | bytes 147488 | tf_op jit(solution)/shard_map/ppermute | solution.py:335
  166.0 2.3 %merge.1 = bf16[2,64,512]{2,1,0:T(8,128)(2,1)} custom-call(bf16[144,512]{1,0:T(8,128)(2,1)} %copy-done.5, bf16[144,512]{1,0:T(8,128)(2,1)} %copy-done.6, bf16[144,512]{1,0:T(8,128)(2,1)} %copy-done.7, bf16[144,512]{1,0:T(8,128)(2,1)} %copy-done.8, bf16[128,512]{1,0:T(8,128)(2,1)} %bitcast.71, bf16[128,64]{1,0:T(8,128)(2,1)} %bitcast.93, ...), custom_call_target="tpu_custom_call" | custom-call | tf_op jit(solution)/shard_map/merge/pallas_call | solution.py:336
  (93 shorter events, 7.3 us)
Async XLA Ops:
  0.0 10.7 %copy-start.9 = (bf16[2,2,32,64]{3,2,1,0:T(8,128)(2,1)S(1)}, bf16[2,2,32,64]{3,2,1,0:T(8,128)(2,1)}, u32[]{:S(2)}) copy-start(bf16[2,2,32,64]{3,2,1,0:T(8,128)(2,1)} %param.13) | copy-start | bytes 49156
  0.0 10.8 %copy-start = (bf16[2,2,32,512]{3,2,1,0:T(8,128)(2,1)S(1)}, bf16[2,2,32,512]{3,2,1,0:T(8,128)(2,1)}, u32[]{:S(2)}) copy-start(bf16[2,2,32,512]{3,2,1,0:T(8,128)(2,1)} %param.12) | copy-start | bytes 393220
  0.0 19.5 %copy-start.1 = (bf16[64,6144]{1,0:T(8,128)(2,1)S(1)}, bf16[64,6144]{1,0:T(8,128)(2,1)}, u32[]{:S(2)}) copy-start(bf16[64,6144]{1,0:T(8,128)(2,1)} %param.9) | copy-start | bytes 2359300
  0.0 133.5 %all-to-all-start = ((bf16[64,96,512]{2,1,0:T(8,128)(2,1)}), bf16[64,96,512]{2,1,0:T(8,128)(2,1)}, u32[]{:S(2)}, u32[]{:S(2)}) async-start(bf16[64,96,512]{2,1,0:T(8,128)(2,1)} %param.8), calls=%async_computation | async-start | bytes 12582912 | tf_op jit(solution)/shard_map/all_to_all | solution.py:291
  10.8 81.8 %collective-permute-start.10 = (bf16[144,512]{1,0:T(8,128)(2,1)S(1)}, bf16[144,512]{1,0:T(8,128)(2,1)S(1)}, u32[]{:S(2)}, u32[]{:S(2)}) collective-permute-start(bf16[144,512]{1,0:T(8,128)(2,1)S(1)} %pad_maximum_fusion.6), channel_id=1, source_target_pairs={{1,0},{66,1},{131,2},{192,3},{5,4},{198,5},{135,6},{68,7},{9,8},{7... | collective-permute-start | bytes 442376 | tf_op jit(solution)/shard_map/ppermute | solution.py:304
  16.3 79.5 %collective-permute-start.11 = (bf16[144,512]{1,0:T(8,128)(2,1)S(1)}, bf16[144,512]{1,0:T(8,128)(2,1)S(1)}, u32[]{:S(2)}, u32[]{:S(2)}) collective-permute-start(bf16[144,512]{1,0:T(8,128)(2,1)S(1)} %pad_maximum_fusion.6), channel_id=1, source_target_pairs={{2,0},{67,1},{128,2},{193,3},{6,4},{199,5},{132,6},{69,7},{10,8},{... | collective-permute-start | bytes 442376 | tf_op jit(solution)/shard_map/ppermute | solution.py:304
  18.9 77.0 %collective-permute-start.12 = (bf16[144,512]{1,0:T(8,128)(2,1)S(1)}, bf16[144,512]{1,0:T(8,128)(2,1)S(1)}, u32[]{:S(2)}, u32[]{:S(2)}) collective-permute-start(bf16[144,512]{1,0:T(8,128)(2,1)S(1)} %pad_maximum_fusion.6), channel_id=1, source_target_pairs={{3,0},{64,1},{129,2},{194,3},{7,4},{196,5},{133,6},{70,7},{11,8},{... | collective-permute-start | bytes 442376 | tf_op jit(solution)/shard_map/ppermute | solution.py:304
  19.8 81.1 %collective-permute-start.2 = (bf16[4,2,2,48,128]{4,3,2,1,0:T(8,128)(2,1)S(1)}, bf16[4,2,2,48,128]{4,3,2,1,0:T(8,128)(2,1)S(1)}, u32[]{:S(2)}, u32[]{:S(2)}) collective-permute-start(bf16[4,2,2,48,128]{4,3,2,1,0:T(8,128)(2,1)S(1)} %get-tuple-element.28), channel_id=1, source_target_pairs={{0,16},{4,20},{8,24},{12,28},{16,0},{20,4},{24,8},{28,12},{32,48},... | collective-permute-start | bytes 589832 | tf_op jit(solution)/shard_map/ppermute | solution.py:255
  22.9 73.1 %collective-permute-start = (bf16[160,512]{1,0:T(8,128)(2,1)S(1)}, bf16[160,512]{1,0:T(8,128)(2,1)S(1)}, u32[]{:S(2)}, u32[]{:S(2)}) collective-permute-start(bf16[160,512]{1,0:T(8,128)(2,1)S(1)} %maximum_maximum_fusion.1), channel_id=1, source_target_pairs={{0,0},{65,1},{130,2},{195,3},{4,4},{197,5},{134,6},{71,7},{8,8},{7... | collective-permute-start | bytes 491528 | tf_op jit(solution)/shard_map/ppermute | solution.py:304
  92.6 9.7 %copy-start.2 = (bf16[144,512]{1,0:T(8,128)(2,1)}, bf16[144,512]{1,0:T(8,128)(2,1)S(1)}, u32[]{:S(2)}) copy-start(bf16[144,512]{1,0:T(8,128)(2,1)S(1)} %collective-permute-done.10) | copy-start | bytes 442372
  92.6 8.2 %collective-permute-start.3 = (bf16[4,2,2,48,128]{4,3,2,1,0:T(8,128)(2,1)S(1)}, bf16[4,2,2,48,128]{4,3,2,1,0:T(8,128)(2,1)S(1)}, u32[]{:S(2)}, u32[]{:S(2)}) collective-permute-start(bf16[4,2,2,48,128]{4,3,2,1,0:T(8,128)(2,1)S(1)} %get-tuple-element.27), channel_id=1, source_target_pairs={{0,24},{4,28},{8,0},{12,4},{16,8},{20,12},{24,16},{28,20},{32,56},... | collective-permute-start | bytes 589832 | tf_op jit(solution)/shard_map/ppermute | solution.py:255
  95.8 6.5 %copy-start.3 = (bf16[144,512]{1,0:T(8,128)(2,1)}, bf16[144,512]{1,0:T(8,128)(2,1)S(1)}, u32[]{:S(2)}) copy-start(bf16[144,512]{1,0:T(8,128)(2,1)S(1)} %collective-permute-done.11) | copy-start | bytes 442372
  95.8 6.4 %collective-permute-start.1 = (bf16[4,2,2,48,128]{4,3,2,1,0:T(8,128)(2,1)S(1)}, bf16[4,2,2,48,128]{4,3,2,1,0:T(8,128)(2,1)S(1)}, u32[]{:S(2)}, u32[]{:S(2)}) collective-permute-start(bf16[4,2,2,48,128]{4,3,2,1,0:T(8,128)(2,1)S(1)} %get-tuple-element.29), channel_id=1, source_target_pairs={{0,8},{4,12},{8,16},{12,20},{16,24},{20,28},{24,0},{28,4},{32,40},... | collective-permute-start | bytes 589832 | tf_op jit(solution)/shard_map/ppermute | solution.py:255
  102.6 12.1 %collective-permute-start.4 = (bf16[2,4,2,48,128]{4,3,1,2,0:T(8,128)(2,1)S(1)}, bf16[2,4,2,48,128]{4,3,1,2,0:T(8,128)(2,1)S(1)}, u32[]{:S(2)}, u32[]{:S(2)}) collective-permute-start(bf16[2,4,2,48,128]{4,3,1,2,0:T(8,128)(2,1)S(1)} %pad_maximum_fusion.3), channel_id=1, source_target_pairs={{0,1},{1,2},{2,3},{3,0},{4,5},{5,6},{6,7},{7,4},{8,9},{9,10},{10,1... | collective-permute-start | bytes 589832 | tf_op jit(solution)/shard_map/ppermute | solution.py:267
  108.2 10.4 %collective-permute-start.5 = (bf16[2,4,2,48,128]{4,3,1,2,0:T(8,128)(2,1)S(1)}, bf16[2,4,2,48,128]{4,3,1,2,0:T(8,128)(2,1)S(1)}, u32[]{:S(2)}, u32[]{:S(2)}) collective-permute-start(bf16[2,4,2,48,128]{4,3,1,2,0:T(8,128)(2,1)S(1)} %pad_maximum_fusion.4), channel_id=1, source_target_pairs={{0,2},{1,3},{2,0},{3,1},{4,6},{5,7},{6,4},{7,5},{8,10},{9,11},{10,... | collective-permute-start | bytes 589832 | tf_op jit(solution)/shard_map/ppermute | solution.py:267
  112.4 8.3 %collective-permute-start.6 = (bf16[2,4,2,48,128]{4,3,1,2,0:T(8,128)(2,1)S(1)}, bf16[2,4,2,48,128]{4,3,1,2,0:T(8,128)(2,1)S(1)}, u32[]{:S(2)}, u32[]{:S(2)}) collective-permute-start(bf16[2,4,2,48,128]{4,3,1,2,0:T(8,128)(2,1)S(1)} %pad_maximum_fusion.5), channel_id=1, source_target_pairs={{0,3},{1,0},{2,1},{3,2},{4,7},{5,4},{6,5},{7,6},{8,11},{9,8},{10,9... | collective-permute-start | bytes 589832 | tf_op jit(solution)/shard_map/ppermute | solution.py:267
  120.9 4.8 %collective-permute-start.7 = (bf16[4,4,48,128]{3,2,1,0:T(8,128)(2,1)S(1)}, bf16[4,4,48,128]{3,2,1,0:T(8,128)(2,1)S(1)}, u32[]{:S(2)}, u32[]{:S(2)}) collective-permute-start(bf16[4,4,48,128]{3,2,1,0:T(8,128)(2,1)S(1)} %get-tuple-element.23), channel_id=1, source_target_pairs={{0,4},{4,0},{8,12},{12,8},{16,20},{20,16},{24,28},{28,24},{32,36},... | collective-permute-start | bytes 589832 | tf_op jit(solution)/shard_map/ppermute | solution.py:279
  122.5 6.5 %collective-permute-start.8 = (bf16[4,4,48,128]{3,2,1,0:T(8,128)(2,1)S(1)}, bf16[4,4,48,128]{3,2,1,0:T(8,128)(2,1)S(1)}, u32[]{:S(2)}, u32[]{:S(2)}) collective-permute-start(bf16[4,4,48,128]{3,2,1,0:T(8,128)(2,1)S(1)} %get-tuple-element.22), channel_id=1, source_target_pairs={{0,32},{4,36},{8,40},{12,44},{16,48},{20,52},{24,56},{28,60},{32,0... | collective-permute-start | bytes 589832 | tf_op jit(solution)/shard_map/ppermute | solution.py:279
  122.5 10.9 %collective-permute-start.9 = (bf16[4,4,48,128]{3,2,1,0:T(8,128)(2,1)S(1)}, bf16[4,4,48,128]{3,2,1,0:T(8,128)(2,1)S(1)}, u32[]{:S(2)}, u32[]{:S(2)}) collective-permute-start(bf16[4,4,48,128]{3,2,1,0:T(8,128)(2,1)S(1)} %get-tuple-element.21), channel_id=1, source_target_pairs={{0,36},{4,32},{8,44},{12,40},{16,52},{20,48},{24,60},{28,56},{32,4... | collective-permute-start | bytes 589832 | tf_op jit(solution)/shard_map/ppermute | solution.py:279
  142.7 12.2 %collective-permute-start.13 = (bf16[144,512]{1,0:T(8,128)(2,1)S(1)}, bf16[144,512]{1,0:T(8,128)(2,1)S(1)}, u32[]{:S(2)}, u32[]{:S(2)}) collective-permute-start(bf16[144,512]{1,0:T(8,128)(2,1)S(1)} %get-tuple-element.9), channel_id=1, source_target_pairs={{0,0},{1,65},{2,130},{3,195},{4,4},{5,197},{6,134},{7,71},{8,8},{9... | collective-permute-start | bytes 442376 | tf_op jit(solution)/shard_map/ppermute | solution.py:335
  143.3 19.4 %collective-permute-start.14 = (bf16[144,512]{1,0:T(8,128)(2,1)S(1)}, bf16[144,512]{1,0:T(8,128)(2,1)S(1)}, u32[]{:S(2)}, u32[]{:S(2)}) collective-permute-start(bf16[144,512]{1,0:T(8,128)(2,1)S(1)} %get-tuple-element.10), channel_id=1, source_target_pairs={{0,1},{1,66},{2,131},{3,192},{4,5},{5,198},{6,135},{7,68},{8,9},{9... | collective-permute-start | bytes 442376 | tf_op jit(solution)/shard_map/ppermute | solution.py:335
  149.3 13.8 %collective-permute-start.15 = (bf16[144,512]{1,0:T(8,128)(2,1)S(1)}, bf16[144,512]{1,0:T(8,128)(2,1)S(1)}, u32[]{:S(2)}, u32[]{:S(2)}) collective-permute-start(bf16[144,512]{1,0:T(8,128)(2,1)S(1)} %get-tuple-element.11), channel_id=1, source_target_pairs={{0,2},{1,67},{2,128},{3,193},{4,6},{5,199},{6,132},{7,69},{8,10},{... | collective-permute-start | bytes 442376 | tf_op jit(solution)/shard_map/ppermute | solution.py:335
  153.8 11.5 %collective-permute-start.16 = (bf16[144,512]{1,0:T(8,128)(2,1)S(1)}, bf16[144,512]{1,0:T(8,128)(2,1)S(1)}, u32[]{:S(2)}, u32[]{:S(2)}) collective-permute-start(bf16[144,512]{1,0:T(8,128)(2,1)S(1)} %get-tuple-element.12), channel_id=1, source_target_pairs={{0,3},{1,64},{2,129},{3,194},{4,7},{5,196},{6,133},{7,70},{8,11},{... | collective-permute-start | bytes 442376 | tf_op jit(solution)/shard_map/ppermute | solution.py:335
  154.8 10.5 %copy-start.5 = (bf16[144,512]{1,0:T(8,128)(2,1)}, bf16[144,512]{1,0:T(8,128)(2,1)S(1)}, u32[]{:S(2)}) copy-start(bf16[144,512]{1,0:T(8,128)(2,1)S(1)} %collective-permute-done.13.p0) | copy-start | bytes 442372
  (9 other events, 32.4 us)

commit v3 on v2

v3 whole, which is shorter than its diff:
```python
import functools
import math

import jax
import jax.numpy as jnp
from jax import lax
from jax.experimental import pallas as pl
from jax.experimental.pallas import tpu as pltpu
from jax.sharding import PartitionSpec as P

ROPE = 64
NOPE = 128
SCALE = float(NOPE + ROPE) ** -0.5 * math.log2(math.e)
NEG = -1e30

NZ, NX, NC, NY = 8, 4, 2, 4
AXES = ("req", "head")
PAIRS = NZ // 2
SLOTS = NZ * NX * NC
PAGE = 96
BLOCK = 8
TOKENS = BLOCK * PAGE
ROWS = 64
META = 16


def device_id(z, x, core, y):
    return ((z * NX + x) * NC + core) * NY + y


def served_pair(pair, y, core):
    return (pair + (1 - 2 * core) * (y + 2 * (pair % 2))) % PAIRS


def serving_y(owner_pair, pair, core):
    return ((1 - 2 * core) * (owner_pair - pair) - 2 * (pair % 2)) % NY


def page_groups():
    return [
        [
            device_id(2 * j + zo % 2, x, c, serving_y(zo // 2, j, c))
            for zo in range(NZ)
            for x in range(NX)
            for c in range(NC)
        ]
        for j in range(PAIRS)
    ]


def home_pairs(d):
    return [
        (
            device_id(z, x, c, y),
            device_id(2 * served_pair(z // 2, y, c) + z % 2, x, c, (y + d) % NY),
        )
        for z in range(NZ)
        for x in range(NX)
        for c in range(NC)
        for y in range(NY)
    ]


def contract(left, right):
    return lax.dot_general(
        left, right, (((1,), (1,)), ((), ())), preferred_element_type=jnp.float32
    )


def spread_kernel(rope_ref, out_ref):
    pages = 4
    token = lax.broadcasted_iota(jnp.int32, (pages * PAGE, pages * PAGE // 2), 0)
    pair = lax.broadcasted_iota(jnp.int32, (pages * PAGE, pages * PAGE // 2), 1)
    spread = (token // 2 == pair).astype(jnp.bfloat16)
    half = (
        lax.broadcasted_iota(jnp.int32, (pages * PAGE, 2 * ROPE), 0) % 2
        == lax.broadcasted_iota(jnp.int32, (pages * PAGE, 2 * ROPE), 1) // ROPE
    )

    def step(i, carry):
        pairs = jnp.concatenate([rope_ref[i * pages + k] for k in range(pages)], axis=0)
        keys = jnp.dot(spread, pairs, preferred_element_type=jnp.float32)
        keys = jnp.where(half, keys, 0.0).astype(jnp.bfloat16)
        for k in range(pages):
            out_ref[i * pages + k] = keys[k * PAGE : (k + 1) * PAGE, :]
        return carry

    lax.fori_loop(0, SLOTS // pages, step, 0)


def attend_kernel(
    order_ref, valid_ref, count_ref, lat_ref, keys_ref, query_ref,
    o0, o1, o2, o3, page_ref, score_ref, acc_ref, sems
):
    outs = (o0, o1, o2, o3)

    def copy(place):
        return pltpu.make_async_copy(
            lat_ref.at[order_ref[place]], page_ref.at[place], sems.at[place]
        )

    def begin(place, carry):
        copy(place).start()
        return carry

    lax.fori_loop(0, count_ref[0] + count_ref[1], begin, 0)
    lane = lax.broadcasted_iota(jnp.int32, (1, TOKENS), 1)
    meta_lane = lax.broadcasted_iota(jnp.int32, (4 * ROWS, 128), 1)
    meta = jnp.zeros((4 * ROWS, 128), jnp.float32)
    for request in range(2):
        rows = slice(request * ROWS, (request + 1) * ROWS)
        start = count_ref[0] * request
        count = count_ref[request]
        blocks = (count + BLOCK - 1) // BLOCK

        def place_of(block, index):
            return start + jnp.minimum(block * BLOCK + index, count - 1)

        def latents(block):
            return jnp.concatenate([page_ref[place_of(block, i)] for i in range(BLOCK)], axis=0)

        def score_block(block, maxima):
            for i in range(BLOCK):

                @pl.when(block * BLOCK + i < count)
                def _():
                    copy(start + block * BLOCK + i).wait()

            rope_keys = jnp.concatenate(
                [keys_ref[order_ref[place_of(block, i)]] for i in range(BLOCK)], axis=0
            )
            keys = jnp.concatenate([latents(block), rope_keys], axis=1)
            limit = jnp.zeros((1, TOKENS), jnp.int32)
            for i in range(BLOCK):
                valid = jnp.where(block * BLOCK + i < count, valid_ref[place_of(block, i)], 0)
                limit = jnp.where(lane >= i * PAGE, i * PAGE + valid, limit)
            score = contract(query_ref[request], keys) * SCALE + jnp.where(lane < limit, 0.0, NEG)
            score_ref[block] = score
            for i in range(TOKENS // 128):
                maxima = jnp.maximum(maxima, score[:, i * 128 : (i + 1) * 128])
            return maxima

        maxima = lax.fori_loop(
            0, blocks, score_block, jnp.full((4 * ROWS, 128), NEG, jnp.float32)
        )
        top = jnp.max(maxima, axis=1, keepdims=True)
        acc_ref[...] = jnp.zeros_like(acc_ref)

        def weigh_block(block, total):
            weight = jnp.exp2(score_ref[block] - top)
            for i in range(TOKENS // 128):
                total = total + weight[:, i * 128 : (i + 1) * 128]
            acc_ref[...] += jnp.dot(
                weight.astype(jnp.bfloat16), latents(block), preferred_element_type=jnp.float32
            )
            return total

        total = lax.fori_loop(
            0, blocks, weigh_block, jnp.zeros((4 * ROWS, 128), jnp.float32)
        )
        total = jnp.sum(total, axis=1, keepdims=True)
        total = jnp.where(total > 0.0, total, 1.0)
        result = (acc_ref[...] / total).astype(jnp.bfloat16)
        for i, out in enumerate(outs):
            out[rows, :] = result[i * ROWS : (i + 1) * ROWS, :]
        rest = top + jnp.log2(total)
        for part in range(3):
            piece = rest.astype(jnp.bfloat16).astype(jnp.float32)
            meta = jnp.where(meta_lane == request * 3 + part, piece, meta)
            rest = rest - piece
    meta = meta.astype(jnp.bfloat16)
    for i, out in enumerate(outs):
        part = meta[i * ROWS : (i + 1) * ROWS, :]
        out[2 * ROWS :, :] = jnp.concatenate(
            [part[k * META : (k + 1) * META, :] for k in range(4)], axis=1
        )


def merge_kernel(p0, p1, p2, p3, fresh_ref, new_lat_ref, out_ref):
    parts = (p0, p1, p2, p3)
    meta = [
        jnp.concatenate(
            [p[2 * ROWS :, k * 128 : (k + 1) * 128] for k in range(4)], axis=0
        ).astype(jnp.float32)
        for p in parts
    ]
    for request in range(2):
        rows = slice(request * ROWS, (request + 1) * ROWS)
        sums = [
            m[:, 3 * request : 3 * request + 1]
            + m[:, 3 * request + 1 : 3 * request + 2]
            + m[:, 3 * request + 2 : 3 * request + 3]
            for m in meta
        ]
        fresh = [fresh_ref[request, :, step : step + 1] for step in range(2)]
        top = functools.reduce(jnp.maximum, sums + fresh)
        total = jnp.zeros((ROWS, 1), jnp.float32)
        acc = jnp.zeros((ROWS, 512), jnp.float32)
        for part, score in zip(parts, sums):
            weight = jnp.exp2(score - top)
            total = total + weight
            acc = acc + weight * part[rows, :].astype(jnp.float32)
        for step, score in enumerate(fresh):
            weight = jnp.exp2(score - top)
            total = total + weight
            key = new_lat_ref[request, step : step + 1, :].astype(jnp.float32)
            acc = acc + weight.astype(jnp.bfloat16).astype(jnp.float32) * key
        out_ref[request] = (acc / total).astype(jnp.bfloat16)


def fresh_scores(q_latent, q_rope, new_latent, new_rope):
    dims = (((3,), (2,)), ((0,), (0,)))
    score = lax.dot_general(q_latent, new_latent, dims, preferred_element_type=jnp.float32)
    score = score + lax.dot_general(q_rope, new_rope, dims, preferred_element_type=jnp.float32)
    step = jnp.arange(2, dtype=jnp.int32)
    seen = step[None, None, None, :] <= step[None, :, None, None]
    return jnp.where(seen, score * SCALE, NEG).reshape(2, ROWS, 2)


def page_table(row, pair):
    slot = jnp.arange(SLOTS, dtype=jnp.int32)
    owner_pair, a_from = slot // (2 * NX * NC), slot // (NX * NC) % 2
    x_from, c_from = slot // NC % NX, slot % NC
    y_from = serving_y(owner_pair, pair, c_from)
    holder = device_id(2 * pair + a_from, x_from, c_from, 0) // NY
    place = row[y_from * SLOTS + holder]
    request = place // 128
    length = jnp.where(
        request == 0, row[256] * 128 + row[258], row[257] * 128 + row[259]
    )
    valid = jnp.clip(length - (place % 128) * PAGE, 0, PAGE)
    key = jnp.where(valid > 0, request, 2)
    before = (key[None, :] < key[:, None]) | (
        (key[None, :] == key[:, None]) & (slot[None, :] < slot[:, None])
    )
    rank = jnp.sum(before.astype(jnp.int32), axis=1)
    hit = rank[:, None] == slot[None, :]
    order, valid = (jnp.sum(jnp.where(hit, v[:, None], 0), axis=0) for v in (slot, valid))
    count = jnp.stack([jnp.sum((key == r).astype(jnp.int32)) for r in range(2)])
    return order, valid, count


def on_device(
    latent_pages, rope_pages, page_place, lengths, q_latent, q_rope, new_latent, new_rope
):
    here = lax.axis_index("req")
    pair = here // (2 * NX * NC)
    place = page_place.astype(jnp.bfloat16)
    length = jnp.concatenate([lengths // 128, lengths % 128]).astype(jnp.bfloat16)
    row = jnp.pad(jnp.concatenate([place, length]), (0, 512 - 260))
    row = jnp.broadcast_to(row[None, :], (META, 512))
    query = jnp.concatenate(
        [q_latent.reshape(2 * ROWS, 512), q_rope.reshape(META, 512)], axis=0
    )
    first = jnp.concatenate([query, row], axis=0)
    came = [
        lax.ppermute(query if d else first, AXES, [(t, s) for s, t in home_pairs(d)])
        for d in range(4)
    ]
    whole = pl.BlockSpec(memory_space=pltpu.VMEM)
    scalars = pl.BlockSpec(memory_space=pltpu.SMEM)
    exchange = functools.partial(
        lax.all_to_all,
        axis_name=AXES,
        split_axis=0,
        concat_axis=0,
        axis_index_groups=page_groups(),
        tiled=True,
    )
    rope = exchange(rope_pages.reshape(SLOTS, PAGE // 2, 2 * ROPE))
    latent_pages, rope, came = lax.optimization_barrier((latent_pages, rope, came))
    lat = exchange(latent_pages)
    queries = []
    for part in came:
        part_rope = part[2 * ROWS : 2 * ROWS + META].reshape(2, ROWS, ROPE)
        part_lat = part[: 2 * ROWS].reshape(2, ROWS, 512)
        queries.append(jnp.concatenate([part_lat, part_rope, part_rope], axis=2))
    queries = jnp.concatenate(queries, axis=1)
    keys = pl.pallas_call(
        spread_kernel,
        out_shape=jax.ShapeDtypeStruct((SLOTS, PAGE, 2 * ROPE), jnp.bfloat16),
        in_specs=[whole],
        out_specs=whole,
        name="spread",
    )(rope)
    table = page_table(came[0][2 * ROWS + META].astype(jnp.int32), pair)
    partial = jax.ShapeDtypeStruct((2 * ROWS + META, 512), jnp.bfloat16)
    parts = pl.pallas_call(
        attend_kernel,
        out_shape=[partial] * 4,
        in_specs=[scalars] * 3 + [pl.BlockSpec(memory_space=pl.ANY), whole, whole],
        out_specs=[whole] * 4,
        scratch_shapes=[
            pltpu.VMEM((SLOTS, PAGE, 512), jnp.bfloat16),
            pltpu.VMEM((SLOTS // BLOCK, 4 * ROWS, TOKENS), jnp.float32),
            pltpu.VMEM((4 * ROWS, 512), jnp.float32),
            pltpu.SemaphoreType.DMA((SLOTS,)),
        ],
        compiler_params=pltpu.CompilerParams(vmem_limit_bytes=20 * 1024 * 1024),
        cost_estimate=pl.CostEstimate(
            flops=4 * ROWS * 6144 * 1152 * 2, bytes_accessed=8 << 20, transcendentals=1 << 20
        ),
        name="attend",
    )(*table, lat, keys, queries)
    home = [lax.ppermute(part, AXES, home_pairs(d)) for d, part in enumerate(parts)]
    out = pl.pallas_call(
        merge_kernel,
        out_shape=jax.ShapeDtypeStruct((2, ROWS, 512), jnp.bfloat16),
        in_specs=[whole] * 6,
        out_specs=whole,
        name="merge",
    )(*home, fresh_scores(q_latent, q_rope, new_latent, new_rope), new_latent)
    return out.reshape(q_latent.shape)


def solution(mesh):
    return jax.shard_map(
        on_device,
        mesh=mesh,
        in_specs=(
            P(("req", "head"), None, None),
            P(("req", "head"), None),
            P("req"),
            P("req"),
            P("req", None, "head", None),
            P("req", None, "head", None),
            P("req", None, None),
            P("req", None, None),
        ),
        out_specs=P("req", None, "head", None),
        check_vma=False,
    )
```

time: 170 us -> 161 us (0.947)
  waiting for transfers between devices: 97.3 us -> 82.6 us
  Pallas kernels: 11.5 us -> 16.5 us
  local copies, waits for them, and re-layouts: 3.19 us -> 6.64 us
  starting transfers between devices: 50.2 us -> 47.4 us
    all_to_all x1 -> x2, waiting for transfers between devices: 0.01 us -> 64.4 us  [the longest x1 64.4 us: on_device(): lat = exchange(latent_pages)]
    ppermute x4, waiting for transfers between devices: 71.8 us -> 9.85 us  [on_device(): lax.ppermute(query if d else first, AXES, [(t, s) for s, t in home_pairs(...]
    ppermute x9 -> x0, starting transfers between devices: 18 us -> none  [the longest x3 11.8 us: move_ropes(): part = lax.ppermute(part, 'head', [(i, (i + t) % NY) for i in range(NY)])]
    ppermute x9 -> x0, waiting for transfers between devices: 15 us -> none  [the longest x6 8.98 us: move_ropes(): part = lax.ppermute(part, 'req', pairs)]
    all_to_all x1 -> x2, starting transfers between devices: 10.7 us -> 23.8 us  [the longest x1 13.5 us: on_device(): lat = exchange(latent_pages)]
    pallas_call x0 -> x1, Pallas kernels: none -> 5.68 us  [on_device(): pl.pallas_call(spread_kernel, out_shape=jax.ShapeDtypeStruct((SLOTS, PAGE...]
    ppermute x4, starting transfers between devices: 9.4 us -> 14.7 us  [on_device(): lax.ppermute(query if d else first, AXES, [(t, s) for s, t in home_pairs(...]
    ppermute x4, starting transfers between devices: 12.2 us -> 8.92 us  [on_device(): lax.ppermute(part, AXES, home_pairs(d))]
  transfers between devices with their start and end apart: 18 -> 10, of which waited for: 10 -> 7; matrix products, arithmetic and copies ran while one was open for 3% -> 3% of each run, Pallas kernels for 0% -> 4%
where the time goes in v3:
time: 161 us; the launch traced here: 159 us
  waiting for transfers between devices  82.6 us (51%)
  starting transfers between devices  47.4 us (29%)
  Pallas kernels  16.5 us (10%)
  local copies, waits for them, and re-layouts  6.64 us (4%)
  between operations  2.95 us (2%)
  other arithmetic  2.52 us (2%)
    all_to_all x1, waiting for transfers between devices, on_device(): lat = exchange(latent_pages)  64.4 us
    ppermute x4, starting transfers between devices, on_device(): lax.ppermute(query if d else first, AXES, [(t, s) for s, t in home_pairs(...  14.7 us
    all_to_all x1, starting transfers between devices, on_device(): lat = exchange(latent_pages)  13.5 us
    all_to_all x1, starting transfers between devices, on_device(): rope = exchange(rope_pages.reshape(SLOTS, PAGE // 2, 2 * ROPE))  10.3 us
    ppermute x4, waiting for transfers between devices, on_device(): lax.ppermute(query if d else first, AXES, [(t, s) for s, t in home_pairs(...  9.85 us
    ppermute x4, starting transfers between devices, on_device(): lax.ppermute(part, AXES, home_pairs(d))  8.92 us
    pallas_call x1, Pallas kernels, on_device(): pl.pallas_call(attend_kernel, out_shape=[partial] * 4, in_specs=[scalars]...  8.55 us
    ppermute x4, waiting for transfers between devices, on_device(): lax.ppermute(part, AXES, home_pairs(d))  8.35 us
  transfers between devices with their start and end apart: 10, of which 7 were waited for; matrix products, arithmetic and copies ran while one was open for 3% of the time, Pallas kernels for 4%

profile of v3, /device:TPU:1, one launch (start us, length us, event | category | flops | bytes accessed | tf_op | source)
XLA Modules:
  0.0 159.0 jit_solution(14773731779363453705)
XLA Ops:
  0.0 2.2 %copy.14 = bf16[8,8,48,128]{3,2,1,0:T(8,128)(2,1)} copy(bf16[8,8,48,128]{3,1,2,0:T(8,128)(2,1)} %bitcast.31) | data formatting | bytes 1572864
  2.2 10.3 %all-to-all-start = ((bf16[64,48,128]{2,1,0:T(8,128)(2,1)}), bf16[64,48,128]{2,1,0:T(8,128)(2,1)S(1)}, u32[]{:S(2)}, u32[]{:S(2)}) async-start(bf16[64,48,128]{2,1,0:T(8,128)(2,1)} %bitcast.20), calls=%async_computation | async-start | bytes 1572864 | tf_op jit(solution)/shard_map/all_to_all | solution.py:270
  12.9 0.7 collective-permute-start
  13.6 6.7 %collective-permute-start.1 = (bf16[144,512]{1,0:T(8,128)(2,1)S(1)}, bf16[144,512]{1,0:T(8,128)(2,1)S(1)}, u32[]{:S(2)}, u32[]{:S(2)}) collective-permute-start(bf16[144,512]{1,0:T(8,128)(2,1)S(1)} %pad_maximum_fusion.1), channel_id=1, source_target_pairs={{1,0},{66,1},{131,2},{192,3},{5,4},{198,5},{135,6},{68,7},{9,8},{7... | collective-permute-start | bytes 442376 | tf_op jit(solution)/shard_map/ppermute | solution.py:257
  20.3 6.0 %collective-permute-start.2 = (bf16[144,512]{1,0:T(8,128)(2,1)S(1)}, bf16[144,512]{1,0:T(8,128)(2,1)S(1)}, u32[]{:S(2)}, u32[]{:S(2)}) collective-permute-start(bf16[144,512]{1,0:T(8,128)(2,1)S(1)} %pad_maximum_fusion.1), channel_id=1, source_target_pairs={{2,0},{67,1},{128,2},{193,3},{6,4},{199,5},{132,6},{69,7},{10,8},{... | collective-permute-start | bytes 442376 | tf_op jit(solution)/shard_map/ppermute | solution.py:257
  26.3 1.3 collective-permute-start.3
  27.6 1.8 %collective-permute-done.1 = bf16[144,512]{1,0:T(8,128)(2,1)S(1)} collective-permute-done((bf16[144,512]{1,0:T(8,128)(2,1)S(1)}, bf16[144,512]{1,0:T(8,128)(2,1)S(1)}, u32[]{:S(2)}, u32[]{:S(2)}) %collective-permute-start.1) | collective-permute-done | bytes 147488 | tf_op jit(solution)/shard_map/ppermute | solution.py:257
  29.4 6.0 %collective-permute-done.2 = bf16[144,512]{1,0:T(8,128)(2,1)S(1)} collective-permute-done((bf16[144,512]{1,0:T(8,128)(2,1)S(1)}, bf16[144,512]{1,0:T(8,128)(2,1)S(1)}, u32[]{:S(2)}, u32[]{:S(2)}) %collective-permute-start.2) | collective-permute-done | bytes 147488 | tf_op jit(solution)/shard_map/ppermute | solution.py:257
  35.4 2.0 %collective-permute-done.3 = bf16[144,512]{1,0:T(8,128)(2,1)S(1)} collective-permute-done((bf16[144,512]{1,0:T(8,128)(2,1)S(1)}, bf16[144,512]{1,0:T(8,128)(2,1)S(1)}, u32[]{:S(2)}, u32[]{:S(2)}) %collective-permute-start.3) | collective-permute-done | bytes 147488 | tf_op jit(solution)/shard_map/ppermute | solution.py:257
  37.4 1.0 copy-done.2
  38.4 13.5 %all-to-all-start.1 = ((bf16[64,96,512]{2,1,0:T(8,128)(2,1)}), bf16[64,96,512]{2,1,0:T(8,128)(2,1)}, u32[]{:S(2)}, u32[]{:S(2)}) async-start(bf16[64,96,512]{2,1,0:T(8,128)(2,1)} %param.8), calls=%async_computation.1 | async-start | bytes 12582912 | tf_op jit(solution)/shard_map/all_to_all | solution.py:272
  54.6 5.7 %spread.1.keys_ref = bf16[64,96,128]{2,1,0:T(8,128)(2,1)} custom-call(bf16[64,48,128]{2,1,0:T(8,128)(2,1)} %copy-done.2), custom_call_target="tpu_custom_call" | custom-call | tf_op jit(solution)/shard_map/spread/pallas_call | solution.py:279
  60.3 0.8 gather_fusion
  62.5 0.7 fusion.23
  63.1 1.3 pad_add_fusion.count_ref
  64.9 64.4 %all-to-all-done.1.lat_ref = bf16[64,96,512]{2,1,0:T(8,128)(2,1)} async-done(((bf16[64,96,512]{2,1,0:T(8,128)(2,1)}), bf16[64,96,512]{2,1,0:T(8,128)(2,1)}, u32[]{:S(2)}, u32[]{:S(2)}) %all-to-all-start.1) | async-done | bytes 6291488 | tf_op jit(solution)/shard_map/all_to_all | solution.py:272
  129.3 8.6 %attend.1 = (bf16[144,512]{1,0:T(8,128)(2,1)S(1)}, bf16[144,512]{1,0:T(8,128)(2,1)S(1)}, bf16[144,512]{1,0:T(8,128)(2,1)S(1)}, bf16[144,512]{1,0:T(8,128)(2,1)S(1)}) custom-call(s32[64]{0:T(128)S(1)} %get-tuple-element.28.order_ref, s32[64]{0:T(128)S(1)} %get-tuple-element.27.valid_ref, s32[2]{0:T(128)S(1)} %pad_add_fusion.count_ref, ...), custom_call_target="tpu_custom_call" | custom-call | flops 3623878656 | bytes 8388608 | tf_op jit(solution)/shard_map/attend/pallas_call | solution.py:288
  138.5 3.1 %collective-permute-start.5 = (bf16[144,512]{1,0:T(8,128)(2,1)S(1)}, bf16[144,512]{1,0:T(8,128)(2,1)S(1)}, u32[]{:S(2)}, u32[]{:S(2)}) collective-permute-start(bf16[144,512]{1,0:T(8,128)(2,1)S(1)} %get-tuple-element.22), channel_id=1, source_target_pairs={{0,1},{1,66},{2,131},{3,192},{4,5},{5,198},{6,135},{7,68},{8,9},{9... | collective-permute-start | bytes 442376 | tf_op jit(solution)/shard_map/ppermute | solution.py:305
  141.6 2.1 %collective-permute-start.6 = (bf16[144,512]{1,0:T(8,128)(2,1)S(1)}, bf16[144,512]{1,0:T(8,128)(2,1)S(1)}, u32[]{:S(2)}, u32[]{:S(2)}) collective-permute-start(bf16[144,512]{1,0:T(8,128)(2,1)S(1)} %get-tuple-element.23), channel_id=1, source_target_pairs={{0,2},{1,67},{2,128},{3,193},{4,6},{5,199},{6,132},{7,69},{8,10},{... | collective-permute-start | bytes 442376 | tf_op jit(solution)/shard_map/ppermute | solution.py:305
  143.7 3.0 %collective-permute-start.7 = (bf16[144,512]{1,0:T(8,128)(2,1)S(1)}, bf16[144,512]{1,0:T(8,128)(2,1)S(1)}, u32[]{:S(2)}, u32[]{:S(2)}) collective-permute-start(bf16[144,512]{1,0:T(8,128)(2,1)S(1)} %get-tuple-element.24), channel_id=1, source_target_pairs={{0,3},{1,64},{2,129},{3,194},{4,7},{5,196},{6,133},{7,70},{8,11},{... | collective-permute-start | bytes 442376 | tf_op jit(solution)/shard_map/ppermute | solution.py:305
  146.9 0.8 copy.11
  147.7 2.4 %collective-permute-done.5.p1 = bf16[144,512]{1,0:T(8,128)(2,1)S(1)} collective-permute-done((bf16[144,512]{1,0:T(8,128)(2,1)S(1)}, bf16[144,512]{1,0:T(8,128)(2,1)S(1)}, u32[]{:S(2)}, u32[]{:S(2)}) %collective-permute-start.5) | collective-permute-done | bytes 147488 | tf_op jit(solution)/shard_map/ppermute | solution.py:305
  150.1 5.5 %collective-permute-done.6.p2 = bf16[144,512]{1,0:T(8,128)(2,1)S(1)} collective-permute-done((bf16[144,512]{1,0:T(8,128)(2,1)S(1)}, bf16[144,512]{1,0:T(8,128)(2,1)S(1)}, u32[]{:S(2)}, u32[]{:S(2)}) %collective-permute-start.6) | collective-permute-done | bytes 147488 | tf_op jit(solution)/shard_map/ppermute | solution.py:305
  156.7 2.3 %merge.1 = bf16[2,64,512]{2,1,0:T(8,128)(2,1)} custom-call(bf16[144,512]{1,0:T(8,128)(2,1)} %copy-done.8, bf16[144,512]{1,0:T(8,128)(2,1)} %copy-done.9, bf16[144,512]{1,0:T(8,128)(2,1)} %copy-done.10, bf16[144,512]{1,0:T(8,128)(2,1)} %copy-done.11, f32[2,64,2]{2,1,0:T(8,128)} %bitcast.38, bf16[2,2,512]{2,1,0:T(2,128)(2,1)} %new_lat_ref.1), custom_call_target="tpu_custom_call" | custom-call | tf_op jit(solution)/shard_map/merge/pallas_call | solution.py:306
  (69 shorter events, 3.9 us)
Async XLA Ops:
  0.0 146.8 %copy-start = (bf16[2,2,64]{2,1,0:T(2,128)(2,1)S(1)}, bf16[2,2,64]{2,1,0:T(2,128)(2,1)}, u32[]{:S(2)}) copy-start(bf16[2,2,64]{2,1,0:T(2,128)(2,1)} %param.15) | copy-start | bytes 1540
  0.0 12.6 %copy-start.14 = (s32[256]{0:T(256)S(1)}, s32[256]{0:T(256)}, u32[]{:S(2)}) copy-start(s32[256]{0:T(256)} %param.10) | copy-start | bytes 3076
  0.0 12.6 %copy-start.12 = (bf16[2,2,32,64]{3,2,1,0:T(8,128)(2,1)S(1)}, bf16[2,2,32,64]{3,2,1,0:T(8,128)(2,1)}, u32[]{:S(2)}) copy-start(bf16[2,2,32,64]{3,2,1,0:T(8,128)(2,1)} %param.13) | copy-start | bytes 49156
  0.0 12.7 %copy-start.15 = (s32[2]{0:T(128)S(1)}, s32[2]{0:T(128)}, u32[]{:S(2)}) copy-start(s32[2]{0:T(128)} %param.11) | copy-start | bytes 28
  0.0 12.8 %copy-start.7 = (bf16[2,2,32,512]{3,2,1,0:T(8,128)(2,1)S(1)}, bf16[2,2,32,512]{3,2,1,0:T(8,128)(2,1)}, u32[]{:S(2)}) copy-start(bf16[2,2,32,512]{3,2,1,0:T(8,128)(2,1)} %param.12) | copy-start | bytes 393220
  2.2 35.2 %all-to-all-start = ((bf16[64,48,128]{2,1,0:T(8,128)(2,1)}), bf16[64,48,128]{2,1,0:T(8,128)(2,1)S(1)}, u32[]{:S(2)}, u32[]{:S(2)}) async-start(bf16[64,48,128]{2,1,0:T(8,128)(2,1)} %bitcast.20), calls=%async_computation | async-start | bytes 1572864 | tf_op jit(solution)/shard_map/all_to_all | solution.py:270
  12.9 24.6 %collective-permute-start = (bf16[160,512]{1,0:T(8,128)(2,1)S(1)}, bf16[160,512]{1,0:T(8,128)(2,1)S(1)}, u32[]{:S(2)}, u32[]{:S(2)}) collective-permute-start(bf16[160,512]{1,0:T(8,128)(2,1)S(1)} %pad_maximum_fusion), channel_id=1, source_target_pairs={{0,0},{65,1},{130,2},{195,3},{4,4},{197,5},{134,6},{71,7},{8,8},{7... | collective-permute-start | bytes 491528 | tf_op jit(solution)/shard_map/ppermute | solution.py:257
  13.6 38.5 %copy-start.13 = (bf16[2,2,512]{2,1,0:T(2,128)(2,1)S(1)}, bf16[2,2,512]{2,1,0:T(2,128)(2,1)}, u32[]{:S(2)}) copy-start(bf16[2,2,512]{2,1,0:T(2,128)(2,1)} %new_lat_ref.1) | copy-start | bytes 12292
  13.6 15.8 %collective-permute-start.1 = (bf16[144,512]{1,0:T(8,128)(2,1)S(1)}, bf16[144,512]{1,0:T(8,128)(2,1)S(1)}, u32[]{:S(2)}, u32[]{:S(2)}) collective-permute-start(bf16[144,512]{1,0:T(8,128)(2,1)S(1)} %pad_maximum_fusion.1), channel_id=1, source_target_pairs={{1,0},{66,1},{131,2},{192,3},{5,4},{198,5},{135,6},{68,7},{9,8},{7... | collective-permute-start | bytes 442376 | tf_op jit(solution)/shard_map/ppermute | solution.py:257
  20.3 15.2 %collective-permute-start.2 = (bf16[144,512]{1,0:T(8,128)(2,1)S(1)}, bf16[144,512]{1,0:T(8,128)(2,1)S(1)}, u32[]{:S(2)}, u32[]{:S(2)}) collective-permute-start(bf16[144,512]{1,0:T(8,128)(2,1)S(1)} %pad_maximum_fusion.1), channel_id=1, source_target_pairs={{2,0},{67,1},{128,2},{193,3},{6,4},{199,5},{132,6},{69,7},{10,8},{... | collective-permute-start | bytes 442376 | tf_op jit(solution)/shard_map/ppermute | solution.py:257
  26.3 11.2 %collective-permute-start.3 = (bf16[144,512]{1,0:T(8,128)(2,1)S(1)}, bf16[144,512]{1,0:T(8,128)(2,1)S(1)}, u32[]{:S(2)}, u32[]{:S(2)}) collective-permute-start(bf16[144,512]{1,0:T(8,128)(2,1)S(1)} %pad_maximum_fusion.1), channel_id=1, source_target_pairs={{3,0},{64,1},{129,2},{194,3},{7,4},{196,5},{133,6},{70,7},{11,8},{... | collective-permute-start | bytes 442376 | tf_op jit(solution)/shard_map/ppermute | solution.py:257
  29.4 22.8 %copy-start.4 = (bf16[144,512]{1,0:T(8,128)(2,1)}, bf16[144,512]{1,0:T(8,128)(2,1)S(1)}, u32[]{:S(2)}) copy-start(bf16[144,512]{1,0:T(8,128)(2,1)S(1)} %collective-permute-done.1) | copy-start | bytes 442372
  35.4 16.8 %copy-start.5 = (bf16[144,512]{1,0:T(8,128)(2,1)}, bf16[144,512]{1,0:T(8,128)(2,1)S(1)}, u32[]{:S(2)}) copy-start(bf16[144,512]{1,0:T(8,128)(2,1)S(1)} %collective-permute-done.2) | copy-start | bytes 442372
  37.4 14.8 %copy-start.6 = (bf16[144,512]{1,0:T(8,128)(2,1)}, bf16[144,512]{1,0:T(8,128)(2,1)S(1)}, u32[]{:S(2)}) copy-start(bf16[144,512]{1,0:T(8,128)(2,1)S(1)} %collective-permute-done.3) | copy-start | bytes 442372
  37.4 15.2 %copy-start.3 = (bf16[160,512]{1,0:T(8,128)(2,1)}, bf16[160,512]{1,0:T(8,128)(2,1)S(1)}, u32[]{:S(2)}) copy-start(bf16[160,512]{1,0:T(8,128)(2,1)S(1)} %collective-permute-done) | copy-start | bytes 491524
  38.4 90.9 %all-to-all-start.1 = ((bf16[64,96,512]{2,1,0:T(8,128)(2,1)}), bf16[64,96,512]{2,1,0:T(8,128)(2,1)}, u32[]{:S(2)}, u32[]{:S(2)}) async-start(bf16[64,96,512]{2,1,0:T(8,128)(2,1)} %param.8), calls=%async_computation.1 | async-start | bytes 12582912 | tf_op jit(solution)/shard_map/all_to_all | solution.py:272
  54.6 10.1 %slice-start = ((bf16[160,512]{1,0:T(8,128)(2,1)}), bf16[128,512]{1,0:T(8,128)(2,1)S(1)}, s32[]{:S(2)}) async-start(bf16[160,512]{1,0:T(8,128)(2,1)} %copy-done.3), calls=%async_computation.2 | async-start | bytes 262144 | tf_op jit(solution)/shard_map/slice | solution.py:276
  54.6 10.1 %slice-start.1 = ((bf16[144,512]{1,0:T(8,128)(2,1)}), bf16[128,512]{1,0:T(8,128)(2,1)S(1)}, s32[]{:S(2)}) async-start(bf16[144,512]{1,0:T(8,128)(2,1)} %copy-done.4), calls=%async_computation.3 | async-start | bytes 262144 | tf_op jit(solution)/shard_map/slice | solution.py:276
  54.6 10.1 %slice-start.2 = ((bf16[144,512]{1,0:T(8,128)(2,1)}), bf16[128,512]{1,0:T(8,128)(2,1)S(1)}, s32[]{:S(2)}) async-start(bf16[144,512]{1,0:T(8,128)(2,1)} %copy-done.5), calls=%async_computation.4 | async-start | bytes 262144 | tf_op jit(solution)/shard_map/slice | solution.py:276
  60.3 69.0 %copy-start.1 = (bf16[64,96,128]{2,1,0:T(8,128)(2,1)S(1)}, bf16[64,96,128]{2,1,0:T(8,128)(2,1)}, u32[]{:S(2)}) copy-start(bf16[64,96,128]{2,1,0:T(8,128)(2,1)} %spread.1.keys_ref) | copy-start | bytes 4718596
  137.8 9.8 %collective-permute-start.4 = (bf16[144,512]{1,0:T(8,128)(2,1)S(1)}, bf16[144,512]{1,0:T(8,128)(2,1)S(1)}, u32[]{:S(2)}, u32[]{:S(2)}) collective-permute-start(bf16[144,512]{1,0:T(8,128)(2,1)S(1)} %get-tuple-element.21), channel_id=1, source_target_pairs={{0,0},{1,65},{2,130},{3,195},{4,4},{5,197},{6,134},{7,71},{8,8},{9... | collective-permute-start | bytes 442376 | tf_op jit(solution)/shard_map/ppermute | solution.py:305
  138.5 11.6 %collective-permute-start.5 = (bf16[144,512]{1,0:T(8,128)(2,1)S(1)}, bf16[144,512]{1,0:T(8,128)(2,1)S(1)}, u32[]{:S(2)}, u32[]{:S(2)}) collective-permute-start(bf16[144,512]{1,0:T(8,128)(2,1)S(1)} %get-tuple-element.22), channel_id=1, source_target_pairs={{0,1},{1,66},{2,131},{3,192},{4,5},{5,198},{6,135},{7,68},{8,9},{9... | collective-permute-start | bytes 442376 | tf_op jit(solution)/shard_map/ppermute | solution.py:305
  141.6 14.0 %collective-permute-start.6 = (bf16[144,512]{1,0:T(8,128)(2,1)S(1)}, bf16[144,512]{1,0:T(8,128)(2,1)S(1)}, u32[]{:S(2)}, u32[]{:S(2)}) collective-permute-start(bf16[144,512]{1,0:T(8,128)(2,1)S(1)} %get-tuple-element.23), channel_id=1, source_target_pairs={{0,2},{1,67},{2,128},{3,193},{4,6},{5,199},{6,132},{7,69},{8,10},{... | collective-permute-start | bytes 442376 | tf_op jit(solution)/shard_map/ppermute | solution.py:305
  143.7 12.3 %collective-permute-start.7 = (bf16[144,512]{1,0:T(8,128)(2,1)S(1)}, bf16[144,512]{1,0:T(8,128)(2,1)S(1)}, u32[]{:S(2)}, u32[]{:S(2)}) collective-permute-start(bf16[144,512]{1,0:T(8,128)(2,1)S(1)} %get-tuple-element.24), channel_id=1, source_target_pairs={{0,3},{1,64},{2,129},{3,194},{4,7},{5,196},{6,133},{7,70},{8,11},{... | collective-permute-start | bytes 442376 | tf_op jit(solution)/shard_map/ppermute | solution.py:305
  (6 other events, 26.7 us)

commit v4 on v3

--- a/solution.py
+++ b/solution.py
@@ -90,79 +90,66 @@
 
 def attend_kernel(
     order_ref, valid_ref, count_ref, lat_ref, keys_ref, query_ref,
-    o0, o1, o2, o3, page_ref, score_ref, acc_ref, sems
+    o0, o1, o2, o3, score_ref, acc_ref
 ):
     outs = (o0, o1, o2, o3)
-
-    def copy(place):
-        return pltpu.make_async_copy(
-            lat_ref.at[order_ref[place]], page_ref.at[place], sems.at[place]
-        )
-
-    def begin(place, carry):
-        copy(place).start()
-        return carry
-
-    lax.fori_loop(0, count_ref[0] + count_ref[1], begin, 0)
-    lane = lax.broadcasted_iota(jnp.int32, (1, TOKENS), 1)
     meta_lane = lax.broadcasted_iota(jnp.int32, (4 * ROWS, 128), 1)
     meta = jnp.zeros((4 * ROWS, 128), jnp.float32)
     for request in range(2):
-        rows = slice(request * ROWS, (request + 1) * ROWS)
         start = count_ref[0] * request
         count = count_ref[request]
         blocks = (count + BLOCK - 1) // BLOCK
-
-        def place_of(block, index):
-            return start + jnp.minimum(block * BLOCK + index, count - 1)
-
-        def latents(block):
-            return jnp.concatenate([page_ref[place_of(block, i)] for i in range(BLOCK)], axis=0)
-
-        def score_block(block, maxima):
-            for i in range(BLOCK):
-
-                @pl.when(block * BLOCK + i < count)
-                def _():
-                    copy(start + block * BLOCK + i).wait()
-
-            rope_keys = jnp.concatenate(
-                [keys_ref[order_ref[place_of(block, i)]] for i in range(BLOCK)], axis=0
-            )
-            keys = jnp.concatenate([latents(block), rope_keys], axis=1)
-            limit = jnp.zeros((1, TOKENS), jnp.int32)
-            for i in range(BLOCK):
-                valid = jnp.where(block * BLOCK + i < count, valid_ref[place_of(block, i)], 0)
+        doubles, single = blocks // 2, blocks % 2
+
+        def slots(block, size):
+            return [
+                start + jnp.minimum(block * BLOCK + i, count - 1) for i in range(size * BLOCK)
+            ]
+
+        def latents(places):
+            return jnp.concatenate([lat_ref[order_ref[p]] for p in places], axis=0)
+
+        def score_blocks(size, block, maxima):
+            places = slots(block, size)
+            rope_keys = jnp.concatenate([keys_ref[order_ref[p]] for p in places], axis=0)
+            keys = jnp.concatenate([latents(places), rope_keys], axis=1)
+            lane = lax.broadcasted_iota(jnp.int32, (1, size * TOKENS), 1)
+            limit = jnp.zeros((1, size * TOKENS), jnp.int32)
+            for i, p in enumerate(places):
+                valid = jnp.where(block * BLOCK + i < count, valid_ref[p], 0)
                 limit = jnp.where(lane >= i * PAGE, i * PAGE + valid, limit)
-            score = contract(query_ref[request], keys) * SCALE + jnp.where(lane < limit, 0.0, NEG)
-            score_ref[block] = score
-            for i in range(TOKENS // 128):
+            score = contract(query_ref[request], keys) * SCALE
+            score = score + jnp.where(lane < limit, 0.0, NEG)
+            for i in range(size):
+                score_ref[block + i] = score[:, i * TOKENS : (i + 1) * TOKENS]
+            for i in range(size * TOKENS // 128):
                 maxima = jnp.maximum(maxima, score[:, i * 128 : (i + 1) * 128])
             return maxima
 
-        maxima = lax.fori_loop(
-            0, blocks, score_block, jnp.full((4 * ROWS, 128), NEG, jnp.float32)
-        )
+        def weigh_blocks(size, block, total):
+            weight = [jnp.exp2(score_ref[block + i] - top) for i in range(size)]
+            for part in weight:
+                for i in range(TOKENS // 128):
+                    total = total + part[:, i * 128 : (i + 1) * 128]
+            weight = jnp.concatenate([w.astype(jnp.bfloat16) for w in weight], axis=1)
+            acc_ref[...] += jnp.dot(
+                weight, latents(slots(block, size)), preferred_element_type=jnp.float32
+            )
+            return total
+
+        def over(step, carry):
+            carry = lax.fori_loop(0, doubles, lambda i, c: step(2, 2 * i, c), carry)
+            return lax.fori_loop(0, single, lambda i, c: step(1, 2 * doubles, c), carry)
+
+        maxima = over(score_blocks, jnp.full((4 * ROWS, 128), NEG, jnp.float32))
         top = jnp.max(maxima, axis=1, keepdims=True)
         acc_ref[...] = jnp.zeros_like(acc_ref)
-
-        def weigh_block(block, total):
-            weight = jnp.exp2(score_ref[block] - top)
-            for i in range(TOKENS // 128):
-                total = total + weight[:, i * 128 : (i + 1) * 128]
-            acc_ref[...] += jnp.dot(
-                weight.astype(jnp.bfloat16), latents(block), preferred_element_type=jnp.float32
-            )
-            return total
-
-        total = lax.fori_loop(
-            0, blocks, weigh_block, jnp.zeros((4 * ROWS, 128), jnp.float32)
-        )
+        total = over(weigh_blocks, jnp.zeros((4 * ROWS, 128), jnp.float32))
         total = jnp.sum(total, axis=1, keepdims=True)
         total = jnp.where(total > 0.0, total, 1.0)
         result = (acc_ref[...] / total).astype(jnp.bfloat16)
         for i, out in enumerate(outs):
-            out[rows, :] = result[i * ROWS : (i + 1) * ROWS, :]
+            out[request * ROWS : (request + 1) * ROWS, :] = result[i * ROWS : (i + 1) * ROWS, :]
         rest = top + jnp.log2(total)
         for part in range(3):
             piece = rest.astype(jnp.bfloat16).astype(jnp.float32)
@@ -281,6 +268,7 @@
         out_shape=jax.ShapeDtypeStruct((SLOTS, PAGE, 2 * ROPE), jnp.bfloat16),
         in_specs=[whole],
         out_specs=whole,
+        compiler_params=pltpu.CompilerParams(vmem_limit_bytes=8 * 1024 * 1024),
         name="spread",
     )(rope)
     table = page_table(came[0][2 * ROWS + META].astype(jnp.int32), pair)
@@ -288,15 +276,13 @@
     parts = pl.pallas_call(
         attend_kernel,
         out_shape=[partial] * 4,
-        in_specs=[scalars] * 3 + [pl.BlockSpec(memory_space=pl.ANY), whole, whole],
+        in_specs=[scalars] * 3 + [whole] * 3,
         out_specs=[whole] * 4,
         scratch_shapes=[
-            pltpu.VMEM((SLOTS, PAGE, 512), jnp.bfloat16),
             pltpu.VMEM((SLOTS // BLOCK, 4 * ROWS, TOKENS), jnp.float32),
             pltpu.VMEM((4 * ROWS, 512), jnp.float32),
-            pltpu.SemaphoreType.DMA((SLOTS,)),
         ],
-        compiler_params=pltpu.CompilerParams(vmem_limit_bytes=20 * 1024 * 1024),
+        compiler_params=pltpu.CompilerParams(vmem_limit_bytes=32 * 1024 * 1024),
         cost_estimate=pl.CostEstimate(
             flops=4 * ROWS * 6144 * 1152 * 2, bytes_accessed=8 << 20, transcendentals=1 << 20
         ),
@@ -308,6 +294,7 @@
         out_shape=jax.ShapeDtypeStruct((2, ROWS, 512), jnp.bfloat16),
         in_specs=[whole] * 6,
         out_specs=whole,
+        compiler_params=pltpu.CompilerParams(vmem_limit_bytes=4 * 1024 * 1024),
         name="merge",
     )(*home, fresh_scores(q_latent, q_rope, new_latent, new_rope), new_latent)
     return out.reshape(q_latent.shape)

time: 161 us -> 157 us (0.975)
  Pallas kernels: 16.5 us -> 13.7 us
  starting transfers between devices: 47.4 us -> 44.9 us
  waiting for transfers between devices: 82.6 us -> 84.6 us
    ppermute x4, starting transfers between devices: 8.92 us -> 6.44 us  [on_device(): lax.ppermute(part, AXES, home_pairs(d))]
    pallas_call x1, Pallas kernels: 5.68 us -> 3.33 us  [on_device(): pl.pallas_call(spread_kernel, out_shape=jax.ShapeDtypeStruct((SLOTS, PAGE...]
    ppermute x4, waiting for transfers between devices: 8.35 us -> 10.2 us  [on_device(): lax.ppermute(part, AXES, home_pairs(d))]
    unnamed x33 -> x21, local copies, waits for them, and re-layouts: 3.9 us -> 2.25 us
  transfers between devices with their start and end apart: 10 -> 10, of which waited for: 7 -> 6; matrix products, arithmetic and copies ran while one was open for 3% -> 5% of each run, Pallas kernels for 4% -> 2%
where the time goes in v4:
time: 157 us; the launch traced here: 156 us
  waiting for transfers between devices  84.6 us (54%)
  starting transfers between devices  44.9 us (29%)
  Pallas kernels  13.7 us (9%)
  local copies, waits for them, and re-layouts  5.64 us (4%)
  other arithmetic  3.61 us (2%)
  between operations  2.86 us (2%)
    all_to_all x1, waiting for transfers between devices, on_device(): lat = exchange(latent_pages)  64.5 us
    ppermute x4, starting transfers between devices, on_device(): lax.ppermute(query if d else first, AXES, [(t, s) for s, t in home_pairs(...  14.7 us
    all_to_all x1, starting transfers between devices, on_device(): lat = exchange(latent_pages)  13.5 us
    all_to_all x1, starting transfers between devices, on_device(): rope = exchange(rope_pages.reshape(SLOTS, PAGE // 2, 2 * ROPE))  10.3 us
    ppermute x4, waiting for transfers between devices, on_device(): lax.ppermute(part, AXES, home_pairs(d))  10.2 us
    ppermute x4, waiting for transfers between devices, on_device(): lax.ppermute(query if d else first, AXES, [(t, s) for s, t in home_pairs(...  9.85 us
    pallas_call x1, Pallas kernels, on_device(): pl.pallas_call(attend_kernel, out_shape=[partial] * 4, in_specs=[scalars]...  9.16 us
    ppermute x4, starting transfers between devices, on_device(): lax.ppermute(part, AXES, home_pairs(d))  6.44 us
  transfers between devices with their start and end apart: 10, of which 6 were waited for; matrix products, arithmetic and copies ran while one was open for 5% of the time, Pallas kernels for 2%

profile of v4, /device:TPU:1, one launch (start us, length us, event | category | flops | bytes accessed | tf_op | source)
XLA Modules:
  0.0 155.6 jit_solution(6520751734153972818)
XLA Ops:
  0.0 2.2 %copy.14 = bf16[8,8,48,128]{3,2,1,0:T(8,128)(2,1)} copy(bf16[8,8,48,128]{3,1,2,0:T(8,128)(2,1)} %bitcast.32) | data formatting | bytes 1572864
  2.2 10.3 %all-to-all-start = ((bf16[64,48,128]{2,1,0:T(8,128)(2,1)}), bf16[64,48,128]{2,1,0:T(8,128)(2,1)S(1)}, u32[]{:S(2)}, u32[]{:S(2)}) async-start(bf16[64,48,128]{2,1,0:T(8,128)(2,1)} %bitcast.20), calls=%async_computation | async-start | bytes 1572864 | tf_op jit(solution)/shard_map/all_to_all | solution.py:257
  13.6 6.7 %collective-permute-start.1 = (bf16[144,512]{1,0:T(8,128)(2,1)S(1)}, bf16[144,512]{1,0:T(8,128)(2,1)S(1)}, u32[]{:S(2)}, u32[]{:S(2)}) collective-permute-start(bf16[144,512]{1,0:T(8,128)(2,1)S(1)} %pad_maximum_fusion.1), channel_id=1, source_target_pairs={{1,0},{66,1},{131,2},{192,3},{5,4},{198,5},{135,6},{68,7},{9,8},{7... | collective-permute-start | bytes 442376 | tf_op jit(solution)/shard_map/ppermute | solution.py:244
  20.3 6.0 %collective-permute-start.2 = (bf16[144,512]{1,0:T(8,128)(2,1)S(1)}, bf16[144,512]{1,0:T(8,128)(2,1)S(1)}, u32[]{:S(2)}, u32[]{:S(2)}) collective-permute-start(bf16[144,512]{1,0:T(8,128)(2,1)S(1)} %pad_maximum_fusion.1), channel_id=1, source_target_pairs={{2,0},{67,1},{128,2},{193,3},{6,4},{199,5},{132,6},{69,7},{10,8},{... | collective-permute-start | bytes 442376 | tf_op jit(solution)/shard_map/ppermute | solution.py:244
  26.3 1.3 collective-permute-start.3
  27.6 1.8 %collective-permute-done.1 = bf16[144,512]{1,0:T(8,128)(2,1)S(1)} collective-permute-done((bf16[144,512]{1,0:T(8,128)(2,1)S(1)}, bf16[144,512]{1,0:T(8,128)(2,1)S(1)}, u32[]{:S(2)}, u32[]{:S(2)}) %collective-permute-start.1) | collective-permute-done | bytes 147488 | tf_op jit(solution)/shard_map/ppermute | solution.py:244
  29.4 6.0 %collective-permute-done.2 = bf16[144,512]{1,0:T(8,128)(2,1)S(1)} collective-permute-done((bf16[144,512]{1,0:T(8,128)(2,1)S(1)}, bf16[144,512]{1,0:T(8,128)(2,1)S(1)}, u32[]{:S(2)}, u32[]{:S(2)}) %collective-permute-start.2) | collective-permute-done | bytes 147488 | tf_op jit(solution)/shard_map/ppermute | solution.py:244
  35.4 2.0 %collective-permute-done.3 = bf16[144,512]{1,0:T(8,128)(2,1)S(1)} collective-permute-done((bf16[144,512]{1,0:T(8,128)(2,1)S(1)}, bf16[144,512]{1,0:T(8,128)(2,1)S(1)}, u32[]{:S(2)}, u32[]{:S(2)}) %collective-permute-start.3) | collective-permute-done | bytes 147488 | tf_op jit(solution)/shard_map/ppermute | solution.py:244
  37.4 13.5 %all-to-all-start.1 = ((bf16[64,96,512]{2,1,0:T(8,128)(2,1)}), bf16[64,96,512]{2,1,0:T(8,128)(2,1)}, u32[]{:S(2)}, u32[]{:S(2)}) async-start(bf16[64,96,512]{2,1,0:T(8,128)(2,1)} %param.8), calls=%async_computation.1 | async-start | bytes 12582912 | tf_op jit(solution)/shard_map/all_to_all | solution.py:259
  52.2 0.7 reshape.446
  52.9 0.7 fusion.33
  54.9 3.3 %spread.1.keys_ref = bf16[64,96,128]{2,1,0:T(8,128)(2,1)S(1)} custom-call(bf16[64,48,128]{2,1,0:T(8,128)(2,1)S(1)} %all-to-all-done.rope_ref), custom_call_target="tpu_custom_call" | custom-call | tf_op jit(solution)/shard_map/spread/pallas_call | solution.py:266
  58.2 0.8 gather_fusion
  60.3 0.7 fusion.23
  61.1 1.4 pad_add_fusion.count_ref
  62.8 1.1 maximum_maximum_fusion.query_ref
  63.8 64.5 %all-to-all-done.1.lat_ref = bf16[64,96,512]{2,1,0:T(8,128)(2,1)} async-done(((bf16[64,96,512]{2,1,0:T(8,128)(2,1)}), bf16[64,96,512]{2,1,0:T(8,128)(2,1)}, u32[]{:S(2)}, u32[]{:S(2)}) %all-to-all-start.1) | async-done | bytes 6291488 | tf_op jit(solution)/shard_map/all_to_all | solution.py:259
  128.3 9.2 %attend.1 = (bf16[144,512]{1,0:T(8,128)(2,1)S(1)}, bf16[144,512]{1,0:T(8,128)(2,1)S(1)}, bf16[144,512]{1,0:T(8,128)(2,1)S(1)}, bf16[144,512]{1,0:T(8,128)(2,1)S(1)}) custom-call(s32[64]{0:T(128)S(1)} %get-tuple-element.28.order_ref, s32[64]{0:T(128)S(1)} %get-tuple-element.27.valid_ref, s32[2]{0:T(128)S(1)} %pad_add_fusion.count_ref, ...), custom_call_target="tpu_custom_call" | custom-call | flops 3623878656 | bytes 8388608 | tf_op jit(solution)/shard_map/attend/pallas_call | solution.py:276
  138.1 2.6 %collective-permute-start.5 = (bf16[144,512]{1,0:T(8,128)(2,1)S(1)}, bf16[144,512]{1,0:T(8,128)(2,1)S(1)}, u32[]{:S(2)}, u32[]{:S(2)}) collective-permute-start(bf16[144,512]{1,0:T(8,128)(2,1)S(1)} %get-tuple-element.22), channel_id=1, source_target_pairs={{0,1},{1,66},{2,131},{3,192},{4,5},{5,198},{6,135},{7,68},{8,9},{9... | collective-permute-start | bytes 442376 | tf_op jit(solution)/shard_map/ppermute | solution.py:291
  140.8 1.2 collective-permute-start.6
  141.9 2.0 %collective-permute-start.7 = (bf16[144,512]{1,0:T(8,128)(2,1)S(1)}, bf16[144,512]{1,0:T(8,128)(2,1)S(1)}, u32[]{:S(2)}, u32[]{:S(2)}) collective-permute-start(bf16[144,512]{1,0:T(8,128)(2,1)S(1)} %get-tuple-element.24), channel_id=1, source_target_pairs={{0,3},{1,64},{2,129},{3,194},{4,7},{5,196},{6,133},{7,70},{8,11},{... | collective-permute-start | bytes 442376 | tf_op jit(solution)/shard_map/ppermute | solution.py:291
  144.2 6.9 %collective-permute-done.5.p1 = bf16[144,512]{1,0:T(8,128)(2,1)S(1)} collective-permute-done((bf16[144,512]{1,0:T(8,128)(2,1)S(1)}, bf16[144,512]{1,0:T(8,128)(2,1)S(1)}, u32[]{:S(2)}, u32[]{:S(2)}) %collective-permute-start.5) | collective-permute-done | bytes 147488 | tf_op jit(solution)/shard_map/ppermute | solution.py:291
  151.0 3.4 %collective-permute-done.6.p2 = bf16[144,512]{1,0:T(8,128)(2,1)S(1)} collective-permute-done((bf16[144,512]{1,0:T(8,128)(2,1)S(1)}, bf16[144,512]{1,0:T(8,128)(2,1)S(1)}, u32[]{:S(2)}, u32[]{:S(2)}) %collective-permute-start.6) | collective-permute-done | bytes 147488 | tf_op jit(solution)/shard_map/ppermute | solution.py:291
  154.4 1.2 merge.1
  (56 shorter events, 3.4 us)
Async XLA Ops:
  0.0 143.9 %copy-start = (bf16[2,2,64]{2,1,0:T(2,128)(2,1)S(1)}, bf16[2,2,64]{2,1,0:T(2,128)(2,1)}, u32[]{:S(2)}) copy-start(bf16[2,2,64]{2,1,0:T(2,128)(2,1)} %param.15) | copy-start | bytes 1540
  0.0 12.6 %copy-start.8 = (s32[256]{0:T(256)S(1)}, s32[256]{0:T(256)}, u32[]{:S(2)}) copy-start(s32[256]{0:T(256)} %param.10) | copy-start | bytes 3076
  0.0 12.6 %copy-start.6 = (bf16[2,2,32,64]{3,2,1,0:T(8,128)(2,1)S(1)}, bf16[2,2,32,64]{3,2,1,0:T(8,128)(2,1)}, u32[]{:S(2)}) copy-start(bf16[2,2,32,64]{3,2,1,0:T(8,128)(2,1)} %param.13) | copy-start | bytes 49156
  0.0 12.7 %copy-start.9 = (s32[2]{0:T(128)S(1)}, s32[2]{0:T(128)}, u32[]{:S(2)}) copy-start(s32[2]{0:T(128)} %param.11) | copy-start | bytes 28
  0.0 12.8 %copy-start.5 = (bf16[2,2,32,512]{3,2,1,0:T(8,128)(2,1)S(1)}, bf16[2,2,32,512]{3,2,1,0:T(8,128)(2,1)}, u32[]{:S(2)}) copy-start(bf16[2,2,32,512]{3,2,1,0:T(8,128)(2,1)} %param.12) | copy-start | bytes 393220
  2.2 35.2 %all-to-all-start = ((bf16[64,48,128]{2,1,0:T(8,128)(2,1)}), bf16[64,48,128]{2,1,0:T(8,128)(2,1)S(1)}, u32[]{:S(2)}, u32[]{:S(2)}) async-start(bf16[64,48,128]{2,1,0:T(8,128)(2,1)} %bitcast.20), calls=%async_computation | async-start | bytes 1572864 | tf_op jit(solution)/shard_map/all_to_all | solution.py:257
  12.9 24.6 %collective-permute-start = (bf16[160,512]{1,0:T(8,128)(2,1)S(1)}, bf16[160,512]{1,0:T(8,128)(2,1)S(1)}, u32[]{:S(2)}, u32[]{:S(2)}) collective-permute-start(bf16[160,512]{1,0:T(8,128)(2,1)S(1)} %pad_maximum_fusion), channel_id=1, source_target_pairs={{0,0},{65,1},{130,2},{195,3},{4,4},{197,5},{134,6},{71,7},{8,8},{7... | collective-permute-start | bytes 491528 | tf_op jit(solution)/shard_map/ppermute | solution.py:244
  13.6 37.5 %copy-start.1 = (bf16[2,2,512]{2,1,0:T(2,128)(2,1)S(1)}, bf16[2,2,512]{2,1,0:T(2,128)(2,1)}, u32[]{:S(2)}) copy-start(bf16[2,2,512]{2,1,0:T(2,128)(2,1)} %new_lat_ref.1) | copy-start | bytes 12292
  13.6 15.8 %collective-permute-start.1 = (bf16[144,512]{1,0:T(8,128)(2,1)S(1)}, bf16[144,512]{1,0:T(8,128)(2,1)S(1)}, u32[]{:S(2)}, u32[]{:S(2)}) collective-permute-start(bf16[144,512]{1,0:T(8,128)(2,1)S(1)} %pad_maximum_fusion.1), channel_id=1, source_target_pairs={{1,0},{66,1},{131,2},{192,3},{5,4},{198,5},{135,6},{68,7},{9,8},{7... | collective-permute-start | bytes 442376 | tf_op jit(solution)/shard_map/ppermute | solution.py:244
  20.3 15.2 %collective-permute-start.2 = (bf16[144,512]{1,0:T(8,128)(2,1)S(1)}, bf16[144,512]{1,0:T(8,128)(2,1)S(1)}, u32[]{:S(2)}, u32[]{:S(2)}) collective-permute-start(bf16[144,512]{1,0:T(8,128)(2,1)S(1)} %pad_maximum_fusion.1), channel_id=1, source_target_pairs={{2,0},{67,1},{128,2},{193,3},{6,4},{199,5},{132,6},{69,7},{10,8},{... | collective-permute-start | bytes 442376 | tf_op jit(solution)/shard_map/ppermute | solution.py:244
  26.3 11.2 %collective-permute-start.3 = (bf16[144,512]{1,0:T(8,128)(2,1)S(1)}, bf16[144,512]{1,0:T(8,128)(2,1)S(1)}, u32[]{:S(2)}, u32[]{:S(2)}) collective-permute-start(bf16[144,512]{1,0:T(8,128)(2,1)S(1)} %pad_maximum_fusion.1), channel_id=1, source_target_pairs={{3,0},{64,1},{129,2},{194,3},{7,4},{196,5},{133,6},{70,7},{11,8},{... | collective-permute-start | bytes 442376 | tf_op jit(solution)/shard_map/ppermute | solution.py:244
  29.4 21.8 %copy-start.3 = (bf16[144,512]{1,0:T(8,128)(2,1)}, bf16[144,512]{1,0:T(8,128)(2,1)S(1)}, u32[]{:S(2)}) copy-start(bf16[144,512]{1,0:T(8,128)(2,1)S(1)} %collective-permute-done.1) | copy-start | bytes 442372
  35.4 15.8 %copy-start.4 = (bf16[144,512]{1,0:T(8,128)(2,1)}, bf16[144,512]{1,0:T(8,128)(2,1)S(1)}, u32[]{:S(2)}) copy-start(bf16[144,512]{1,0:T(8,128)(2,1)S(1)} %collective-permute-done.2) | copy-start | bytes 442372
  37.4 15.5 %copy-start.2 = (bf16[160,512]{1,0:T(8,128)(2,1)}, bf16[160,512]{1,0:T(8,128)(2,1)S(1)}, u32[]{:S(2)}) copy-start(bf16[160,512]{1,0:T(8,128)(2,1)S(1)} %collective-permute-done) | copy-start | bytes 491524
  37.4 90.9 %all-to-all-start.1 = ((bf16[64,96,512]{2,1,0:T(8,128)(2,1)}), bf16[64,96,512]{2,1,0:T(8,128)(2,1)}, u32[]{:S(2)}, u32[]{:S(2)}) async-start(bf16[64,96,512]{2,1,0:T(8,128)(2,1)} %param.8), calls=%async_computation.1 | async-start | bytes 12582912 | tf_op jit(solution)/shard_map/all_to_all | solution.py:259
  54.9 7.9 %slice-start = ((bf16[160,512]{1,0:T(8,128)(2,1)}), bf16[128,512]{1,0:T(8,128)(2,1)S(1)}, s32[]{:S(2)}) async-start(bf16[160,512]{1,0:T(8,128)(2,1)} %copy-done.2), calls=%async_computation.2 | async-start | bytes 262144 | tf_op jit(solution)/shard_map/slice | solution.py:263
  54.9 7.9 %slice-start.1 = ((bf16[144,512]{1,0:T(8,128)(2,1)}), bf16[128,512]{1,0:T(8,128)(2,1)S(1)}, s32[]{:S(2)}) async-start(bf16[144,512]{1,0:T(8,128)(2,1)} %copy-done.3), calls=%async_computation.3 | async-start | bytes 262144 | tf_op jit(solution)/shard_map/slice | solution.py:263
  54.9 7.9 %slice-start.2 = ((bf16[144,512]{1,0:T(8,128)(2,1)}), bf16[128,512]{1,0:T(8,128)(2,1)S(1)}, s32[]{:S(2)}) async-start(bf16[144,512]{1,0:T(8,128)(2,1)} %copy-done.4), calls=%async_computation.4 | async-start | bytes 262144 | tf_op jit(solution)/shard_map/slice | solution.py:263
  128.3 15.6 %copy-start.7 = (bf16[2,2,32,64]{3,2,1,0:T(8,128)(2,1)S(1)}, bf16[2,2,32,64]{3,2,1,0:T(8,128)(2,1)}, u32[]{:S(2)}) copy-start(bf16[2,2,32,64]{3,2,1,0:T(8,128)(2,1)} %param.13) | copy-start | bytes 49156
  137.5 6.7 %collective-permute-start.4 = (bf16[144,512]{1,0:T(8,128)(2,1)S(1)}, bf16[144,512]{1,0:T(8,128)(2,1)S(1)}, u32[]{:S(2)}, u32[]{:S(2)}) collective-permute-start(bf16[144,512]{1,0:T(8,128)(2,1)S(1)} %get-tuple-element.21), channel_id=1, source_target_pairs={{0,0},{1,65},{2,130},{3,195},{4,4},{5,197},{6,134},{7,71},{8,8},{9... | collective-permute-start | bytes 442376 | tf_op jit(solution)/shard_map/ppermute | solution.py:291
  138.1 12.9 %collective-permute-start.5 = (bf16[144,512]{1,0:T(8,128)(2,1)S(1)}, bf16[144,512]{1,0:T(8,128)(2,1)S(1)}, u32[]{:S(2)}, u32[]{:S(2)}) collective-permute-start(bf16[144,512]{1,0:T(8,128)(2,1)S(1)} %get-tuple-element.22), channel_id=1, source_target_pairs={{0,1},{1,66},{2,131},{3,192},{4,5},{5,198},{6,135},{7,68},{8,9},{9... | collective-permute-start | bytes 442376 | tf_op jit(solution)/shard_map/ppermute | solution.py:291
  140.8 13.7 %collective-permute-start.6 = (bf16[144,512]{1,0:T(8,128)(2,1)S(1)}, bf16[144,512]{1,0:T(8,128)(2,1)S(1)}, u32[]{:S(2)}, u32[]{:S(2)}) collective-permute-start(bf16[144,512]{1,0:T(8,128)(2,1)S(1)} %get-tuple-element.23), channel_id=1, source_target_pairs={{0,2},{1,67},{2,128},{3,193},{4,6},{5,199},{6,132},{7,69},{8,10},{... | collective-permute-start | bytes 442376 | tf_op jit(solution)/shard_map/ppermute | solution.py:291
  141.9 12.5 %collective-permute-start.7 = (bf16[144,512]{1,0:T(8,128)(2,1)S(1)}, bf16[144,512]{1,0:T(8,128)(2,1)S(1)}, u32[]{:S(2)}, u32[]{:S(2)}) collective-permute-start(bf16[144,512]{1,0:T(8,128)(2,1)S(1)} %get-tuple-element.24), channel_id=1, source_target_pairs={{0,3},{1,64},{2,129},{3,194},{4,7},{5,196},{6,133},{7,70},{8,11},{... | collective-permute-start | bytes 442376 | tf_op jit(solution)/shard_map/ppermute | solution.py:291

commit v5 on v4

--- a/solution.py
+++ b/solution.py
@@ -19,9 +19,11 @@
 SLOTS = NZ * NX * NC
 PAGE = 96
 BLOCK = 8
+SPREAD = 4
 TOKENS = BLOCK * PAGE
 ROWS = 64
 META = 16
+QCOST = 10**11
 
 
 def device_id(z, x, core, y):
@@ -67,32 +69,35 @@
     )
 
 
-def spread_kernel(rope_ref, out_ref):
-    pages = 4
-    token = lax.broadcasted_iota(jnp.int32, (pages * PAGE, pages * PAGE // 2), 0)
-    pair = lax.broadcasted_iota(jnp.int32, (pages * PAGE, pages * PAGE // 2), 1)
-    spread = (token // 2 == pair).astype(jnp.bfloat16)
-    half = (
-        lax.broadcasted_iota(jnp.int32, (pages * PAGE, 2 * ROPE), 0) % 2
-        == lax.broadcasted_iota(jnp.int32, (pages * PAGE, 2 * ROPE), 1) // ROPE
-    )
-
-    def step(i, carry):
-        pairs = jnp.concatenate([rope_ref[i * pages + k] for k in range(pages)], axis=0)
-        keys = jnp.dot(spread, pairs, preferred_element_type=jnp.float32)
-        keys = jnp.where(half, keys, 0.0).astype(jnp.bfloat16)
-        for k in range(pages):
-            out_ref[i * pages + k] = keys[k * PAGE : (k + 1) * PAGE, :]
-        return carry
-
-    lax.fori_loop(0, SLOTS // pages, step, 0)
+def query_kernel(q0, q1, q2, q3, out_ref):
+    for request in range(2):
+        for i, query in enumerate((q0, q1, q2, q3)):
+            rows = slice(i * ROWS, (i + 1) * ROWS)
+            out_ref[request, rows, :512] = query[request * ROWS : (request + 1) * ROWS, :]
+            for k in range(2):
+                rows = slice(i * ROWS + k * 32, i * ROWS + (k + 1) * 32)
+                tile = slice((2 * request + k) * 128, (2 * request + k + 1) * 128)
+                out_ref[request, rows, 512:] = query[2 * ROWS : 2 * ROWS + 32, tile]
 
 
 def attend_kernel(
-    order_ref, valid_ref, count_ref, lat_ref, keys_ref, query_ref,
+    order_ref, valid_ref, count_ref, lat_ref, rope_ref, query_ref,
     o0, o1, o2, o3, score_ref, acc_ref
 ):
     outs = (o0, o1, o2, o3)
+    token = lax.broadcasted_iota(jnp.int32, (SPREAD * PAGE, SPREAD * PAGE // 2), 0)
+    pair = lax.broadcasted_iota(jnp.int32, (SPREAD * PAGE, SPREAD * PAGE // 2), 1)
+    spread = (token // 2 == pair).astype(jnp.bfloat16)
+    half = (
+        lax.broadcasted_iota(jnp.int32, (SPREAD * PAGE, 2 * ROPE), 0) % 2
+        == lax.broadcasted_iota(jnp.int32, (SPREAD * PAGE, 2 * ROPE), 1) // ROPE
+    )
+
+    def rope_keys(places):
+        pairs = jnp.concatenate([rope_ref[order_ref[p]] for p in places], axis=0)
+        keys = jnp.dot(spread, pairs, preferred_element_type=jnp.float32)
+        return jnp.where(half, keys, 0.0).astype(jnp.bfloat16)
+
     meta_lane = lax.broadcasted_iota(jnp.int32, (4 * ROWS, 128), 1)
     meta = jnp.zeros((4 * ROWS, 128), jnp.float32)
     for request in range(2):
@@ -111,8 +116,8 @@
 
         def score_blocks(size, block, maxima):
             places = slots(block, size)
-            rope_keys = jnp.concatenate([keys_ref[order_ref[p]] for p in places], axis=0)
-            keys = jnp.concatenate([latents(places), rope_keys], axis=1)
+            ropes = [rope_keys(places[i : i + SPREAD]) for i in range(0, len(places), SPREAD)]
+            keys = jnp.concatenate([latents(places), jnp.concatenate(ropes, axis=0)], axis=1)
             lane = lax.broadcasted_iota(jnp.int32, (1, size * TOKENS), 1)
             limit = jnp.zeros((1, size * TOKENS), jnp.int32)
             for i, p in enumerate(places):
@@ -236,9 +241,10 @@
     length = jnp.concatenate([lengths // 128, lengths % 128]).astype(jnp.bfloat16)
     row = jnp.pad(jnp.concatenate([place, length]), (0, 512 - 260))
     row = jnp.broadcast_to(row[None, :], (META, 512))
-    query = jnp.concatenate(
-        [q_latent.reshape(2 * ROWS, 512), q_rope.reshape(META, 512)], axis=0
-    )
+    query_rope = q_rope.reshape(2 * ROWS, ROPE)
+    twice = jnp.concatenate([query_rope, query_rope], axis=1).reshape(4, 32, 2 * ROPE)
+    twice = jnp.concatenate([twice[k] for k in range(4)], axis=1)
+    query = jnp.concatenate([q_latent.reshape(2 * ROWS, 512), twice], axis=0)
     first = jnp.concatenate([query, row], axis=0)
     came = [
         lax.ppermute(query if d else first, AXES, [(t, s) for s, t in home_pairs(d)])
@@ -254,24 +260,20 @@
         axis_index_groups=page_groups(),
         tiled=True,
     )
-    rope = exchange(rope_pages.reshape(SLOTS, PAGE // 2, 2 * ROPE))
-    latent_pages, rope, came = lax.optimization_barrier((latent_pages, rope, came))
     lat = exchange(latent_pages)
-    queries = []
-    for part in came:
-        part_rope = part[2 * ROWS : 2 * ROWS + META].reshape(2, ROWS, ROPE)
-        part_lat = part[: 2 * ROWS].reshape(2, ROWS, 512)
-        queries.append(jnp.concatenate([part_lat, part_rope, part_rope], axis=2))
-    queries = jnp.concatenate(queries, axis=1)
-    keys = pl.pallas_call(
-        spread_kernel,
-        out_shape=jax.ShapeDtypeStruct((SLOTS, PAGE, 2 * ROPE), jnp.bfloat16),
-        in_specs=[whole],
+    ropes = rope_pages.reshape(SLOTS, PAGE // 2, 2 * ROPE)
+    lat, ropes = lax.optimization_barrier((lat, ropes))
+    rope = exchange(ropes)
+    queries = pl.pallas_call(
+        query_kernel,
+        out_shape=jax.ShapeDtypeStruct((2, 4 * ROWS, 512 + 2 * ROPE), jnp.bfloat16),
+        in_specs=[whole] * 4,
         out_specs=whole,
+        cost_estimate=pl.CostEstimate(flops=QCOST, bytes_accessed=2 << 20, transcendentals=0),
         compiler_params=pltpu.CompilerParams(vmem_limit_bytes=8 * 1024 * 1024),
-        name="spread",
-    )(rope)
-    table = page_table(came[0][2 * ROWS + META].astype(jnp.int32), pair)
+        name="queries",
+    )(*came)
+    table = page_table(came[0][2 * ROWS + 32].astype(jnp.int32), pair)
     partial = jax.ShapeDtypeStruct((2 * ROWS + META, 512), jnp.bfloat16)
     parts = pl.pallas_call(
         attend_kernel,
@@ -282,12 +284,12 @@
             pltpu.VMEM((SLOTS // BLOCK, 4 * ROWS, TOKENS), jnp.float32),
             pltpu.VMEM((4 * ROWS, 512), jnp.float32),
         ],
-        compiler_params=pltpu.CompilerParams(vmem_limit_bytes=32 * 1024 * 1024),
+        compiler_params=pltpu.CompilerParams(vmem_limit_bytes=18 * 1024 * 1024),
         cost_estimate=pl.CostEstimate(
             flops=4 * ROWS * 6144 * 1152 * 2, bytes_accessed=8 << 20, transcendentals=1 << 20
         ),
         name="attend",
-    )(*table, lat, keys, queries)
+    )(*table, lat, rope, queries)
     home = [lax.ppermute(part, AXES, home_pairs(d)) for d, part in enumerate(parts)]
     out = pl.pallas_call(
         merge_kernel,

time: 157 us -> 152 us (0.968)
  waiting for transfers between devices: 84.6 us -> 89.1 us
  Pallas kernels: 13.7 us -> 10.6 us
  local copies, waits for them, and re-layouts: 5.64 us -> 2.64 us
  starting transfers between devices: 44.9 us -> 42.1 us
    ppermute x4, waiting for transfers between devices: 9.85 us -> 0.01 us  [on_device(): lax.ppermute(query if d else first, AXES, [(t, s) for s, t in home_pairs(...]
    all_to_all x1, waiting for transfers between devices: 0.01 us -> 8.66 us  [on_device(): rope = exchange(ropes)]
    ppermute x4, starting transfers between devices: 6.44 us -> 13.2 us  [on_device(): lax.ppermute(part, AXES, home_pairs(d))]
    all_to_all x1, waiting for transfers between devices: 64.5 us -> 70.5 us  [on_device(): lat = exchange(latent_pages)]
    ppermute x4, starting transfers between devices: 14.7 us -> 9.4 us  [on_device(): lax.ppermute(query if d else first, AXES, [(t, s) for s, t in home_pairs(...]
    pallas_call x1, Pallas kernels: 3.33 us -> 0.06 us  [on_device(): pl.pallas_call(query_kernel, out_shape=jax.ShapeDtypeStruct((2, 4 * ROWS,...]
    all_to_all x1, starting transfers between devices: 13.5 us -> 10.7 us  [on_device(): lat = exchange(latent_pages)]
  transfers between devices with their start and end apart: 10 -> 10, of which waited for: 6 -> 4; matrix products, arithmetic and copies ran while one was open for 5% -> 4% of each run, Pallas kernels for 2% -> 0%
where the time goes in v5:
time: 152 us; the launch traced here: 150 us
  waiting for transfers between devices  89.1 us (59%)
  starting transfers between devices  42.1 us (28%)
  Pallas kernels  10.6 us (7%)
  between operations  2.84 us (2%)
  other arithmetic  2.65 us (2%)
  local copies, waits for them, and re-layouts  2.64 us (2%)
    all_to_all x1, waiting for transfers between devices, on_device(): lat = exchange(latent_pages)  70.5 us
    ppermute x4, starting transfers between devices, on_device(): lax.ppermute(part, AXES, home_pairs(d))  13.2 us
    all_to_all x1, starting transfers between devices, on_device(): lat = exchange(latent_pages)  10.7 us
    ppermute x4, waiting for transfers between devices, on_device(): lax.ppermute(part, AXES, home_pairs(d))  10 us
    ppermute x4, starting transfers between devices, on_device(): lax.ppermute(query if d else first, AXES, [(t, s) for s, t in home_pairs(...  9.4 us
    pallas_call x1, Pallas kernels, on_device(): pl.pallas_call(attend_kernel, out_shape=[partial] * 4, in_specs=[scalars]...  9.34 us
    all_to_all x1, starting transfers between devices, on_device(): rope = exchange(ropes)  8.82 us
    all_to_all x1, waiting for transfers between devices, on_device(): rope = exchange(ropes)  8.66 us
  transfers between devices with their start and end apart: 10, of which 4 were waited for; matrix products, arithmetic and copies ran while one was open for 4% of the time, Pallas kernels for 0%

profile of v5, /device:TPU:1, one launch (start us, length us, event | category | flops | bytes accessed | tf_op | source)
XLA Modules:
  0.0 150.2 jit_solution(6536884550409535110)
XLA Ops:
  0.1 10.7 %all-to-all-start = ((bf16[64,96,512]{2,1,0:T(8,128)(2,1)}), bf16[64,96,512]{2,1,0:T(8,128)(2,1)}, u32[]{:S(2)}, u32[]{:S(2)}) async-start(bf16[64,96,512]{2,1,0:T(8,128)(2,1)} %param.8), calls=%async_computation | async-start | bytes 12582912 | tf_op jit(solution)/shard_map/all_to_all | solution.py:263
  10.8 5.5 %collective-permute-start.1 = (bf16[160,512]{1,0:T(8,128)(2,1)S(1)}, bf16[160,512]{1,0:T(8,128)(2,1)S(1)}, u32[]{:S(2)}, u32[]{:S(2)}) collective-permute-start(bf16[160,512]{1,0:T(8,128)(2,1)S(1)} %maximum_maximum_fusion), channel_id=1, source_target_pairs={{1,0},{66,1},{131,2},{192,3},{5,4},{198,5},{135,6},{68,7},{9,8},{7... | collective-permute-start | bytes 491528 | tf_op jit(solution)/shard_map/ppermute | solution.py:250
  16.3 2.6 %collective-permute-start.2 = (bf16[160,512]{1,0:T(8,128)(2,1)S(1)}, bf16[160,512]{1,0:T(8,128)(2,1)S(1)}, u32[]{:S(2)}, u32[]{:S(2)}) collective-permute-start(bf16[160,512]{1,0:T(8,128)(2,1)S(1)} %maximum_maximum_fusion), channel_id=1, source_target_pairs={{2,0},{67,1},{128,2},{193,3},{6,4},{199,5},{132,6},{69,7},{10,8},{... | collective-permute-start | bytes 491528 | tf_op jit(solution)/shard_map/ppermute | solution.py:250
  18.9 0.6 collective-permute-start.3
  19.7 0.7 collective-permute-start
  20.4 0.2 fusion.7
  20.7 1.0 copy.14
  21.7 70.5 %all-to-all-done.lat_ref = bf16[64,96,512]{2,1,0:T(8,128)(2,1)} async-done(((bf16[64,96,512]{2,1,0:T(8,128)(2,1)}), bf16[64,96,512]{2,1,0:T(8,128)(2,1)}, u32[]{:S(2)}, u32[]{:S(2)}) %all-to-all-start) | async-done | bytes 6291488 | tf_op jit(solution)/shard_map/all_to_all | solution.py:263
  92.2 8.8 %all-to-all-start.1 = ((bf16[64,48,128]{2,1,0:T(8,128)(2,1)}), bf16[64,48,128]{2,1,0:T(8,128)(2,1)S(1)}, u32[]{:S(2)}, u32[]{:S(2)}) async-start(bf16[64,48,128]{2,1,0:T(8,128)(2,1)} %bitcast.17), calls=%async_computation.1 | async-start | bytes 1572864 | tf_op jit(solution)/shard_map/all_to_all | solution.py:266
  101.1 0.7 fusion.36
  103.1 0.8 gather_fusion
  105.2 0.7 fusion.26
  105.9 1.4 pad_add_fusion.count_ref
  107.3 0.2 convert_reduce_fusion
  107.5 8.7 %all-to-all-done.1.rope_ref = bf16[64,48,128]{2,1,0:T(8,128)(2,1)S(1)} async-done(((bf16[64,48,128]{2,1,0:T(8,128)(2,1)}), bf16[64,48,128]{2,1,0:T(8,128)(2,1)S(1)}, u32[]{:S(2)}, u32[]{:S(2)}) %all-to-all-start.1) | async-done | bytes 786464 | tf_op jit(solution)/shard_map/all_to_all | solution.py:266
  116.2 9.3 %attend.1 = (bf16[144,512]{1,0:T(8,128)(2,1)S(1)}, bf16[144,512]{1,0:T(8,128)(2,1)S(1)}, bf16[144,512]{1,0:T(8,128)(2,1)S(1)}, bf16[144,512]{1,0:T(8,128)(2,1)S(1)}) custom-call(s32[64]{0:T(128)S(1)} %get-tuple-element.20.order_ref, s32[64]{0:T(128)S(1)} %get-tuple-element.19.valid_ref, s32[2]{0:T(128)S(1)} %pad_add_fusion.count_ref, ...), custom_call_target="tpu_custom_call" | custom-call | flops 3623878656 | bytes 8388608 | tf_op jit(solution)/shard_map/attend/pallas_call | solution.py:278
  125.5 0.7 collective-permute-start.4
  126.2 9.8 %collective-permute-start.5 = (bf16[144,512]{1,0:T(8,128)(2,1)S(1)}, bf16[144,512]{1,0:T(8,128)(2,1)S(1)}, u32[]{:S(2)}, u32[]{:S(2)}) collective-permute-start(bf16[144,512]{1,0:T(8,128)(2,1)S(1)} %get-tuple-element.14), channel_id=1, source_target_pairs={{0,1},{1,66},{2,131},{3,192},{4,5},{5,198},{6,135},{7,68},{8,9},{9... | collective-permute-start | bytes 442376 | tf_op jit(solution)/shard_map/ppermute | solution.py:293
  136.0 2.6 %collective-permute-start.6 = (bf16[144,512]{1,0:T(8,128)(2,1)S(1)}, bf16[144,512]{1,0:T(8,128)(2,1)S(1)}, u32[]{:S(2)}, u32[]{:S(2)}) collective-permute-start(bf16[144,512]{1,0:T(8,128)(2,1)S(1)} %get-tuple-element.15), channel_id=1, source_target_pairs={{0,2},{1,67},{2,128},{3,193},{4,6},{5,199},{6,132},{7,69},{8,10},{... | collective-permute-start | bytes 442376 | tf_op jit(solution)/shard_map/ppermute | solution.py:293
  138.8 0.1 fusion.1
  138.9 0.1 copy.11
  139.1 9.1 %collective-permute-done.6.p2 = bf16[144,512]{1,0:T(8,128)(2,1)S(1)} collective-permute-done((bf16[144,512]{1,0:T(8,128)(2,1)S(1)}, bf16[144,512]{1,0:T(8,128)(2,1)S(1)}, u32[]{:S(2)}, u32[]{:S(2)}) %collective-permute-start.6) | collective-permute-done | bytes 147488 | tf_op jit(solution)/shard_map/ppermute | solution.py:293
  148.1 0.9 collective-permute-done.7.p3
  149.1 1.2 merge.1
  (34 shorter events, 0.6 us)
Async XLA Ops:
  0.0 138.8 %copy-start = (bf16[2,2,64]{2,1,0:T(2,128)(2,1)S(1)}, bf16[2,2,64]{2,1,0:T(2,128)(2,1)}, u32[]{:S(2)}) copy-start(bf16[2,2,64]{2,1,0:T(2,128)(2,1)} %param.15) | copy-start | bytes 1540
  0.0 10.7 %copy-start.4 = (bf16[2,2,32,64]{3,2,1,0:T(8,128)(2,1)S(1)}, bf16[2,2,32,64]{3,2,1,0:T(8,128)(2,1)}, u32[]{:S(2)}) copy-start(bf16[2,2,32,64]{3,2,1,0:T(8,128)(2,1)} %param.13) | copy-start | bytes 49156
  0.0 10.8 %copy-start.3 = (bf16[2,2,32,512]{3,2,1,0:T(8,128)(2,1)S(1)}, bf16[2,2,32,512]{3,2,1,0:T(8,128)(2,1)}, u32[]{:S(2)}) copy-start(bf16[2,2,32,512]{3,2,1,0:T(8,128)(2,1)} %param.12) | copy-start | bytes 393220
  0.0 19.6 %copy-start.5 = (s32[256]{0:T(256)S(1)}, s32[256]{0:T(256)}, u32[]{:S(2)}) copy-start(s32[256]{0:T(256)} %param.10) | copy-start | bytes 3076
  0.0 19.6 %copy-start.6 = (s32[2]{0:T(128)S(1)}, s32[2]{0:T(128)}, u32[]{:S(2)}) copy-start(s32[2]{0:T(128)} %param.11) | copy-start | bytes 28
  0.0 20.4 %copy-start.1 = (bf16[2,2,512]{2,1,0:T(2,128)(2,1)S(1)}, bf16[2,2,512]{2,1,0:T(2,128)(2,1)}, u32[]{:S(2)}) copy-start(bf16[2,2,512]{2,1,0:T(2,128)(2,1)} %new_lat_ref.1) | copy-start | bytes 12292
  0.0 20.6 %copy-start.2 = (bf16[64,6144]{1,0:T(8,128)(2,1)S(1)}, bf16[64,6144]{1,0:T(8,128)(2,1)}, u32[]{:S(2)}) copy-start(bf16[64,6144]{1,0:T(8,128)(2,1)} %param.9) | copy-start | bytes 2359300
  0.1 92.1 %all-to-all-start = ((bf16[64,96,512]{2,1,0:T(8,128)(2,1)}), bf16[64,96,512]{2,1,0:T(8,128)(2,1)}, u32[]{:S(2)}, u32[]{:S(2)}) async-start(bf16[64,96,512]{2,1,0:T(8,128)(2,1)} %param.8), calls=%async_computation | async-start | bytes 12582912 | tf_op jit(solution)/shard_map/all_to_all | solution.py:263
  10.8 90.2 %collective-permute-start.1 = (bf16[160,512]{1,0:T(8,128)(2,1)S(1)}, bf16[160,512]{1,0:T(8,128)(2,1)S(1)}, u32[]{:S(2)}, u32[]{:S(2)}) collective-permute-start(bf16[160,512]{1,0:T(8,128)(2,1)S(1)} %maximum_maximum_fusion), channel_id=1, source_target_pairs={{1,0},{66,1},{131,2},{192,3},{5,4},{198,5},{135,6},{68,7},{9,8},{7... | collective-permute-start | bytes 491528 | tf_op jit(solution)/shard_map/ppermute | solution.py:250
  16.3 84.7 %collective-permute-start.2 = (bf16[160,512]{1,0:T(8,128)(2,1)S(1)}, bf16[160,512]{1,0:T(8,128)(2,1)S(1)}, u32[]{:S(2)}, u32[]{:S(2)}) collective-permute-start(bf16[160,512]{1,0:T(8,128)(2,1)S(1)} %maximum_maximum_fusion), channel_id=1, source_target_pairs={{2,0},{67,1},{128,2},{193,3},{6,4},{199,5},{132,6},{69,7},{10,8},{... | collective-permute-start | bytes 491528 | tf_op jit(solution)/shard_map/ppermute | solution.py:250
  18.9 82.1 %collective-permute-start.3 = (bf16[160,512]{1,0:T(8,128)(2,1)S(1)}, bf16[160,512]{1,0:T(8,128)(2,1)S(1)}, u32[]{:S(2)}, u32[]{:S(2)}) collective-permute-start(bf16[160,512]{1,0:T(8,128)(2,1)S(1)} %maximum_maximum_fusion), channel_id=1, source_target_pairs={{3,0},{64,1},{129,2},{194,3},{7,4},{196,5},{133,6},{70,7},{11,8},{... | collective-permute-start | bytes 491528 | tf_op jit(solution)/shard_map/ppermute | solution.py:250
  19.7 81.3 %collective-permute-start = (bf16[176,512]{1,0:T(8,128)(2,1)S(1)}, bf16[176,512]{1,0:T(8,128)(2,1)S(1)}, u32[]{:S(2)}, u32[]{:S(2)}) collective-permute-start(bf16[176,512]{1,0:T(8,128)(2,1)S(1)} %pad_maximum_fusion), channel_id=1, source_target_pairs={{0,0},{65,1},{130,2},{195,3},{4,4},{197,5},{134,6},{71,7},{8,8},{7... | collective-permute-start | bytes 540680 | tf_op jit(solution)/shard_map/ppermute | solution.py:250
  92.2 24.0 %all-to-all-start.1 = ((bf16[64,48,128]{2,1,0:T(8,128)(2,1)}), bf16[64,48,128]{2,1,0:T(8,128)(2,1)S(1)}, u32[]{:S(2)}, u32[]{:S(2)}) async-start(bf16[64,48,128]{2,1,0:T(8,128)(2,1)} %bitcast.17), calls=%async_computation.1 | async-start | bytes 1572864 | tf_op jit(solution)/shard_map/all_to_all | solution.py:266
  125.5 13.5 %collective-permute-start.4 = (bf16[144,512]{1,0:T(8,128)(2,1)S(1)}, bf16[144,512]{1,0:T(8,128)(2,1)S(1)}, u32[]{:S(2)}, u32[]{:S(2)}) collective-permute-start(bf16[144,512]{1,0:T(8,128)(2,1)S(1)} %get-tuple-element.13), channel_id=1, source_target_pairs={{0,0},{1,65},{2,130},{3,195},{4,4},{5,197},{6,134},{7,71},{8,8},{9... | collective-permute-start | bytes 442376 | tf_op jit(solution)/shard_map/ppermute | solution.py:293
  126.2 12.8 %collective-permute-start.5 = (bf16[144,512]{1,0:T(8,128)(2,1)S(1)}, bf16[144,512]{1,0:T(8,128)(2,1)S(1)}, u32[]{:S(2)}, u32[]{:S(2)}) collective-permute-start(bf16[144,512]{1,0:T(8,128)(2,1)S(1)} %get-tuple-element.14), channel_id=1, source_target_pairs={{0,1},{1,66},{2,131},{3,192},{4,5},{5,198},{6,135},{7,68},{8,9},{9... | collective-permute-start | bytes 442376 | tf_op jit(solution)/shard_map/ppermute | solution.py:293
  136.0 12.1 %collective-permute-start.6 = (bf16[144,512]{1,0:T(8,128)(2,1)S(1)}, bf16[144,512]{1,0:T(8,128)(2,1)S(1)}, u32[]{:S(2)}, u32[]{:S(2)}) collective-permute-start(bf16[144,512]{1,0:T(8,128)(2,1)S(1)} %get-tuple-element.15), channel_id=1, source_target_pairs={{0,2},{1,67},{2,128},{3,193},{4,6},{5,199},{6,132},{7,69},{8,10},{... | collective-permute-start | bytes 442376 | tf_op jit(solution)/shard_map/ppermute | solution.py:293
  138.7 10.4 %collective-permute-start.7 = (bf16[144,512]{1,0:T(8,128)(2,1)S(1)}, bf16[144,512]{1,0:T(8,128)(2,1)S(1)}, u32[]{:S(2)}, u32[]{:S(2)}) collective-permute-start(bf16[144,512]{1,0:T(8,128)(2,1)S(1)} %get-tuple-element.16), channel_id=1, source_target_pairs={{0,3},{1,64},{2,129},{3,194},{4,7},{5,196},{6,133},{7,70},{8,11},{... | collective-permute-start | bytes 442376 | tf_op jit(solution)/shard_map/ppermute | solution.py:293

commit v6 on v5

--- a/solution.py
+++ b/solution.py
@@ -70,14 +70,19 @@
 
 
 def query_kernel(q0, q1, q2, q3, out_ref):
+    first = lax.broadcasted_iota(jnp.int32, (META, 2 * ROPE), 1) < ROPE
     for request in range(2):
         for i, query in enumerate((q0, q1, q2, q3)):
             rows = slice(i * ROWS, (i + 1) * ROWS)
             out_ref[request, rows, :512] = query[request * ROWS : (request + 1) * ROWS, :]
             for k in range(2):
-                rows = slice(i * ROWS + k * 32, i * ROWS + (k + 1) * 32)
                 tile = slice((2 * request + k) * 128, (2 * request + k + 1) * 128)
-                out_ref[request, rows, 512:] = query[2 * ROWS : 2 * ROWS + 32, tile]
+                both = query[2 * ROWS : 2 * ROWS + META, tile].astype(jnp.float32)
+                swapped = pltpu.roll(both, ROPE, 1)
+                pair = (jnp.where(first, both, swapped), jnp.where(first, swapped, both))
+                for h, part in enumerate(pair):
+                    row = i * ROWS + k * 32 + h * META
+                    out_ref[request, row : row + META, 512:] = part.astype(jnp.bfloat16)
 
 
 def attend_kernel(
@@ -241,10 +246,8 @@
     length = jnp.concatenate([lengths // 128, lengths % 128]).astype(jnp.bfloat16)
     row = jnp.pad(jnp.concatenate([place, length]), (0, 512 - 260))
     row = jnp.broadcast_to(row[None, :], (META, 512))
-    query_rope = q_rope.reshape(2 * ROWS, ROPE)
-    twice = jnp.concatenate([query_rope, query_rope], axis=1).reshape(4, 32, 2 * ROPE)
-    twice = jnp.concatenate([twice[k] for k in range(4)], axis=1)
-    query = jnp.concatenate([q_latent.reshape(2 * ROWS, 512), twice], axis=0)
+    rotary = q_rope.reshape(4, 2, META, ROPE).transpose(2, 0, 1, 3).reshape(META, 512)
+    query = jnp.concatenate([q_latent.reshape(2 * ROWS, 512), rotary], axis=0)
     first = jnp.concatenate([query, row], axis=0)
     came = [
         lax.ppermute(query if d else first, AXES, [(t, s) for s, t in home_pairs(d)])
@@ -273,7 +276,7 @@
         compiler_params=pltpu.CompilerParams(vmem_limit_bytes=8 * 1024 * 1024),
         name="queries",
     )(*came)
-    table = page_table(came[0][2 * ROWS + 32].astype(jnp.int32), pair)
+    table = page_table(came[0][2 * ROWS + META].astype(jnp.int32), pair)
     partial = jax.ShapeDtypeStruct((2 * ROWS + META, 512), jnp.bfloat16)
     parts = pl.pallas_call(
         attend_kernel,

time: 152 us -> 151 us (level)
  starting transfers between devices: 42.1 us -> 44.7 us
    ppermute x4, starting transfers between devices: 13.2 us -> 15.8 us  [on_device(): lax.ppermute(part, AXES, home_pairs(d))]
where the time goes in v6:
time: 151 us
  waiting for transfers between devices  88 us (58%)
  starting transfers between devices  44.7 us (30%)
  Pallas kernels  9.59 us (6%)
  between operations  2.77 us (2%)
  local copies, waits for them, and re-layouts  2.72 us (2%)
  other arithmetic  2.48 us (2%)
    all_to_all x1, waiting for transfers between devices, on_device(): lat = exchange(latent_pages)  69.7 us
    ppermute x4, starting transfers between devices, on_device(): lax.ppermute(part, AXES, home_pairs(d))  15.8 us
    all_to_all x1, starting transfers between devices, on_device(): lat = exchange(latent_pages)  10.7 us
    ppermute x4, waiting for transfers between devices, on_device(): lax.ppermute(part, AXES, home_pairs(d))  9.51 us
    ppermute x4, starting transfers between devices, on_device(): lax.ppermute(query if d else first, AXES, [(t, s) for s, t in home_pairs(...  9.4 us
    all_to_all x1, starting transfers between devices, on_device(): rope = exchange(ropes)  8.79 us
    all_to_all x1, waiting for transfers between devices, on_device(): rope = exchange(ropes)  8.77 us
    pallas_call x1, Pallas kernels, on_device(): pl.pallas_call(attend_kernel, out_shape=[partial] * 4, in_specs=[scalars]...  8.29 us
  transfers between devices with their start and end apart: 10, of which 4 were waited for; matrix products, arithmetic and copies ran while one was open for 4% of the time, Pallas kernels for 0%

profile of v6, /device:TPU:1, one launch (start us, length us, event | category | flops | bytes accessed | tf_op | source)
XLA Modules:
  0.0 150.5 jit_solution(13130882844789603107)
XLA Ops:
  0.1 10.7 %all-to-all-start = ((bf16[64,96,512]{2,1,0:T(8,128)(2,1)}), bf16[64,96,512]{2,1,0:T(8,128)(2,1)}, u32[]{:S(2)}, u32[]{:S(2)}) async-start(bf16[64,96,512]{2,1,0:T(8,128)(2,1)} %param.8), calls=%async_computation | async-start | bytes 12582912 | tf_op jit(solution)/shard_map/all_to_all | solution.py:266
  10.9 5.5 %collective-permute-start.1 = (bf16[144,512]{1,0:T(8,128)(2,1)S(1)}, bf16[144,512]{1,0:T(8,128)(2,1)S(1)}, u32[]{:S(2)}, u32[]{:S(2)}) collective-permute-start(bf16[144,512]{1,0:T(8,128)(2,1)S(1)} %pad_maximum_fusion.1), channel_id=1, source_target_pairs={{1,0},{66,1},{131,2},{192,3},{5,4},{198,5},{135,6},{68,7},{9,8},{7... | collective-permute-start | bytes 442376 | tf_op jit(solution)/shard_map/ppermute | solution.py:253
  16.3 2.6 %collective-permute-start.2 = (bf16[144,512]{1,0:T(8,128)(2,1)S(1)}, bf16[144,512]{1,0:T(8,128)(2,1)S(1)}, u32[]{:S(2)}, u32[]{:S(2)}) collective-permute-start(bf16[144,512]{1,0:T(8,128)(2,1)S(1)} %pad_maximum_fusion.1), channel_id=1, source_target_pairs={{2,0},{67,1},{128,2},{193,3},{6,4},{199,5},{132,6},{69,7},{10,8},{... | collective-permute-start | bytes 442376 | tf_op jit(solution)/shard_map/ppermute | solution.py:253
  19.0 0.6 collective-permute-start.3
  19.7 0.7 collective-permute-start
  20.5 0.2 fusion.4
  20.7 1.0 copy.17
  21.8 69.7 %all-to-all-done.lat_ref = bf16[64,96,512]{2,1,0:T(8,128)(2,1)} async-done(((bf16[64,96,512]{2,1,0:T(8,128)(2,1)}), bf16[64,96,512]{2,1,0:T(8,128)(2,1)}, u32[]{:S(2)}, u32[]{:S(2)}) %all-to-all-start) | async-done | bytes 6291488 | tf_op jit(solution)/shard_map/all_to_all | solution.py:266
  91.4 8.8 %all-to-all-start.1 = ((bf16[64,48,128]{2,1,0:T(8,128)(2,1)}), bf16[64,48,128]{2,1,0:T(8,128)(2,1)S(1)}, u32[]{:S(2)}, u32[]{:S(2)}) async-start(bf16[64,48,128]{2,1,0:T(8,128)(2,1)} %bitcast.18), calls=%async_computation.1 | async-start | bytes 1572864 | tf_op jit(solution)/shard_map/all_to_all | solution.py:269
  100.4 0.6 fusion.33
  102.3 0.8 gather_fusion
  104.3 0.7 fusion.23
  105.0 1.3 pad_add_fusion.count_ref
  106.3 0.2 convert_reduce_fusion
  106.6 8.8 %all-to-all-done.1.rope_ref = bf16[64,48,128]{2,1,0:T(8,128)(2,1)S(1)} async-done(((bf16[64,48,128]{2,1,0:T(8,128)(2,1)}), bf16[64,48,128]{2,1,0:T(8,128)(2,1)S(1)}, u32[]{:S(2)}, u32[]{:S(2)}) %all-to-all-start.1) | async-done | bytes 786464 | tf_op jit(solution)/shard_map/all_to_all | solution.py:269
  115.4 8.3 %attend.1 = (bf16[144,512]{1,0:T(8,128)(2,1)S(1)}, bf16[144,512]{1,0:T(8,128)(2,1)S(1)}, bf16[144,512]{1,0:T(8,128)(2,1)S(1)}, bf16[144,512]{1,0:T(8,128)(2,1)S(1)}) custom-call(s32[64]{0:T(128)S(1)} %get-tuple-element.20.order_ref, s32[64]{0:T(128)S(1)} %get-tuple-element.19.valid_ref, s32[2]{0:T(128)S(1)} %pad_add_fusion.count_ref, ...), custom_call_target="tpu_custom_call" | custom-call | flops 3623878656 | bytes 8388608 | tf_op jit(solution)/shard_map/attend/pallas_call | solution.py:281
  123.7 0.7 collective-permute-start.4
  124.4 8.2 %collective-permute-start.5 = (bf16[144,512]{1,0:T(8,128)(2,1)S(1)}, bf16[144,512]{1,0:T(8,128)(2,1)S(1)}, u32[]{:S(2)}, u32[]{:S(2)}) collective-permute-start(bf16[144,512]{1,0:T(8,128)(2,1)S(1)} %get-tuple-element.14), channel_id=1, source_target_pairs={{0,1},{1,66},{2,131},{3,192},{4,5},{5,198},{6,135},{7,68},{8,9},{9... | collective-permute-start | bytes 442376 | tf_op jit(solution)/shard_map/ppermute | solution.py:296
  132.5 7.0 %collective-permute-start.6 = (bf16[144,512]{1,0:T(8,128)(2,1)S(1)}, bf16[144,512]{1,0:T(8,128)(2,1)S(1)}, u32[]{:S(2)}, u32[]{:S(2)}) collective-permute-start(bf16[144,512]{1,0:T(8,128)(2,1)S(1)} %get-tuple-element.15), channel_id=1, source_target_pairs={{0,2},{1,67},{2,128},{3,193},{4,6},{5,199},{6,132},{7,69},{8,10},{... | collective-permute-start | bytes 442376 | tf_op jit(solution)/shard_map/ppermute | solution.py:296
  139.5 0.1 fusion.1
  139.7 0.1 copy.14
  139.8 5.1 %collective-permute-done.6.p2 = bf16[144,512]{1,0:T(8,128)(2,1)S(1)} collective-permute-done((bf16[144,512]{1,0:T(8,128)(2,1)S(1)}, bf16[144,512]{1,0:T(8,128)(2,1)S(1)}, u32[]{:S(2)}, u32[]{:S(2)}) %collective-permute-start.6) | collective-permute-done | bytes 147488 | tf_op jit(solution)/shard_map/ppermute | solution.py:296
  144.9 4.4 %collective-permute-done.7.p3 = bf16[144,512]{1,0:T(8,128)(2,1)S(1)} collective-permute-done((bf16[144,512]{1,0:T(8,128)(2,1)S(1)}, bf16[144,512]{1,0:T(8,128)(2,1)S(1)}, u32[]{:S(2)}, u32[]{:S(2)}) %collective-permute-start.7) | collective-permute-done | bytes 147488 | tf_op jit(solution)/shard_map/ppermute | solution.py:296
  149.3 1.2 merge.1
  (35 shorter events, 0.6 us)
Async XLA Ops:
  0.0 139.5 %copy-start = (bf16[2,2,64]{2,1,0:T(2,128)(2,1)S(1)}, bf16[2,2,64]{2,1,0:T(2,128)(2,1)}, u32[]{:S(2)}) copy-start(bf16[2,2,64]{2,1,0:T(2,128)(2,1)} %param.15) | copy-start | bytes 1540
  0.0 10.7 %copy-start.4 = (bf16[2,2,32,64]{3,2,1,0:T(8,128)(2,1)S(1)}, bf16[2,2,32,64]{3,2,1,0:T(8,128)(2,1)}, u32[]{:S(2)}) copy-start(bf16[2,2,32,64]{3,2,1,0:T(8,128)(2,1)} %param.13) | copy-start | bytes 49156
  0.0 10.9 %copy-start.3 = (bf16[2,2,32,512]{3,2,1,0:T(8,128)(2,1)S(1)}, bf16[2,2,32,512]{3,2,1,0:T(8,128)(2,1)}, u32[]{:S(2)}) copy-start(bf16[2,2,32,512]{3,2,1,0:T(8,128)(2,1)} %param.12) | copy-start | bytes 393220
  0.0 19.6 %copy-start.5 = (s32[256]{0:T(256)S(1)}, s32[256]{0:T(256)}, u32[]{:S(2)}) copy-start(s32[256]{0:T(256)} %param.10) | copy-start | bytes 3076
  0.0 19.6 %copy-start.6 = (s32[2]{0:T(128)S(1)}, s32[2]{0:T(128)}, u32[]{:S(2)}) copy-start(s32[2]{0:T(128)} %param.11) | copy-start | bytes 28
  0.0 20.4 %copy-start.1 = (bf16[2,2,512]{2,1,0:T(2,128)(2,1)S(1)}, bf16[2,2,512]{2,1,0:T(2,128)(2,1)}, u32[]{:S(2)}) copy-start(bf16[2,2,512]{2,1,0:T(2,128)(2,1)} %new_lat_ref.1) | copy-start | bytes 12292
  0.0 20.7 %copy-start.2 = (bf16[64,6144]{1,0:T(8,128)(2,1)S(1)}, bf16[64,6144]{1,0:T(8,128)(2,1)}, u32[]{:S(2)}) copy-start(bf16[64,6144]{1,0:T(8,128)(2,1)} %param.9) | copy-start | bytes 2359300
  0.1 91.4 %all-to-all-start = ((bf16[64,96,512]{2,1,0:T(8,128)(2,1)}), bf16[64,96,512]{2,1,0:T(8,128)(2,1)}, u32[]{:S(2)}, u32[]{:S(2)}) async-start(bf16[64,96,512]{2,1,0:T(8,128)(2,1)} %param.8), calls=%async_computation | async-start | bytes 12582912 | tf_op jit(solution)/shard_map/all_to_all | solution.py:266
  10.9 89.3 %collective-permute-start.1 = (bf16[144,512]{1,0:T(8,128)(2,1)S(1)}, bf16[144,512]{1,0:T(8,128)(2,1)S(1)}, u32[]{:S(2)}, u32[]{:S(2)}) collective-permute-start(bf16[144,512]{1,0:T(8,128)(2,1)S(1)} %pad_maximum_fusion.1), channel_id=1, source_target_pairs={{1,0},{66,1},{131,2},{192,3},{5,4},{198,5},{135,6},{68,7},{9,8},{7... | collective-permute-start | bytes 442376 | tf_op jit(solution)/shard_map/ppermute | solution.py:253
  16.3 83.9 %collective-permute-start.2 = (bf16[144,512]{1,0:T(8,128)(2,1)S(1)}, bf16[144,512]{1,0:T(8,128)(2,1)S(1)}, u32[]{:S(2)}, u32[]{:S(2)}) collective-permute-start(bf16[144,512]{1,0:T(8,128)(2,1)S(1)} %pad_maximum_fusion.1), channel_id=1, source_target_pairs={{2,0},{67,1},{128,2},{193,3},{6,4},{199,5},{132,6},{69,7},{10,8},{... | collective-permute-start | bytes 442376 | tf_op jit(solution)/shard_map/ppermute | solution.py:253
  19.0 81.3 %collective-permute-start.3 = (bf16[144,512]{1,0:T(8,128)(2,1)S(1)}, bf16[144,512]{1,0:T(8,128)(2,1)S(1)}, u32[]{:S(2)}, u32[]{:S(2)}) collective-permute-start(bf16[144,512]{1,0:T(8,128)(2,1)S(1)} %pad_maximum_fusion.1), channel_id=1, source_target_pairs={{3,0},{64,1},{129,2},{194,3},{7,4},{196,5},{133,6},{70,7},{11,8},{... | collective-permute-start | bytes 442376 | tf_op jit(solution)/shard_map/ppermute | solution.py:253
  19.7 80.5 %collective-permute-start = (bf16[160,512]{1,0:T(8,128)(2,1)S(1)}, bf16[160,512]{1,0:T(8,128)(2,1)S(1)}, u32[]{:S(2)}, u32[]{:S(2)}) collective-permute-start(bf16[160,512]{1,0:T(8,128)(2,1)S(1)} %pad_maximum_fusion), channel_id=1, source_target_pairs={{0,0},{65,1},{130,2},{195,3},{4,4},{197,5},{134,6},{71,7},{8,8},{7... | collective-permute-start | bytes 491528 | tf_op jit(solution)/shard_map/ppermute | solution.py:253
  91.4 24.0 %all-to-all-start.1 = ((bf16[64,48,128]{2,1,0:T(8,128)(2,1)}), bf16[64,48,128]{2,1,0:T(8,128)(2,1)S(1)}, u32[]{:S(2)}, u32[]{:S(2)}) async-start(bf16[64,48,128]{2,1,0:T(8,128)(2,1)} %bitcast.18), calls=%async_computation.1 | async-start | bytes 1572864 | tf_op jit(solution)/shard_map/all_to_all | solution.py:269
  123.7 16.1 %collective-permute-start.4 = (bf16[144,512]{1,0:T(8,128)(2,1)S(1)}, bf16[144,512]{1,0:T(8,128)(2,1)S(1)}, u32[]{:S(2)}, u32[]{:S(2)}) collective-permute-start(bf16[144,512]{1,0:T(8,128)(2,1)S(1)} %get-tuple-element.13), channel_id=1, source_target_pairs={{0,0},{1,65},{2,130},{3,195},{4,4},{5,197},{6,134},{7,71},{8,8},{9... | collective-permute-start | bytes 442376 | tf_op jit(solution)/shard_map/ppermute | solution.py:296
  124.4 15.4 %collective-permute-start.5 = (bf16[144,512]{1,0:T(8,128)(2,1)S(1)}, bf16[144,512]{1,0:T(8,128)(2,1)S(1)}, u32[]{:S(2)}, u32[]{:S(2)}) collective-permute-start(bf16[144,512]{1,0:T(8,128)(2,1)S(1)} %get-tuple-element.14), channel_id=1, source_target_pairs={{0,1},{1,66},{2,131},{3,192},{4,5},{5,198},{6,135},{7,68},{8,9},{9... | collective-permute-start | bytes 442376 | tf_op jit(solution)/shard_map/ppermute | solution.py:296
  132.5 12.4 %collective-permute-start.6 = (bf16[144,512]{1,0:T(8,128)(2,1)S(1)}, bf16[144,512]{1,0:T(8,128)(2,1)S(1)}, u32[]{:S(2)}, u32[]{:S(2)}) collective-permute-start(bf16[144,512]{1,0:T(8,128)(2,1)S(1)} %get-tuple-element.15), channel_id=1, source_target_pairs={{0,2},{1,67},{2,128},{3,193},{4,6},{5,199},{6,132},{7,69},{8,10},{... | collective-permute-start | bytes 442376 | tf_op jit(solution)/shard_map/ppermute | solution.py:296
  139.5 9.8 %collective-permute-start.7 = (bf16[144,512]{1,0:T(8,128)(2,1)S(1)}, bf16[144,512]{1,0:T(8,128)(2,1)S(1)}, u32[]{:S(2)}, u32[]{:S(2)}) collective-permute-start(bf16[144,512]{1,0:T(8,128)(2,1)S(1)} %get-tuple-element.16), channel_id=1, source_target_pairs={{0,3},{1,64},{2,129},{3,194},{4,7},{5,196},{6,133},{7,70},{8,11},{... | collective-permute-start | bytes 442376 | tf_op jit(solution)/shard_map/ppermute | solution.py:296

commit v7 on v6

--- a/solution.py
+++ b/solution.py
@@ -109,7 +109,7 @@
         start = count_ref[0] * request
         count = count_ref[request]
         blocks = (count + BLOCK - 1) // BLOCK
-        doubles, single = blocks // 2, blocks % 2
+        fours, double, single = blocks // 4, blocks // 2 % 2, blocks % 2
 
         def slots(block, size):
             return [
@@ -148,8 +148,9 @@
             return total
 
         def over(step, carry):
-            carry = lax.fori_loop(0, doubles, lambda i, c: step(2, 2 * i, c), carry)
-            return lax.fori_loop(0, single, lambda i, c: step(1, 2 * doubles, c), carry)
+            carry = lax.fori_loop(0, fours, lambda i, c: step(4, 4 * i, c), carry)
+            carry = lax.fori_loop(0, double, lambda i, c: step(2, 4 * fours, c), carry)
+            return lax.fori_loop(0, single, lambda i, c: step(1, blocks - 1, c), carry)
 
         maxima = over(score_blocks, jnp.full((4 * ROWS, 128), NEG, jnp.float32))
         top = jnp.max(maxima, axis=1, keepdims=True)
@@ -287,7 +288,7 @@
             pltpu.VMEM((SLOTS // BLOCK, 4 * ROWS, TOKENS), jnp.float32),
             pltpu.VMEM((4 * ROWS, 512), jnp.float32),
         ],
-        compiler_params=pltpu.CompilerParams(vmem_limit_bytes=18 * 1024 * 1024),
+        compiler_params=pltpu.CompilerParams(vmem_limit_bytes=30 * 1024 * 1024),
         cost_estimate=pl.CostEstimate(
             flops=4 * ROWS * 6144 * 1152 * 2, bytes_accessed=8 << 20, transcendentals=1 << 20
         ),

time: 151 us -> 150 us (level)
  Pallas kernels: 9.59 us -> 7.62 us
    pallas_call x1, Pallas kernels: 8.29 us -> 6.32 us  [on_device(): pl.pallas_call(attend_kernel, out_shape=[partial] * 4, in_specs=[scalars]...]
where the time goes in v7:
time: 150 us; the launch traced here: 149 us
  waiting for transfers between devices  87.8 us (59%)
  starting transfers between devices  45.5 us (30%)
  Pallas kernels  7.62 us (5%)
  between operations  2.77 us (2%)
  local copies, waits for them, and re-layouts  2.72 us (2%)
  other arithmetic  2.48 us (2%)
    all_to_all x1, waiting for transfers between devices, on_device(): lat = exchange(latent_pages)  69.7 us
    ppermute x4, starting transfers between devices, on_device(): lax.ppermute(part, AXES, home_pairs(d))  16.6 us
    all_to_all x1, starting transfers between devices, on_device(): lat = exchange(latent_pages)  10.7 us
    ppermute x4, starting transfers between devices, on_device(): lax.ppermute(query if d else first, AXES, [(t, s) for s, t in home_pairs(...  9.4 us
    ppermute x4, waiting for transfers between devices, on_device(): lax.ppermute(part, AXES, home_pairs(d))  9.38 us
    all_to_all x1, starting transfers between devices, on_device(): rope = exchange(ropes)  8.79 us
    all_to_all x1, waiting for transfers between devices, on_device(): rope = exchange(ropes)  8.77 us
    pallas_call x1, Pallas kernels, on_device(): pl.pallas_call(attend_kernel, out_shape=[partial] * 4, in_specs=[scalars]...  6.32 us
  transfers between devices with their start and end apart: 10, of which 4 were waited for; matrix products, arithmetic and copies ran while one was open for 4% of the time, Pallas kernels for 0%

profile of v7, /device:TPU:1, one launch (start us, length us, event | category | flops | bytes accessed | tf_op | source)
XLA Modules:
  0.0 149.2 jit_solution(15475247630879509856)
XLA Ops:
  0.1 10.7 %all-to-all-start = ((bf16[64,96,512]{2,1,0:T(8,128)(2,1)}), bf16[64,96,512]{2,1,0:T(8,128)(2,1)}, u32[]{:S(2)}, u32[]{:S(2)}) async-start(bf16[64,96,512]{2,1,0:T(8,128)(2,1)} %param.8), calls=%async_computation | async-start | bytes 12582912 | tf_op jit(solution)/shard_map/all_to_all | solution.py:267
  10.9 5.5 %collective-permute-start.1 = (bf16[144,512]{1,0:T(8,128)(2,1)S(1)}, bf16[144,512]{1,0:T(8,128)(2,1)S(1)}, u32[]{:S(2)}, u32[]{:S(2)}) collective-permute-start(bf16[144,512]{1,0:T(8,128)(2,1)S(1)} %pad_maximum_fusion.1), channel_id=1, source_target_pairs={{1,0},{66,1},{131,2},{192,3},{5,4},{198,5},{135,6},{68,7},{9,8},{7... | collective-permute-start | bytes 442376 | tf_op jit(solution)/shard_map/ppermute | solution.py:254
  16.3 2.6 %collective-permute-start.2 = (bf16[144,512]{1,0:T(8,128)(2,1)S(1)}, bf16[144,512]{1,0:T(8,128)(2,1)S(1)}, u32[]{:S(2)}, u32[]{:S(2)}) collective-permute-start(bf16[144,512]{1,0:T(8,128)(2,1)S(1)} %pad_maximum_fusion.1), channel_id=1, source_target_pairs={{2,0},{67,1},{128,2},{193,3},{6,4},{199,5},{132,6},{69,7},{10,8},{... | collective-permute-start | bytes 442376 | tf_op jit(solution)/shard_map/ppermute | solution.py:254
  19.0 0.6 collective-permute-start.3
  19.7 0.7 collective-permute-start
  20.5 0.2 fusion.4
  20.7 1.0 copy.17
  21.8 69.7 %all-to-all-done.lat_ref = bf16[64,96,512]{2,1,0:T(8,128)(2,1)} async-done(((bf16[64,96,512]{2,1,0:T(8,128)(2,1)}), bf16[64,96,512]{2,1,0:T(8,128)(2,1)}, u32[]{:S(2)}, u32[]{:S(2)}) %all-to-all-start) | async-done | bytes 6291488 | tf_op jit(solution)/shard_map/all_to_all | solution.py:267
  91.4 8.8 %all-to-all-start.1 = ((bf16[64,48,128]{2,1,0:T(8,128)(2,1)}), bf16[64,48,128]{2,1,0:T(8,128)(2,1)S(1)}, u32[]{:S(2)}, u32[]{:S(2)}) async-start(bf16[64,48,128]{2,1,0:T(8,128)(2,1)} %bitcast.18), calls=%async_computation.1 | async-start | bytes 1572864 | tf_op jit(solution)/shard_map/all_to_all | solution.py:270
  100.4 0.6 fusion.33
  102.3 0.8 gather_fusion
  104.3 0.7 fusion.23
  105.0 1.3 pad_add_fusion.count_ref
  106.3 0.2 convert_reduce_fusion
  106.6 8.8 %all-to-all-done.1.rope_ref = bf16[64,48,128]{2,1,0:T(8,128)(2,1)S(1)} async-done(((bf16[64,48,128]{2,1,0:T(8,128)(2,1)}), bf16[64,48,128]{2,1,0:T(8,128)(2,1)S(1)}, u32[]{:S(2)}, u32[]{:S(2)}) %all-to-all-start.1) | async-done | bytes 786464 | tf_op jit(solution)/shard_map/all_to_all | solution.py:270
  115.4 6.3 %attend.1 = (bf16[144,512]{1,0:T(8,128)(2,1)S(1)}, bf16[144,512]{1,0:T(8,128)(2,1)S(1)}, bf16[144,512]{1,0:T(8,128)(2,1)S(1)}, bf16[144,512]{1,0:T(8,128)(2,1)S(1)}) custom-call(s32[64]{0:T(128)S(1)} %get-tuple-element.20.order_ref, s32[64]{0:T(128)S(1)} %get-tuple-element.19.valid_ref, s32[2]{0:T(128)S(1)} %pad_add_fusion.count_ref, ...), custom_call_target="tpu_custom_call" | custom-call | flops 3623878656 | bytes 8388608 | tf_op jit(solution)/shard_map/attend/pallas_call | solution.py:282
  121.7 0.7 collective-permute-start.4
  122.4 9.3 %collective-permute-start.5 = (bf16[144,512]{1,0:T(8,128)(2,1)S(1)}, bf16[144,512]{1,0:T(8,128)(2,1)S(1)}, u32[]{:S(2)}, u32[]{:S(2)}) collective-permute-start(bf16[144,512]{1,0:T(8,128)(2,1)S(1)} %get-tuple-element.14), channel_id=1, source_target_pairs={{0,1},{1,66},{2,131},{3,192},{4,5},{5,198},{6,135},{7,68},{8,9},{9... | collective-permute-start | bytes 442376 | tf_op jit(solution)/shard_map/ppermute | solution.py:297
  131.7 6.7 %collective-permute-start.6 = (bf16[144,512]{1,0:T(8,128)(2,1)S(1)}, bf16[144,512]{1,0:T(8,128)(2,1)S(1)}, u32[]{:S(2)}, u32[]{:S(2)}) collective-permute-start(bf16[144,512]{1,0:T(8,128)(2,1)S(1)} %get-tuple-element.15), channel_id=1, source_target_pairs={{0,2},{1,67},{2,128},{3,193},{4,6},{5,199},{6,132},{7,69},{8,10},{... | collective-permute-start | bytes 442376 | tf_op jit(solution)/shard_map/ppermute | solution.py:297
  138.4 0.1 fusion.1
  138.5 0.1 copy.14
  138.7 3.4 %collective-permute-done.6.p2 = bf16[144,512]{1,0:T(8,128)(2,1)S(1)} collective-permute-done((bf16[144,512]{1,0:T(8,128)(2,1)S(1)}, bf16[144,512]{1,0:T(8,128)(2,1)S(1)}, u32[]{:S(2)}, u32[]{:S(2)}) %collective-permute-start.6) | collective-permute-done | bytes 147488 | tf_op jit(solution)/shard_map/ppermute | solution.py:297
  142.0 6.0 %collective-permute-done.7.p3 = bf16[144,512]{1,0:T(8,128)(2,1)S(1)} collective-permute-done((bf16[144,512]{1,0:T(8,128)(2,1)S(1)}, bf16[144,512]{1,0:T(8,128)(2,1)S(1)}, u32[]{:S(2)}, u32[]{:S(2)}) %collective-permute-start.7) | collective-permute-done | bytes 147488 | tf_op jit(solution)/shard_map/ppermute | solution.py:297
  148.0 1.2 merge.1
  (35 shorter events, 0.6 us)
Async XLA Ops:
  0.0 138.4 %copy-start = (bf16[2,2,64]{2,1,0:T(2,128)(2,1)S(1)}, bf16[2,2,64]{2,1,0:T(2,128)(2,1)}, u32[]{:S(2)}) copy-start(bf16[2,2,64]{2,1,0:T(2,128)(2,1)} %param.15) | copy-start | bytes 1540
  0.0 10.7 %copy-start.4 = (bf16[2,2,32,64]{3,2,1,0:T(8,128)(2,1)S(1)}, bf16[2,2,32,64]{3,2,1,0:T(8,128)(2,1)}, u32[]{:S(2)}) copy-start(bf16[2,2,32,64]{3,2,1,0:T(8,128)(2,1)} %param.13) | copy-start | bytes 49156
  0.0 10.9 %copy-start.3 = (bf16[2,2,32,512]{3,2,1,0:T(8,128)(2,1)S(1)}, bf16[2,2,32,512]{3,2,1,0:T(8,128)(2,1)}, u32[]{:S(2)}) copy-start(bf16[2,2,32,512]{3,2,1,0:T(8,128)(2,1)} %param.12) | copy-start | bytes 393220
  0.0 19.6 %copy-start.5 = (s32[256]{0:T(256)S(1)}, s32[256]{0:T(256)}, u32[]{:S(2)}) copy-start(s32[256]{0:T(256)} %param.10) | copy-start | bytes 3076
  0.0 19.6 %copy-start.6 = (s32[2]{0:T(128)S(1)}, s32[2]{0:T(128)}, u32[]{:S(2)}) copy-start(s32[2]{0:T(128)} %param.11) | copy-start | bytes 28
  0.0 20.4 %copy-start.1 = (bf16[2,2,512]{2,1,0:T(2,128)(2,1)S(1)}, bf16[2,2,512]{2,1,0:T(2,128)(2,1)}, u32[]{:S(2)}) copy-start(bf16[2,2,512]{2,1,0:T(2,128)(2,1)} %new_lat_ref.1) | copy-start | bytes 12292
  0.0 20.7 %copy-start.2 = (bf16[64,6144]{1,0:T(8,128)(2,1)S(1)}, bf16[64,6144]{1,0:T(8,128)(2,1)}, u32[]{:S(2)}) copy-start(bf16[64,6144]{1,0:T(8,128)(2,1)} %param.9) | copy-start | bytes 2359300
  0.1 91.4 %all-to-all-start = ((bf16[64,96,512]{2,1,0:T(8,128)(2,1)}), bf16[64,96,512]{2,1,0:T(8,128)(2,1)}, u32[]{:S(2)}, u32[]{:S(2)}) async-start(bf16[64,96,512]{2,1,0:T(8,128)(2,1)} %param.8), calls=%async_computation | async-start | bytes 12582912 | tf_op jit(solution)/shard_map/all_to_all | solution.py:267
  10.9 89.3 %collective-permute-start.1 = (bf16[144,512]{1,0:T(8,128)(2,1)S(1)}, bf16[144,512]{1,0:T(8,128)(2,1)S(1)}, u32[]{:S(2)}, u32[]{:S(2)}) collective-permute-start(bf16[144,512]{1,0:T(8,128)(2,1)S(1)} %pad_maximum_fusion.1), channel_id=1, source_target_pairs={{1,0},{66,1},{131,2},{192,3},{5,4},{198,5},{135,6},{68,7},{9,8},{7... | collective-permute-start | bytes 442376 | tf_op jit(solution)/shard_map/ppermute | solution.py:254
  16.3 83.9 %collective-permute-start.2 = (bf16[144,512]{1,0:T(8,128)(2,1)S(1)}, bf16[144,512]{1,0:T(8,128)(2,1)S(1)}, u32[]{:S(2)}, u32[]{:S(2)}) collective-permute-start(bf16[144,512]{1,0:T(8,128)(2,1)S(1)} %pad_maximum_fusion.1), channel_id=1, source_target_pairs={{2,0},{67,1},{128,2},{193,3},{6,4},{199,5},{132,6},{69,7},{10,8},{... | collective-permute-start | bytes 442376 | tf_op jit(solution)/shard_map/ppermute | solution.py:254
  19.0 81.3 %collective-permute-start.3 = (bf16[144,512]{1,0:T(8,128)(2,1)S(1)}, bf16[144,512]{1,0:T(8,128)(2,1)S(1)}, u32[]{:S(2)}, u32[]{:S(2)}) collective-permute-start(bf16[144,512]{1,0:T(8,128)(2,1)S(1)} %pad_maximum_fusion.1), channel_id=1, source_target_pairs={{3,0},{64,1},{129,2},{194,3},{7,4},{196,5},{133,6},{70,7},{11,8},{... | collective-permute-start | bytes 442376 | tf_op jit(solution)/shard_map/ppermute | solution.py:254
  19.7 80.5 %collective-permute-start = (bf16[160,512]{1,0:T(8,128)(2,1)S(1)}, bf16[160,512]{1,0:T(8,128)(2,1)S(1)}, u32[]{:S(2)}, u32[]{:S(2)}) collective-permute-start(bf16[160,512]{1,0:T(8,128)(2,1)S(1)} %pad_maximum_fusion), channel_id=1, source_target_pairs={{0,0},{65,1},{130,2},{195,3},{4,4},{197,5},{134,6},{71,7},{8,8},{7... | collective-permute-start | bytes 491528 | tf_op jit(solution)/shard_map/ppermute | solution.py:254
  91.4 24.0 %all-to-all-start.1 = ((bf16[64,48,128]{2,1,0:T(8,128)(2,1)}), bf16[64,48,128]{2,1,0:T(8,128)(2,1)S(1)}, u32[]{:S(2)}, u32[]{:S(2)}) async-start(bf16[64,48,128]{2,1,0:T(8,128)(2,1)} %bitcast.18), calls=%async_computation.1 | async-start | bytes 1572864 | tf_op jit(solution)/shard_map/all_to_all | solution.py:270
  121.7 16.9 %collective-permute-start.4 = (bf16[144,512]{1,0:T(8,128)(2,1)S(1)}, bf16[144,512]{1,0:T(8,128)(2,1)S(1)}, u32[]{:S(2)}, u32[]{:S(2)}) collective-permute-start(bf16[144,512]{1,0:T(8,128)(2,1)S(1)} %get-tuple-element.13), channel_id=1, source_target_pairs={{0,0},{1,65},{2,130},{3,195},{4,4},{5,197},{6,134},{7,71},{8,8},{9... | collective-permute-start | bytes 442376 | tf_op jit(solution)/shard_map/ppermute | solution.py:297
  122.4 16.3 %collective-permute-start.5 = (bf16[144,512]{1,0:T(8,128)(2,1)S(1)}, bf16[144,512]{1,0:T(8,128)(2,1)S(1)}, u32[]{:S(2)}, u32[]{:S(2)}) collective-permute-start(bf16[144,512]{1,0:T(8,128)(2,1)S(1)} %get-tuple-element.14), channel_id=1, source_target_pairs={{0,1},{1,66},{2,131},{3,192},{4,5},{5,198},{6,135},{7,68},{8,9},{9... | collective-permute-start | bytes 442376 | tf_op jit(solution)/shard_map/ppermute | solution.py:297
  131.7 10.3 %collective-permute-start.6 = (bf16[144,512]{1,0:T(8,128)(2,1)S(1)}, bf16[144,512]{1,0:T(8,128)(2,1)S(1)}, u32[]{:S(2)}, u32[]{:S(2)}) collective-permute-start(bf16[144,512]{1,0:T(8,128)(2,1)S(1)} %get-tuple-element.15), channel_id=1, source_target_pairs={{0,2},{1,67},{2,128},{3,193},{4,6},{5,199},{6,132},{7,69},{8,10},{... | collective-permute-start | bytes 442376 | tf_op jit(solution)/shard_map/ppermute | solution.py:297
  138.4 9.7 %collective-permute-start.7 = (bf16[144,512]{1,0:T(8,128)(2,1)S(1)}, bf16[144,512]{1,0:T(8,128)(2,1)S(1)}, u32[]{:S(2)}, u32[]{:S(2)}) collective-permute-start(bf16[144,512]{1,0:T(8,128)(2,1)S(1)} %get-tuple-element.16), channel_id=1, source_target_pairs={{0,3},{1,64},{2,129},{3,194},{4,7},{5,196},{6,133},{7,70},{8,11},{... | collective-permute-start | bytes 442376 | tf_op jit(solution)/shard_map/ppermute | solution.py:297
